TPU v7x, 32 devices: a whole 2x2x4 slice. The times are simulated.
32 devices in a mesh: heads: 4 (over z), blk: 8 (over y, x, core).
Axes of the slice: x: 2, y: 2, z: 4, core: 2. Of those that a mesh axis runs over, the one named last changes fastest.
Arguments:
- versions: bfloat16 [4, 4096, 2048], P(None, ('blk', 'heads')), may hold values from -6 to 6
- layer_input: bfloat16 [4096, 256], P(('blk', 'heads')), may hold values from -6 to 6
- positions: int32 [4096], P(('blk', 'heads')), may hold values from 0 to 8191, as said below
- documents: int32 [4096], replicated, may hold values from 0 to 2, as said below
- cotangent: bfloat16 [4, 4096, 2048], P(None, ('blk', 'heads')), may hold values from -6 to 6
- norm_gains: bfloat16 [8, 2048], replicated, may hold values from 0.5 to 1.5
- router_weight: bfloat16 [4, 2048], replicated, may hold values from -0.125 to 0.125
- coefficients: bfloat16 [4, 20], replicated, may hold values from -2.5 to 2.5
- query_key_gains: bfloat16 [2, 256], replicated, may hold values from 0.25 to 0.44921875
- query_weight: bfloat16 [2048, 2048], P('blk'), may hold values from -0.125 to 0.125
- key_matrix: bfloat16 [2048, 512], P('blk'), may hold values from -0.125 to 0.125
- value_matrix: bfloat16 [2048, 512], P('blk'), may hold values from -0.125 to 0.125
- out_weight: bfloat16 [2048, 2048], P('blk'), may hold values from -0.125 to 0.125
- laurel_weight: bfloat16 [2048, 128], P('blk'), may hold values from -0.125 to 0.125
- input_gate: bfloat16 [2048, 256], P('blk'), may hold values from -0.125 to 0.125
- input_projection: bfloat16 [2048, 256], P('blk'), may hold values from -0.375 to 0.375
- gate_weight: bfloat16 [2048, 8192], P('blk', 'heads'), may hold values from -0.125 to 0.125
- up_weight: bfloat16 [2048, 8192], P('blk', 'heads'), may hold values from -0.125 to 0.125
- down_weight: bfloat16 [2048, 8192], P('blk', 'heads'), may hold values from -0.0625 to 0.0625
Outputs:
- out_versions: bfloat16 [4, 4096, 2048], P(None, ('blk', 'heads'))
- versions_grad: bfloat16 [4, 4096, 2048], P(None, ('blk', 'heads'))
- layer_input_grad: bfloat16 [4096, 256], P(('blk', 'heads'))
- norm_gains_grad: float32 [8, 2048], replicated
- router_weight_grad: float32 [4, 2048], replicated
- coefficients_grad: float32 [4, 20], replicated
- head_gains_grad: float32 [2, 256], replicated
- query_weight_grad: float32 [2048, 2048], P('blk')
- key_weight_grad: float32 [2048, 512], P('blk')
- value_weight_grad: float32 [2048, 512], P('blk')
- out_weight_grad: float32 [2048, 2048], P('blk')
- laurel_weight_grad: float32 [2048, 128], P('blk')
- input_gate_grad: float32 [2048, 256], P('blk')
- input_projection_grad: float32 [2048, 256], P('blk')
- gate_weight_grad: float32 [2048, 8192], P('blk', 'heads')
- up_weight_grad: float32 [2048, 8192], P('blk', 'heads')
- down_weight_grad: float32 [2048, 8192], P('blk', 'heads')
Inputs may be any that keep to these rules, and one draw needn't show every extreme that they name: Never falls along the row; documents 0 and 2 hold 1 to half of 512 tokens each, document 1 all others. `positions`: A token's position is its document's start position plus its place in the document; document 1 starts at 0, and the last token of the row is at position 4096 + 4095.
All inputs are finite; a program needn't handle non-finite values.
Results may differ from a plain program's by a relative error of at most 0.039.
Values may be sent and summed in bfloat16 or wider, within the bound.
No kernel may reach another device: no remote copies, remote signals or barrier semaphores. Data moves between devices by JAX's collectives and lax.ppermute only.
A program may use at most 320 MiB of HBM per device.

v0:
```python
import jax
import jax.numpy as jnp
from jax import lax
from jax.sharding import PartitionSpec as P

QUERY_HEAD_COUNT = 8
KEY_VALUE_HEADS = 2
HEAD_WIDTH = 256
LAUREL_RANK = 64
LAYER_INPUT_SIZE = 256
KEYB = 2048


epsilon = 1e-06
rotary_base = 1000000.0
highest = lax.Precision.HIGHEST
root_half = 0.5**0.5


def rms_norm_apply(value_states, gain):
    return (
        value_states
        * lax.rsqrt(jnp.mean(value_states * value_states, axis=-1, keepdims=True) + epsilon)
        * gain
    )


def rotary_apply(value_states, cosine_table, sine_table):
    half = value_states.shape[-1] // 2
    turned = jnp.concatenate([-value_states[..., half:], value_states[..., :half]], axis=-1)
    return value_states * cosine_table + turned * sine_table


def angles(positions):
    frequency = rotary_base ** (-2.0 * jnp.arange(HEAD_WIDTH // 2, dtype=jnp.float32) / HEAD_WIDTH)
    phase = positions.astype(jnp.float32)[:, None] * frequency[None, :]
    phase = jnp.concatenate([phase, phase], axis=-1)[:, None, :]
    return (jnp.cos(phase), jnp.sin(phase))


def modes(value_states, gain, router):
    return jnp.tanh(jnp.dot(rms_norm_apply(value_states, gain), router.T, precision=highest))


def predict(versions, gain_rows, router, coefficients):
    token_count = versions.shape[1]
    table = jnp.dot(
        modes(versions[0], gain_rows[0], router), coefficients[:, :16], precision=highest
    ).reshape(token_count, 4, 4)
    predicted = versions + jnp.einsum("tij,jtd->itd", table, versions, precision=highest)
    return (predicted, rms_norm_apply(predicted[0], gain_rows[1]))


def prepare(query_states, key, value_states, query_key_gains, cosine_table, sine_table):
    token_count = query_states.shape[0]
    query_states = rotary_apply(
        rms_norm_apply(
            query_states.reshape(token_count, QUERY_HEAD_COUNT, HEAD_WIDTH), query_key_gains[0]
        ),
        cosine_table,
        sine_table,
    )
    key = rotary_apply(
        rms_norm_apply(key.reshape(token_count, KEY_VALUE_HEADS, HEAD_WIDTH), query_key_gains[1]),
        cosine_table,
        sine_table,
    )
    value_states = value_states.reshape(token_count, KEY_VALUE_HEADS, HEAD_WIDTH)
    value_states = value_states * lax.rsqrt(
        jnp.mean(value_states * value_states, axis=-1, keepdims=True) + epsilon
    )
    return (
        query_states,
        jnp.repeat(key, QUERY_HEAD_COUNT // KEY_VALUE_HEADS, axis=1),
        jnp.repeat(value_states, QUERY_HEAD_COUNT // KEY_VALUE_HEADS, axis=1),
    )


def combine(active, attention_out, normed, lifted, gain_rows):
    merged = (
        active
        + rms_norm_apply(attention_out, gain_rows[2])
        + normed
        + rms_norm_apply(lifted, gain_rows[3])
    ) * root_half
    return (merged, rms_norm_apply(merged, gain_rows[4]))


def activate(gate, up):
    return jax.nn.gelu(gate, approximate=True) * up


def correct(merged, fed, predicted, gain_rows, router, coefficients):
    activated = merged + rms_norm_apply(fed, gain_rows[5])
    scale = (
        jnp.dot(modes(activated, gain_rows[0], router), coefficients[:, 16:], precision=highest)
        + 1.0
    )
    corrected = predicted + scale.T[:, :, None] * (activated - predicted[0])[None]
    return (corrected, corrected[0] * gain_rows[6])


def finish(corrected, projected, gain_rows):
    extra = rms_norm_apply(projected, gain_rows[7])
    return corrected + jnp.stack([jnp.zeros_like(extra), extra, extra, extra])


def forward_product(left, right):
    return jnp.dot(left, right, preferred_element_type=jnp.float32)


def transposed_product(left, right):
    return lax.dot_general(
        left, right, (((1,), (1,)), ((), ())), preferred_element_type=jnp.float32
    )


def weight_product(left, right):
    return lax.dot_general(
        left, right, (((0,), (0,)), ((), ())), preferred_element_type=jnp.float32
    )


def on_device(
    versions,
    layer_input,
    positions,
    documents,
    cotangent,
    norm_gains,
    router_weight,
    coefficients,
    query_key_gains,
    query_weight,
    key_matrix,
    value_matrix,
    out_weight,
    laurel_weight,
    input_gate,
    input_projection,
    gate_weight,
    up_weight,
    down_weight,
):
    narrow = jnp.bfloat16
    wide = jnp.float32
    (
        query_full,
        key_full,
        value_full,
        out_full,
        laurel_full,
        gate_full,
        projection_full,
        unit_gate,
        unit_up,
        unit_down,
    ) = (
        lax.all_gather(query_weight, "blk", axis=0, tiled=True),
        lax.all_gather(key_matrix, "blk", axis=0, tiled=True),
        lax.all_gather(value_matrix, "blk", axis=0, tiled=True),
        lax.all_gather(out_weight, "blk", axis=0, tiled=True),
        lax.all_gather(laurel_weight, "blk", axis=0, tiled=True),
        lax.all_gather(input_gate, "blk", axis=0, tiled=True),
        lax.all_gather(input_projection, "blk", axis=0, tiled=True),
        lax.all_gather(gate_weight, "blk", axis=0, tiled=True),
        lax.all_gather(up_weight, "blk", axis=0, tiled=True),
        lax.all_gather(down_weight, "blk", axis=0, tiled=True),
    )
    gain_rows = norm_gains.astype(wide)
    router_wide = router_weight.astype(wide)
    coef_wide = coefficients.astype(wide)
    head_wide = query_key_gains.astype(wide)
    (predicted, normed), pull_predict = jax.vjp(
        predict, versions.astype(wide), gain_rows, router_wide, coef_wide
    )
    normed_low = normed.astype(narrow)
    cosine_table, sine_table = angles(positions)

    def prepare_here(query_states, key, value_states, gains_here):
        return prepare(query_states, key, value_states, gains_here, cosine_table, sine_table)

    (rotated, keys_rep, values_rep), pull_prepare = jax.vjp(
        prepare_here,
        forward_product(normed_low, query_full),
        forward_product(normed_low, key_full),
        forward_product(normed_low, value_full),
        head_wide,
    )
    query_heads, key_heads, value_heads = (
        lax.all_to_all(rotated.astype(narrow), "heads", split_axis=1, concat_axis=0, tiled=True),
        lax.all_to_all(keys_rep.astype(narrow), "heads", split_axis=1, concat_axis=0, tiled=True),
        lax.all_to_all(values_rep.astype(narrow), "heads", split_axis=1, concat_axis=0, tiled=True),
    )
    keys_all, values_all = (
        lax.all_gather(key_heads, "blk", axis=0, tiled=True),
        lax.all_gather(value_heads, "blk", axis=0, tiled=True),
    )
    piece, local_heads, head_size = query_heads.shape
    first_row = lax.axis_index("blk") * piece
    last_row = first_row + piece - 1
    query_rows = first_row + jnp.arange(piece, dtype=jnp.int32)
    query_docs = lax.dynamic_slice_in_dim(documents, first_row, piece)
    block_starts = jnp.arange(keys_all.shape[0] // KEYB, dtype=jnp.int32) * KEYB

    def block_scores(offset):
        key_block = lax.dynamic_slice_in_dim(keys_all, offset, KEYB)
        value_block = lax.dynamic_slice_in_dim(values_all, offset, KEYB)
        key_rows = offset + jnp.arange(KEYB, dtype=jnp.int32)
        key_docs = lax.dynamic_slice_in_dim(documents, offset, KEYB)
        allowed = (key_rows[None, :] <= query_rows[:, None]) & (
            key_docs[None, :] == query_docs[:, None]
        )
        scores = jnp.einsum("qhd,khd->hqk", query_heads, key_block, preferred_element_type=wide)
        return (key_block, value_block, allowed[None], jnp.where(allowed[None], scores, -1e30))

    def attend(state, offset):

        def visit(carry):
            top, total, summed = carry
            key_block, value_block, allowed, scores = block_scores(offset)
            new_top = jnp.maximum(top, jnp.max(scores, axis=-1))
            weights = jnp.where(allowed, jnp.exp(scores - new_top[:, :, None]), 0.0)
            decay = jnp.exp(top - new_top)
            summed = summed * decay.T[:, :, None] + jnp.einsum(
                "hqk,khd->qhd", weights.astype(narrow), value_block, preferred_element_type=wide
            )
            return (new_top, total * decay + jnp.sum(weights, axis=-1), summed)

        def keep(carry):
            return carry

        return (lax.cond(offset <= last_row, visit, keep, state), None)

    start_state = (
        jnp.full((local_heads, piece), -1e30, wide),
        jnp.zeros((local_heads, piece), wide),
        jnp.zeros((piece, local_heads, head_size), wide),
    )
    (top, total, summed), unused = lax.scan(attend, start_state, block_starts)
    log_total = top + jnp.log(total)
    attended = summed / total.T[:, :, None]
    mixed = lax.all_to_all(
        attended.astype(narrow), "heads", split_axis=0, concat_axis=1, tiled=True
    )
    mixed_low = mixed.reshape(mixed.shape[0], -1)
    attention_out = transposed_product(mixed_low, out_full)
    down_low = forward_product(normed_low, laurel_full[:, :LAUREL_RANK]).astype(narrow)
    lifted = transposed_product(down_low, laurel_full[:, LAUREL_RANK:])
    (merged, feed_in), pull_combine = jax.vjp(
        combine, predicted[0], attention_out, normed_low.astype(wide), lifted, gain_rows
    )
    feed_low = feed_in.astype(narrow)
    unit_rows = lax.all_gather(feed_low, "heads", axis=0, tiled=True)
    hidden, pull_activate = jax.vjp(
        activate, forward_product(unit_rows, unit_gate), forward_product(unit_rows, unit_up)
    )
    hidden_low = hidden.astype(narrow)
    fed = transposed_product(hidden_low, unit_down)
    fed = lax.psum_scatter(
        fed.astype(jnp.bfloat16), "heads", scatter_dimension=0, tiled=True
    ).astype(jnp.float32)
    (corrected, first), pull_correct = jax.vjp(
        correct, merged, fed, predicted, gain_rows, router_wide, coef_wide
    )
    first_low = first.astype(narrow)
    gated, pull_gate = jax.vjp(
        activate, forward_product(first_low, gate_full), layer_input.astype(wide)
    )
    gated_low = gated.astype(narrow)
    projected = transposed_product(gated_low, projection_full)
    result, pull_finish = jax.vjp(finish, corrected, projected, gain_rows)
    corrected_grad, projected_grad, gains_finish = pull_finish(cotangent.astype(wide))
    projected_low = projected_grad.astype(narrow)
    gate_pre_grad, layer_grad = pull_gate(forward_product(projected_low, projection_full))
    gate_pre_low = gate_pre_grad.astype(narrow)
    merged_grad, fed_grad, predicted_grad, gains_correct, router_correct, coef_correct = (
        pull_correct((corrected_grad, transposed_product(gate_pre_low, gate_full)))
    )
    fed_low = fed_grad.astype(narrow)
    fed_rows = lax.all_gather(fed_low, "heads", axis=0, tiled=True)
    gate_grad, up_grad = pull_activate(forward_product(fed_rows, unit_down))
    gate_low = gate_grad.astype(narrow)
    up_low = up_grad.astype(narrow)
    feed_grad = transposed_product(gate_low, unit_gate) + transposed_product(up_low, unit_up)
    feed_grad = lax.psum_scatter(
        feed_grad.astype(jnp.bfloat16), "heads", scatter_dimension=0, tiled=True
    ).astype(jnp.float32)
    active_grad, attention_grad, normed_combine, lifted_grad, gains_combine = pull_combine(
        (merged_grad, feed_grad)
    )
    lifted_low = lifted_grad.astype(narrow)
    down_grad_low = forward_product(lifted_low, laurel_full[:, LAUREL_RANK:]).astype(narrow)
    attention_low = attention_grad.astype(narrow)
    mixed_grad = forward_product(attention_low, out_full).astype(narrow).reshape(mixed.shape)
    attended_grad = lax.all_to_all(mixed_grad, "heads", split_axis=1, concat_axis=0, tiled=True)
    delta = jnp.sum(attended_grad.astype(wide) * attended, axis=-1).T

    def attend_back(query_grad, offset):

        def visit(query_grad):
            key_block, value_block, allowed, scores = block_scores(offset)
            shares = jnp.where(allowed, jnp.exp(scores - log_total[:, :, None]), 0.0)
            share_grad = jnp.einsum(
                "qhd,khd->hqk", attended_grad, value_block, preferred_element_type=wide
            )
            score_low = (shares * (share_grad - delta[:, :, None])).astype(narrow)
            query_grad = query_grad + jnp.einsum(
                "hqk,khd->qhd", score_low, key_block, preferred_element_type=wide
            )
            key_grad = jnp.einsum(
                "hqk,qhd->khd", score_low, query_heads, preferred_element_type=wide
            )
            value_grad = jnp.einsum(
                "hqk,qhd->khd", shares.astype(narrow), attended_grad, preferred_element_type=wide
            )
            return (query_grad, (key_grad, value_grad))

        def skip(query_grad):
            empty = jnp.zeros((KEYB, local_heads, head_size), wide)
            return (query_grad, (empty, empty))

        return lax.cond(offset <= last_row, visit, skip, query_grad)

    query_grad, (key_grads, value_grads) = lax.scan(
        attend_back, jnp.zeros((piece, local_heads, head_size), wide), block_starts
    )
    key_own, value_own = (
        lax.psum_scatter(
            key_grads.reshape(keys_all.shape).astype(jnp.bfloat16),
            "blk",
            scatter_dimension=0,
            tiled=True,
        ).astype(jnp.float32),
        lax.psum_scatter(
            value_grads.reshape(keys_all.shape).astype(jnp.bfloat16),
            "blk",
            scatter_dimension=0,
            tiled=True,
        ).astype(jnp.float32),
    )
    query_back, key_back, value_back = (
        lax.all_to_all(query_grad.astype(narrow), "heads", split_axis=0, concat_axis=1, tiled=True),
        lax.all_to_all(key_own.astype(narrow), "heads", split_axis=0, concat_axis=1, tiled=True),
        lax.all_to_all(value_own.astype(narrow), "heads", split_axis=0, concat_axis=1, tiled=True),
    )
    query_pre, key_pre, value_pre, head_grad = pull_prepare(
        (query_back.astype(wide), key_back.astype(wide), value_back.astype(wide))
    )
    query_low = query_pre.astype(narrow)
    key_low = key_pre.astype(narrow)
    value_low = value_pre.astype(narrow)
    normed_grad = (
        normed_combine
        + transposed_product(query_low, query_full)
        + transposed_product(key_low, key_full)
        + transposed_product(value_low, value_full)
        + transposed_product(down_grad_low, laurel_full[:, :LAUREL_RANK])
    )
    predicted_grad = predicted_grad.at[0].add(active_grad)
    version_grad, gains_predict, router_predict, coef_predict = pull_predict(
        (predicted_grad, normed_grad)
    )
    small = lax.psum(
        (
            gains_finish + gains_correct + gains_combine + gains_predict,
            router_correct + router_predict,
            coef_correct + coef_predict,
            head_grad,
        ),
        ("heads", "blk"),
    )
    normed_targets = jnp.concatenate([query_low, key_low, value_low, down_grad_low], axis=1)
    summed_grads = lax.psum_scatter(
        jnp.concatenate(
            [
                weight_product(normed_low, normed_targets),
                weight_product(attention_low, mixed_low),
                weight_product(lifted_low, down_low),
                weight_product(first_low, gate_pre_low),
                weight_product(projected_low, gated_low),
                weight_product(unit_rows, gate_low),
                weight_product(unit_rows, up_low),
                weight_product(fed_rows, hidden_low),
            ],
            axis=1,
        ).astype(jnp.bfloat16),
        "blk",
        scatter_dimension=0,
        tiled=True,
    ).astype(jnp.float32)
    bounds = [0]
    for feature_width in (
        QUERY_HEAD_COUNT * HEAD_WIDTH,
        KEY_VALUE_HEADS * HEAD_WIDTH,
        KEY_VALUE_HEADS * HEAD_WIDTH,
        LAUREL_RANK,
        QUERY_HEAD_COUNT * HEAD_WIDTH,
        LAUREL_RANK,
        LAYER_INPUT_SIZE,
        LAYER_INPUT_SIZE,
    ):
        bounds.append(bounds[-1] + feature_width)
    attention_sum = lax.psum(summed_grads[:, : bounds[8]].astype(jnp.bfloat16), "heads").astype(
        jnp.float32
    )
    parts = [attention_sum[:, bounds[place] : bounds[place + 1]] for place in range(8)]
    unit_width = (summed_grads.shape[1] - bounds[8]) // 3
    gate_part = summed_grads[:, bounds[8] : bounds[8] + unit_width]
    up_part = summed_grads[:, bounds[8] + unit_width : bounds[8] + 2 * unit_width]
    down_part = summed_grads[:, bounds[8] + 2 * unit_width :]
    return (
        result.astype(narrow),
        version_grad.astype(narrow),
        layer_grad.astype(narrow),
        small[0],
        small[1],
        small[2],
        small[3],
        parts[0],
        parts[1],
        parts[2],
        parts[4],
        jnp.concatenate([parts[3], parts[5]], axis=1),
        parts[6],
        parts[7],
        gate_part,
        up_part,
        down_part,
    )


def solution(mesh):
    in_specs = (
        P(None, ("blk", "heads"), None),
        P(("blk", "heads"), None),
        P(("blk", "heads")),
        P(),
        P(None, ("blk", "heads"), None),
        P(),
        P(),
        P(),
        P(),
        P("blk", None),
        P("blk", None),
        P("blk", None),
        P("blk", None),
        P("blk", None),
        P("blk", None),
        P("blk", None),
        P("blk", "heads"),
        P("blk", "heads"),
        P("blk", "heads"),
    )
    out_specs = (
        P(None, ("blk", "heads"), None),
        P(None, ("blk", "heads"), None),
        P(("blk", "heads"), None),
        P(),
        P(),
        P(),
        P(),
        P("blk", None),
        P("blk", None),
        P("blk", None),
        P("blk", None),
        P("blk", None),
        P("blk", None),
        P("blk", None),
        P("blk", "heads"),
        P("blk", "heads"),
        P("blk", "heads"),
    )
    return jax.shard_map(
        on_device, mesh=mesh, in_specs=in_specs, out_specs=out_specs, check_vma=False
    )
```

profile of v0, /device:TPU:0, one launch (start us, length us, event | category | flops | bytes accessed | tf_op | source)
XLA Modules:
  0.0 1496.1 jit_solution(12660200209908402788)
XLA Ops:
  14.9 10.6 bitcast_add_fusion.1
  29.3 11.2 all-gather.20.cloned.1.call-done
  47.9 19.3 %all_to_all.114 = bf16[128,8,256]{2,0,1:T(8,128)(2,1)S(1)} all-to-all(bf16[128,8,256]{2,0,1:T(8,128)(2,1)S(1)} %bitcast.318), channel_id=1, replica_groups=mesh['heads'=4,'blk'=8] {'heads'}, dimensions={1} | all-to-all | bytes 1048576 | tf_op jit(solution)/shard_map/all_to_all | solution.py:193
  77.7 19.3 %all_to_all.115 = bf16[128,8,256]{2,0,1:T(8,128)(2,1)S(1)} all-to-all(bf16[128,8,256]{2,0,1:T(8,128)(2,1)S(1)} %bitcast.319), channel_id=1, replica_groups=mesh['heads'=4,'blk'=8] {'heads'}, dimensions={1} | all-to-all | bytes 1048576 | tf_op jit(solution)/shard_map/all_to_all | solution.py:192
  99.2 27.5 %all-gather.18.cloned.1.call-done = bf16[2048,2048]{1,0:T(8,128)(2,1)} async-done(((bf16[256,2048]{1,0:T(8,128)(2,1)}), bf16[2048,2048]{1,0:T(8,128)(2,1)}) %all-gather.18.cloned.1.call-update) | async-done | bytes 8388624 | tf_op jit(solution)/shard_map/all_gather | solution.py:159
  126.7 12.4 copy.261
  139.1 6.3 multiply_reduce_fusion.22
  152.1 13.8 all-gather.22.cloned.1.call-done
  165.8 6.4 copy.265
  172.3 32.6 %all-gather.16.cloned.1.call-done = bf16[4096,2,256]{2,0,1:T(8,128)(2,1)} async-done(((bf16[512,2,256]{2,0,1:T(8,128)(2,1)}), bf16[4096,2,256]{2,0,1:T(8,128)(2,1)}) %all-gather.16.cloned.1.call-update) | async-done | bytes 4194320 | tf_op jit(solution)/shard_map/all_gather | solution.py:196
  205.0 16.2 %while.34 = (s32[]{:T(128)}, f32[2,512]{1,0:T(2,128)S(1)}, f32[2,512]{1,0:T(2,128)S(1)}, f32[512,2,256]{0,2,1:T(8,128)S(1)}, s32[2]{0:T(128)S(1)}, /*index=5*/s3...) while((s32[]{:T(128)}, f32[2,512]{1,0:T(2,128)S(1)}, ...), condition=%wide.region_10.11_spmd.clone, body=%wide.region_5.10_spmd.clone.sunk | while | flops 2172130816 | bytes 53070208 | solution.py:240
  206.3 13.6 conditional.6
  230.0 25.9 %all_gather.48 = bf16[2048,128]{1,0:T(8,128)(2,1)S(1)} all-gather(bf16[256,128]{1,0:T(8,128)(2,1)S(1)} %copy-done.88), channel_id=1, replica_groups=mesh['heads'=4,'blk'=8] {'blk'}, dimensions={0}, use_global_device_ids=true | all-gather | bytes 589824 | tf_op jit(solution)/shard_map/all_gather | solution.py:163
  263.2 6.3 multiply_reduce_fusion.21
  274.5 45.0 %all-gather.28.cloned.1.call-done = bf16[2048,2048]{1,0:T(8,128)(2,1)} async-done(((bf16[256,2048]{1,0:T(8,128)(2,1)}), bf16[2048,2048]{1,0:T(8,128)(2,1)}) %all-gather.28.cloned.1.call-update) | async-done | bytes 8388624 | tf_op jit(solution)/shard_map/all_gather | solution.py:166
  319.5 48.1 %all-gather.26.cloned.1.call-done = bf16[512,2048]{1,0:T(8,128)(2,1)} async-done(((bf16[128,2048]{1,0:T(8,128)(2,1)}), bf16[512,2048]{1,0:T(8,128)(2,1)}) %all-gather.26.cloned.1.call-update) | async-done | bytes 2097168 | tf_op jit(solution)/shard_map/all_gather | solution.py:254
  367.6 10.5 fusion.190
  378.1 44.5 %all-gather.30.cloned.1.call-done = bf16[2048,2048]{1,0:T(8,128)(2,1)} async-done(((bf16[256,2048]{1,0:T(8,128)(2,1)}), bf16[2048,2048]{1,0:T(8,128)(2,1)}) %all-gather.30.cloned.1.call-update) | async-done | bytes 8388624 | tf_op jit(solution)/shard_map/all_gather | solution.py:167
  422.6 13.0 multiply_convert_fusion.1
  435.6 43.2 %all-gather.32.cloned.1.call-done = bf16[2048,2048]{1,0:T(8,128)(2,1)} async-done(((bf16[256,2048]{1,0:T(8,128)(2,1)}), bf16[2048,2048]{1,0:T(8,128)(2,1)}) %all-gather.32.cloned.1.call-update) | async-done | bytes 8388624 | tf_op jit(solution)/shard_map/all_gather | solution.py:168
  478.8 9.9 convolution_convert_fusion.1
  494.3 38.4 %reduce-scatter.6.cloned.1.call-done = bf16[128,2048]{1,0:T(8,128)(2,1)} async-done(((bf16[512,2048]{1,0:T(8,128)(2,1)}), bf16[128,2048]{1,0:T(8,128)(2,1)}) %reduce-scatter.6.cloned.1.call-update) | async-done | bytes 524304 | tf_op jit(solution)/shard_map/reduce_scatter | solution.py:260
  544.9 12.6 all-gather.34.cloned.1.call-done
  559.2 23.9 %all-gather.36.cloned.1.call-done = bf16[2048,256]{1,0:T(8,128)(2,1)} async-done(((bf16[256,256]{1,0:T(8,128)(2,1)}), bf16[2048,256]{1,0:T(8,128)(2,1)}) %all-gather.36.cloned.1.call-update) | async-done | bytes 1048592 | tf_op jit(solution)/shard_map/all_gather | solution.py:165
  597.9 45.8 %all-gather.38.cloned.1.call-done = bf16[512,2048]{1,0:T(8,128)(2,1)} async-done(((bf16[128,2048]{1,0:T(8,128)(2,1)}), bf16[512,2048]{1,0:T(8,128)(2,1)}) %all-gather.38.cloned.1.call-update) | async-done | bytes 2097168 | tf_op jit(solution)/shard_map/all_gather | solution.py:281
  643.7 11.9 multiply_convert_fusion
  655.6 8.5 fusion.191
  664.1 9.5 add_convert_fusion
  673.7 42.7 %reduce-scatter.8.cloned.1.call-done = bf16[128,2048]{1,0:T(8,128)(2,1)} async-done(((bf16[512,2048]{1,0:T(8,128)(2,1)}), bf16[128,2048]{1,0:T(8,128)(2,1)}) %reduce-scatter.8.cloned.1.call-update) | async-done | bytes 524304 | tf_op jit(solution)/shard_map/reduce_scatter | solution.py:286
  732.6 14.0 all-to-all-done.4
  749.9 30.5 %while.35 = (s32[]{:T(128)}, f32[512,2,256]{0,2,1:T(8,128)}, bf16[2,2048,2,256]{3,1,0,2:T(8,128)(2,1)}, bf16[2,2048,2,256]{3,1,0,2:T(8,128)(2,1)}, s32[2]{0:T(12...) while((s32[]{:T(128)}, f32[512,2,256]{0,2,1:T(8,128)}, ...), condition=%wide.region_30.31_spmd.clone, body=%wide.region_27.0_spmd.clone.sunk | while | flops 5393091072 | bytes 108067320 | solution.py:325
  751.3 18.4 %conditional.7 = (f32[512,2,256]{0,2,1:T(8,128)}, bf16[1,2048,2,256]{3,1,2,0:T(8,128)(2,1)}, bf16[1,2048,2,256]{3,1,2,0:T(8,128)(2,1)S(1)}) conditional(s32[]{:T(128)} %convert_element_type.374, f32[512,2,256]{0,2,1:T(8,128)} %get-tuple-element.956, (s32[]{:T(128)}, bf16[4096,2,256]{2,0,1:T(8,128)(2,1)}, s32[]{:T(128)}, s32[4096]{0:T(1024)S(1)}, ...), branch_computations={%region_28.28_spmd, %region_29.29_spmd} | conditional | flops 5393091072 | bytes 99676384 | solution.py:323
  787.7 12.7 all-to-all-done.5
  803.5 44.3 %reduce-scatter.12.cloned.1.call-done = bf16[512,2,256]{2,0,1:T(8,128)(2,1)} async-done(((bf16[4096,2,256]{2,0,1:T(8,128)(2,1)}), bf16[512,2,256]{2,0,1:T(8,128)(2,1)}) %reduce-scatter.12.cloned.1.call-update) | async-done | bytes 524304 | tf_op jit(solution)/shard_map/reduce_scatter | solution.py:335
  858.2 44.5 %reduce-scatter.10.cloned.1.call-done = bf16[512,2,256]{2,0,1:T(8,128)(2,1)} async-done(((bf16[4096,2,256]{2,0,1:T(8,128)(2,1)}), bf16[512,2,256]{2,0,1:T(8,128)(2,1)}) %reduce-scatter.10.cloned.1.call-update) | async-done | bytes 524304 | tf_op jit(solution)/shard_map/reduce_scatter | solution.py:329
  917.2 7.1 all-to-all-done.6
  930.0 7.7 fusion.61
  937.8 5.7 convert_dynamic-update-slice_fusion.3
  947.4 6.9 convert_dynamic-update-slice_fusion.2
  954.3 6.9 convert_dynamic-update-slice_fusion.1
  961.2 7.3 convert_dynamic-update-slice_fusion
  970.5 5.3 fusion.69
  994.4 11.0 fusion.72
  1005.8 238.6 %reduce-scatter.14.cloned.1.call-done = bf16[256,11904]{0,1:T(8,128)(2,1)} async-done(((bf16[2048,11904]{0,1:T(8,128)(2,1)}), bf16[256,11904]{0,1:T(8,128)(2,1)}) %reduce-scatter.14.cloned.1.call-update) | async-done | bytes 6094864 | tf_op jit(solution)/shard_map/reduce_scatter | solution.py:374
  1253.3 12.4 fusion.74
  1271.1 43.5 %all-reduce.21 = (f32[4,2048]{1,0:T(4,128)}, f32[4,20]{1,0:T(4,128)}, f32[2,256]{1,0:T(2,128)}) all-reduce(f32[4,2048]{1,0:T(4,128)S(1)} %convolution_add_fusion.4, f32[4,20]{1,0:T(4,128)S(1)} %pad_add_fusion.5, f32[2,256]{1,0:T(2,128)S(1)} %pad_add_fusion.4), channel_id=1, replica_groups=mesh['heads'=4,'blk'=8] {'heads','blk'}, use_global_device_ids=true, to_apply=%region_53.54 | all-reduce | flops 8784 | bytes 70272 | tf_op jit(solution)/shard_map/psum | solution.py:364
  1326.6 37.4 %all-reduce.27.cloned.1.call-done = bf16[256,5760]{0,1:T(8,128)(2,1)} async-done(((bf16[256,5760]{0,1:T(8,128)(2,1)}), bf16[256,5760]{0,1:T(8,128)(2,1)}) %all-reduce.27.cloned.1.call-update) | async-done | bytes 2949136 | tf_op jit(solution)/shard_map/psum | solution.py:404
  1379.5 108.1 %all-reduce.25.cloned.1.call-done = f32[8,2048]{1,0:T(8,128)} async-done(((f32[8,2048]{1,0:T(8,128)}), f32[8,2048]{1,0:T(8,128)}) %all-reduce.25.cloned.1.call-update) | async-done | bytes 65552 | tf_op jit(solution)/shard_map/psum | solution.py:364
  (531 shorter events, 261.7 us)
Async XLA Ops:
  7.2 33.4 %all-gather.20.cloned.1.call-start = ((), (), s32[]{:S(2)}) async-start(), calls=%async_computation.16 | async-start | bytes 2359296 | tf_op jit(solution)/shard_map/all_gather | solution.py:161
  7.9 62.4 %all-gather.14.cloned.1.call-start = ((), (), s32[]{:S(2)}) async-start(), calls=%async_computation.13 | async-start | bytes 2359296 | tf_op jit(solution)/shard_map/all_gather | solution.py:160
  8.7 118.0 %all-gather.18.cloned.1.call-start = ((), (), s32[]{:S(2)}) async-start(), calls=%async_computation.15 | async-start | bytes 9437184 | tf_op jit(solution)/shard_map/all_gather | solution.py:159
  9.5 156.4 %all-gather.22.cloned.1.call-start = ((), (), s32[]{:S(2)}) async-start(), calls=%async_computation.17 | async-start | bytes 4718592 | tf_op jit(solution)/shard_map/all_gather | solution.py:197
  12.7 256.8 %copy-start.74 = (f32[1,2048]{1,0:T(1,128)}, f32[1,2048]{1,0:T(1,128)S(1)}, u32[]{:S(2)}) copy-start(f32[1,2048]{1,0:T(1,128)S(1)} %get-tuple-element.683) | copy-start | bytes 24580
  12.7 577.7 %copy-start.82 = (f32[1,2048]{1,0:T(1,128)}, f32[1,2048]{1,0:T(1,128)S(1)}, u32[]{:S(2)}) copy-start(f32[1,2048]{1,0:T(1,128)S(1)} %get-tuple-element.678) | copy-start | bytes 24580
  12.7 581.4 %copy-start.70 = (f32[1,2048]{1,0:T(1,128)}, f32[1,2048]{1,0:T(1,128)S(1)}, u32[]{:S(2)}) copy-start(f32[1,2048]{1,0:T(1,128)S(1)} %get-tuple-element.684) | copy-start | bytes 24580
  28.5 507.3 %copy-start.3 = (f32[1,128,2048]{2,0,1:T(1,128)}, f32[1,128,2048]{2,0,1:T(1,128)S(1)}, u32[]{:S(2)}) copy-start(f32[1,128,2048]{2,0,1:T(1,128)S(1)} %slice.163) | copy-start | bytes 3145732
  28.9 240.7 %copy-start.110 = (f32[128]{0:T(128)}, f32[128]{0:T(128)S(1)}, u32[]{:S(2)}) copy-start(f32[128]{0:T(128)S(1)} %fusion.165) | copy-start | bytes 1540
  68.0 136.9 %all-gather.16.cloned.1.call-start = ((), (), s32[]{:S(2)}) async-start(), calls=%async_computation.14 | async-start | bytes 4718592 | tf_op jit(solution)/shard_map/all_gather | solution.py:196
  68.7 77.1 %copy-start.59 = (f32[128,256]{1,0:T(8,128)}, f32[128,256]{1,0:T(8,128)S(1)}, u32[]{:S(2)}) copy-start(f32[128,256]{1,0:T(8,128)S(1)} %get-tuple-element.675) | copy-start | bytes 393220
  68.7 77.1 %copy-start.61 = (f32[128,256]{1,0:T(8,128)}, f32[128,256]{1,0:T(8,128)S(1)}, u32[]{:S(2)}) copy-start(f32[128,256]{1,0:T(8,128)S(1)} %get-tuple-element.676) | copy-start | bytes 393220
  68.7 77.1 %copy-start.100 = (f32[1,256]{1,0:T(1,128)}, f32[1,256]{1,0:T(1,128)S(1)}, u32[]{:S(2)}) copy-start(f32[1,256]{1,0:T(1,128)S(1)} %get-tuple-element.685) | copy-start | bytes 3076
  97.9 165.3 %all-gather.24.cloned.1.call-start = ((), (), s32[]{:S(2)}) async-start(), calls=%async_computation.18 | async-start | bytes 9437184 | tf_op jit(solution)/shard_map/all_gather | solution.py:162
  98.4 221.0 %all-gather.28.cloned.1.call-start = ((), (), s32[]{:S(2)}) async-start(), calls=%async_computation.20 | async-start | bytes 9437184 | tf_op jit(solution)/shard_map/all_gather | solution.py:166
  147.5 24.8 %all-to-all-start.1 = ((bf16[128,8,256]{2,0,1:T(8,128)(2,1)}), bf16[128,8,256]{2,0,1:T(8,128)(2,1)S(1)}, u32[]{:S(2)}, u32[]{:S(2)}) async-start(bf16[128,8,256]{2,0,1:T(8,128)(2,1)} %fusion.104), calls=%async_computation.1 | async-start | bytes 1048576 | tf_op jit(solution)/shard_map/all_to_all | solution.py:191
  225.4 32.0 %all-to-all-start.3 = ((bf16[512,2,256]{2,1,0:T(2,128)(2,1)}), bf16[512,2,256]{2,1,0:T(2,128)(2,1)S(1)}, u32[]{:S(2)}, u32[]{:S(2)}) async-start(bf16[512,2,256]{2,1,0:T(2,128)(2,1)} %get-tuple-element.639), calls=%async_computation.3 | async-start | bytes 1048576 | tf_op jit(solution)/shard_map/all_to_all | solution.py:243
  230.0 137.6 %all-gather.26.cloned.1.call-start = ((), (), s32[]{:S(2)}) async-start(), calls=%async_computation.19 | async-start | bytes 2621440 | tf_op jit(solution)/shard_map/all_gather | solution.py:254
  273.1 149.5 %all-gather.30.cloned.1.call-start = ((), (), s32[]{:S(2)}) async-start(), calls=%async_computation.21 | async-start | bytes 9437184 | tf_op jit(solution)/shard_map/all_gather | solution.py:167
  273.9 204.9 %all-gather.32.cloned.1.call-start = ((), (), s32[]{:S(2)}) async-start(), calls=%async_computation.22 | async-start | bytes 9437184 | tf_op jit(solution)/shard_map/all_gather | solution.py:168
  274.5 258.2 %reduce-scatter.6.cloned.1.call-start = ((), (), s32[]{:S(2)}) async-start(), calls=%async_computation.23 | async-start | bytes 2621440 | tf_op jit(solution)/shard_map/reduce_scatter | solution.py:260
  488.7 68.8 %all-gather.34.cloned.1.call-start = ((), (), s32[]{:S(2)}) async-start(), calls=%async_computation.24 | async-start | bytes 1179648 | tf_op jit(solution)/shard_map/all_gather | solution.py:164
  489.3 93.8 %all-gather.36.cloned.1.call-start = ((), (), s32[]{:S(2)}) async-start(), calls=%async_computation.25 | async-start | bytes 1179648 | tf_op jit(solution)/shard_map/all_gather | solution.py:165
  490.0 153.7 %all-gather.38.cloned.1.call-start = ((), (), s32[]{:S(2)}) async-start(), calls=%async_computation.26 | async-start | bytes 2621440 | tf_op jit(solution)/shard_map/all_gather | solution.py:281
  597.6 118.8 %reduce-scatter.8.cloned.1.call-start = ((), (), s32[]{:S(2)}) async-start(), calls=%async_computation.27 | async-start | bytes 2621440 | tf_op jit(solution)/shard_map/reduce_scatter | solution.py:286
  728.6 18.0 %all-to-all-start.4 = ((bf16[128,8,256]{2,0,1:T(8,128)(2,1)}), bf16[128,8,256]{2,0,1:T(8,128)(2,1)S(1)}, u32[]{:S(2)}, u32[]{:S(2)}) async-start(bf16[128,8,256]{2,0,1:T(8,128)(2,1)} %bitcast.324), calls=%async_computation.6 | async-start | bytes 1048576 | tf_op jit(solution)/shard_map/all_to_all | solution.py:296
  732.0 115.7 %reduce-scatter.12.cloned.1.call-start = ((), (), s32[]{:S(2)}) async-start(), calls=%async_computation.29 | async-start | bytes 4718592 | tf_op jit(solution)/shard_map/reduce_scatter | solution.py:335
  780.5 122.2 %reduce-scatter.10.cloned.1.call-start = ((), (), s32[]{:S(2)}) async-start(), calls=%async_computation.28 | async-start | bytes 4718592 | tf_op jit(solution)/shard_map/reduce_scatter | solution.py:329
  783.0 17.4 %all-to-all-start.5 = ((bf16[512,2,256]{2,1,0:T(2,128)(2,1)}), bf16[512,2,256]{2,1,0:T(2,128)(2,1)S(1)}, u32[]{:S(2)}, u32[]{:S(2)}) async-start(bf16[512,2,256]{2,1,0:T(2,128)(2,1)} %copy.276), calls=%async_computation.7 | async-start | bytes 1048576 | tf_op jit(solution)/shard_map/all_to_all | solution.py:343
  787.7 68.5 %copy-start.15 = (f32[128,8,256]{2,0,1:T(8,128)S(1)}, f32[128,8,256]{2,0,1:T(8,128)}, u32[]{:S(2)}) copy-start(f32[128,8,256]{2,0,1:T(8,128)} %copy-done.14) | copy-start | bytes 3145732
  787.7 68.6 %copy-start.60 = (f32[128,256]{1,0:T(8,128)S(1)}, f32[128,256]{1,0:T(8,128)}, u32[]{:S(2)}) copy-start(f32[128,256]{1,0:T(8,128)} %copy-done.59) | copy-start | bytes 393220
  787.7 68.6 %copy-start.86 = (f32[128,8]{0,1:T(8,128)S(1)}, f32[128,8]{0,1:T(8,128)}, u32[]{:S(2)}) copy-start(f32[128,8]{0,1:T(8,128)} %copy-done.85) | copy-start | bytes 12292
  787.7 68.6 %copy-start.101 = (f32[1,256]{1,0:T(1,128)S(1)}, f32[1,256]{1,0:T(1,128)}, u32[]{:S(2)}) copy-start(f32[1,256]{1,0:T(1,128)} %copy-done.100) | copy-start | bytes 3076
  850.1 55.0 %all-to-all-start.7 = ((bf16[512,2,256]{2,1,0:T(2,128)(2,1)}), bf16[512,2,256]{2,1,0:T(2,128)(2,1)}, u32[]{:S(2)}, u32[]{:S(2)}) async-start(bf16[512,2,256]{2,1,0:T(2,128)(2,1)} %copy.283), calls=%async_computation.11 | async-start | bytes 1048576 | tf_op jit(solution)/shard_map/all_to_all | solution.py:345
  905.1 19.2 %all-to-all-start.6 = ((bf16[512,2,256]{2,1,0:T(2,128)(2,1)}), bf16[512,2,256]{2,1,0:T(2,128)(2,1)}, u32[]{:S(2)}, u32[]{:S(2)}) async-start(bf16[512,2,256]{2,1,0:T(2,128)(2,1)} %copy.280), calls=%async_computation.9 | async-start | bytes 1048576 | tf_op jit(solution)/shard_map/all_to_all | solution.py:344
  909.7 334.7 %reduce-scatter.14.cloned.1.call-start = ((), (), s32[]{:S(2)}) async-start(), calls=%async_computation.31 | async-start | bytes 54853632 | tf_op jit(solution)/shard_map/reduce_scatter | solution.py:374
  968.5 395.5 %all-reduce.27.cloned.1.call-start = ((), (), s32[]{:S(2)}) async-start(), calls=%async_computation.32 | async-start | bytes 5898240 | tf_op jit(solution)/shard_map/psum | solution.py:404
  1005.7 242.6 %copy-start.124 = (bf16[4,20]{1,0:T(4,128)(2,1)S(1)}, bf16[4,20]{1,0:T(4,128)(2,1)}, u32[]{:S(2)}) copy-start(bf16[4,20]{1,0:T(4,128)(2,1)} %param.36) | copy-start | bytes 484
  1005.7 242.7 %copy-start.118 = (f32[128]{0:T(128)S(1)}, f32[128]{0:T(128)}, u32[]{:S(2)}) copy-start(f32[128]{0:T(128)} %copy-done.117) | copy-start | bytes 1540
  1005.7 244.8 %copy-start.127 = (f32[128]{0:T(128)S(1)}, f32[128]{0:T(128)}, u32[]{:S(2)}) copy-start(f32[128]{0:T(128)} %copy-done.126) | copy-start | bytes 1540
  1005.7 244.8 %copy-start.91 = (f32[2048]{0:T(1024)S(1)}, f32[2048]{0:T(1024)}, u32[]{:S(2)}) copy-start(f32[2048]{0:T(1024)} %get-tuple-element.553) | copy-start | bytes 24580
  1005.7 244.8 %copy-start.92 = (f32[2048]{0:T(1024)S(1)}, f32[2048]{0:T(1024)}, u32[]{:S(2)}) copy-start(f32[2048]{0:T(1024)} %get-tuple-element.660) | copy-start | bytes 24580
  1005.7 244.8 %copy-start.93 = (f32[2048]{0:T(1024)S(1)}, f32[2048]{0:T(1024)}, u32[]{:S(2)}) copy-start(f32[2048]{0:T(1024)} %get-tuple-element.555) | copy-start | bytes 24580
  1005.8 244.8 %copy-start.94 = (f32[2048]{0:T(1024)S(1)}, f32[2048]{0:T(1024)}, u32[]{:S(2)}) copy-start(f32[2048]{0:T(1024)} %get-tuple-element.563) | copy-start | bytes 24580
  1005.8 244.8 %copy-start.95 = (f32[2048]{0:T(1024)S(1)}, f32[2048]{0:T(1024)}, u32[]{:S(2)}) copy-start(f32[2048]{0:T(1024)} %get-tuple-element.565) | copy-start | bytes 24580
  1005.8 244.8 %copy-start.96 = (f32[2048]{0:T(1024)S(1)}, f32[2048]{0:T(1024)}, u32[]{:S(2)}) copy-start(f32[2048]{0:T(1024)} %get-tuple-element.557) | copy-start | bytes 24580
  1005.8 244.8 %copy-start.97 = (f32[2048]{0:T(1024)S(1)}, f32[2048]{0:T(1024)}, u32[]{:S(2)}) copy-start(f32[2048]{0:T(1024)} %get-tuple-element.568) | copy-start | bytes 24580
  1248.2 239.4 %all-reduce.25.cloned.1.call-start = ((), (), s32[]{:S(2)}) async-start(), calls=%async_computation.30 | async-start | bytes 131072 | tf_op jit(solution)/shard_map/psum | solution.py:364
  (118 other events, 1519.6 us)
Sparse Core Ops, SparseCore 0:
  9.9 30.5 all-gather.19
  42.4 27.8 all-gather.13
  72.3 54.3 all-gather.17
  129.0 36.7 all-gather.21
  168.2 36.7 all-gather.15
  206.6 56.4 all-gather.23
  265.1 54.3 all-gather.27
  321.6 45.9 all-gather.25
  369.5 53.0 all-gather.29
  424.4 54.3 all-gather.31
  488.8 43.8 reduce-scatter.5
  534.6 22.8 all-gather.33
  559.5 23.4 all-gather.35
  597.7 45.9 all-gather.37
  673.8 42.5 reduce-scatter.7
  780.6 67.0 reduce-scatter.11
  851.3 51.3 reduce-scatter.9
  968.6 275.8 reduce-scatter.13
  1248.3 115.6 all-reduce.26
  1370.9 116.5 all-reduce.24
where the time goes:
time: 1510 us; the launch traced here: 1500 us
  waiting for transfers between devices  947 us (63%)
  matrix products  201 us (13%)
  local copies, waits for them, and re-layouts  116 us (8%)
  blocking collectives  108 us (7%)
  other arithmetic  73.1 us (5%)
  starting transfers between devices  27.2 us (2%)
  between operations  16.4 us (1%)
    reduce_scatter x1, waiting for transfers between devices, on_device(): lax.psum_scatter(jnp.concatenate([weight_product(normed_low, normed_targe...  239 us
    psum x1, waiting for transfers between devices, on_device(): lax.psum((gains_finish + gains_correct + gains_combine + gains_predict, r...  108 us
    dot_general x11, matrix products, forward_product(): return jnp.dot(left, right, preferred_element_type=jnp.float32)  55.8 us
    unnamed x283, local copies, waits for them, and re-layouts  50.8 us
    all_gather x1, waiting for transfers between devices, on_device(): unit_rows = lax.all_gather(feed_low, 'heads', axis=0, tiled=True)  48.1 us
    all_gather x1, waiting for transfers between devices, on_device(): fed_rows = lax.all_gather(fed_low, 'heads', axis=0, tiled=True)  45.8 us
    all_gather x1, waiting for transfers between devices, on_device(): lax.all_gather(gate_weight, 'blk', axis=0, tiled=True)  45 us
    reduce_scatter x1, waiting for transfers between devices, on_device(): lax.psum_scatter(key_grads.reshape(keys_all.shape).astype(jnp.bfloat16),...  44.5 us
  transfers between devices with their start and end apart: 26, of which 23 were waited for; matrix products, arithmetic and copies ran while one was open for 15% of the time, Pallas kernels for 0%

commit v1 on v0

--- a/solution.py
+++ b/solution.py
@@ -1,6 +1,8 @@
 import jax
 import jax.numpy as jnp
 from jax import lax
+from jax.experimental import pallas as pl
+from jax.experimental.pallas import tpu as pltpu
 from jax.sharding import PartitionSpec as P
 
 QUERY_HEAD_COUNT = 8
@@ -121,7 +123,7 @@
     )
 
 
-def on_device(
+def general_device(
     versions,
     layer_input,
     positions,
@@ -430,7 +432,696 @@
     )
 
 
+CORES = 2
+LINE = 4
+CHIPS = 4
+
+
+def along_heads(x, step):
+    return lax.ppermute(x, "heads", [(i, (i + step) % LINE) for i in range(LINE)])
+
+
+def across_blk(x, mask):
+    return lax.ppermute(x, "blk", [(i, i ^ mask) for i in range(CORES * CHIPS)])
+
+
+def other_core(x):
+    return across_blk(x, 1)
+
+
+def gather_chip(x):
+    half = x.shape[0] // 2
+    before = along_heads(x, 1)
+    after = along_heads(x, -1)
+    far = jnp.concatenate([along_heads(before[:half], 1), along_heads(after[half:], -1)], axis=0)
+    own = [before, x, after, far]
+    return jnp.concatenate(own + [other_core(part) for part in own], axis=0)
+
+
+def scatter_chip(y):
+    wide = jnp.float32
+    n = y.shape[0] // 8
+    half = n // 2
+    before, own, after, far = (
+        y[k * n : (k + 1) * n].astype(wide) + other_core(y[(k + 4) * n : (k + 5) * n]).astype(wide)
+        for k in range(4)
+    )
+    far = far.astype(jnp.bfloat16)
+    first = along_heads(far[:half], 1).astype(wide)
+    second = along_heads(far[half:], -1).astype(wide)
+    after = jnp.concatenate([after[:half] + first, after[half:]], axis=0).astype(jnp.bfloat16)
+    before = jnp.concatenate([before[:half], before[half:] + second], axis=0).astype(jnp.bfloat16)
+    return own + along_heads(after, 1).astype(wide) + along_heads(before, -1).astype(wide)
+
+
+def turn(x, blocks):
+    rows = x.shape[0] // LINE
+    twice = jnp.concatenate([x, x], axis=0)
+    return lax.dynamic_slice_in_dim(twice, blocks * rows, x.shape[0])
+
+
+def natural(x, core, line):
+    half = x.shape[0] // 2
+    own, other = (turn(part, (1 - line) % LINE) for part in (x[:half], x[half:]))
+    first = core == 0
+    return jnp.concatenate([jnp.where(first, own, other), jnp.where(first, other, own)], axis=0)
+
+
+def arrival(x, core, line):
+    half = x.shape[0] // 2
+    first = core == 0
+    own, other = jnp.where(first, x[:half], x[half:]), jnp.where(first, x[half:], x[:half])
+    return jnp.concatenate([turn(part, (line - 1) % LINE) for part in (own, other)], axis=0)
+
+
+def gather_chips(x):
+    half = x.shape[0] // 2
+    side = across_blk(x, 2)
+    front = across_blk(x, 4)
+    return side, front, across_blk(side[:half], 4), across_blk(front[half:], 2)
+
+
+def scatter_chips(parts):
+    wide = jnp.float32
+    half = parts[0].shape[0] // 2
+    own, side, front, far = parts
+    low = across_blk(jnp.concatenate([side[:half], far[:half]], axis=0), 2)
+    high = across_blk(jnp.concatenate([front[half:], far[half:]], axis=0), 4)
+    front_sum = (front[:half].astype(wide) + low[half:].astype(wide)).astype(jnp.bfloat16)
+    side_sum = (side[half:].astype(wide) + high[half:].astype(wide)).astype(jnp.bfloat16)
+    upper = own[:half].astype(wide) + low[:half].astype(wide) + across_blk(front_sum, 4).astype(wide)
+    lower = own[half:].astype(wide) + high[:half].astype(wide) + across_blk(side_sum, 2).astype(wide)
+    return jnp.concatenate([upper, lower], axis=0)
+
+
+def butterfly(x):
+    for mask in (1, 2, 4):
+        x = x + across_blk(x, mask)
+    for mask in (1, 2):
+        x = x + lax.ppermute(x, "heads", [(i, i ^ mask) for i in range(LINE)])
+    return x
+
+
+def chip_groups():
+    return [[core + CORES * chip for chip in range(CHIPS)] for core in range(CORES)]
+
+
+def weight_rows(keep, send, core):
+    got = other_core(send)
+    first = core == 0
+    return jnp.concatenate([jnp.where(first, keep, got), jnp.where(first, got, keep)], axis=0)
+
+
+def all_rows(x):
+    return lax.all_gather(x, "blk", axis=0, tiled=True, axis_index_groups=chip_groups())
+
+
+def own_rows(x):
+    return lax.psum_scatter(
+        x, "blk", scatter_dimension=0, tiled=True, axis_index_groups=chip_groups()
+    )
+
+
+def pick(x, start, size):
+    return lax.dynamic_slice_in_dim(x, start, size, axis=1)
+
+
+QUERY_ROWS = 512
+KEY_ROWS = 512
+
+
+def place_rows(target, parts, chip):
+    own, side, front, near, far = parts
+    size = own.shape[0]
+    half = size // 2
+    target[pl.ds(pl.multiple_of(chip * size, size), size), :] = own[...]
+    target[pl.ds(pl.multiple_of((chip ^ 1) * size, size), size), :] = side[...]
+    target[pl.ds(pl.multiple_of((chip ^ 2) * size, size), size), :] = front[...]
+    base = (chip ^ 3) * size
+    target[pl.ds(pl.multiple_of(base, size), half), :] = near[...]
+    target[pl.ds(pl.multiple_of(base + half, half), half), :] = far[...]
+
+
+def place_both(meta, mine, theirs, k_all, v_all):
+    chip = meta[0]
+
+    @pl.when(meta[1] == 0)
+    def _():
+        place_rows(k_all, mine, chip)
+        place_rows(v_all, theirs, chip)
+
+    @pl.when(meta[1] != 0)
+    def _():
+        place_rows(v_all, mine, chip)
+        place_rows(k_all, theirs, chip)
+
+
+def rows_times_rows(left, right):
+    return lax.dot_general(
+        left, right, (((1,), (1,)), ((), ())), preferred_element_type=jnp.float32
+    )
+
+
+def columns_times_columns(left, right):
+    return lax.dot_general(
+        left, right, (((0,), (0,)), ((), ())), preferred_element_type=jnp.float32
+    )
+
+
+def attend_kernel(meta, q_ref, lo_ref, *refs):
+    mine, theirs = refs[:5], refs[5:10]
+    out_ref, lse_ref, k_all, v_all, total, summed = refs[10:]
+    place_both(meta, mine, theirs, k_all, v_all)
+    own = q_ref.shape[0]
+    for part in range(own // QUERY_ROWS):
+        rows = pl.ds(part * QUERY_ROWS, QUERY_ROWS)
+        first = meta[0] * own + part * QUERY_ROWS
+        total[...] = jnp.zeros_like(total)
+        summed[...] = jnp.zeros_like(summed)
+
+        def visit(block, masked, rows=rows, first=first):
+            at = pl.multiple_of(block * KEY_ROWS, KEY_ROWS)
+            scores = rows_times_rows(q_ref[rows, :], k_all[pl.ds(at, KEY_ROWS), :])
+            weights = jnp.exp(scores)
+            if masked:
+                key = at + lax.broadcasted_iota(jnp.int32, weights.shape, 1)
+                query = first + lax.broadcasted_iota(jnp.int32, weights.shape, 0)
+                weights = jnp.where((key >= lo_ref[rows, :]) & (key <= query), weights, 0.0)
+            for lane in range(0, KEY_ROWS, 128):
+                total[...] += weights[:, lane : lane + 128]
+            summed[...] += jnp.dot(
+                weights.astype(jnp.bfloat16),
+                v_all[pl.ds(at, KEY_ROWS), :],
+                preferred_element_type=jnp.float32,
+            )
+
+        start, full_from = meta[2 + 2 * part], meta[3 + 2 * part]
+        end = (first + QUERY_ROWS - 1) // KEY_ROWS + 1
+        full_from = jnp.minimum(full_from, end)
+        full_to = jnp.maximum(jnp.minimum((first + 1) // KEY_ROWS, end), full_from)
+
+        @pl.loop(start, full_from)
+        def _(block, visit=visit):
+            visit(block, True)
+
+        @pl.loop(full_from, full_to)
+        def _(block, visit=visit):
+            visit(block, False)
+
+        @pl.loop(full_to, end)
+        def _(block, visit=visit):
+            visit(block, True)
+
+        denominator = jnp.sum(total[...], axis=1, keepdims=True)
+        out_ref[rows, :] = summed[...] / denominator
+        lse_ref[rows, :] = jnp.log(denominator)
+
+
+def attend_back_kernel(meta, q_ref, grad_ref, lse_ref, delta_ref, lo_ref, *refs):
+    mine, theirs = refs[:5], refs[5:10]
+    dq_ref, keep_ref, send_ref, k_all, v_all, dk_sum, dv_sum = refs[10:]
+    place_both(meta, mine, theirs, k_all, v_all)
+    chip = meta[0]
+    own = q_ref.shape[0]
+    parts = own // QUERY_ROWS
+    keep_ref[...] = jnp.zeros_like(keep_ref)
+    send_ref[...] = jnp.zeros_like(send_ref)
+    dq_ref[...] = jnp.zeros_like(dq_ref)
+    per_chip = own // KEY_ROWS
+
+    @pl.loop(meta[2], (chip + 1) * per_chip)
+    def _(block):
+        at = pl.multiple_of(block * KEY_ROWS, KEY_ROWS)
+        dk_sum[...] = jnp.zeros_like(dk_sum)
+        dv_sum[...] = jnp.zeros_like(dv_sum)
+        for part in range(parts):
+            rows = pl.ds(part * QUERY_ROWS, QUERY_ROWS)
+            first = chip * own + part * QUERY_ROWS
+
+            def visit(masked, rows=rows, first=first):
+                keys = k_all[pl.ds(at, KEY_ROWS), :]
+                queries = q_ref[rows, :]
+                grads = grad_ref[rows, :]
+                shares = jnp.exp(rows_times_rows(keys, queries) - lse_ref[:, rows])
+                if masked:
+                    key = at + lax.broadcasted_iota(jnp.int32, shares.shape, 0)
+                    query = first + lax.broadcasted_iota(jnp.int32, shares.shape, 1)
+                    shares = jnp.where((key >= lo_ref[:, rows]) & (key <= query), shares, 0.0)
+                share_grad = rows_times_rows(v_all[pl.ds(at, KEY_ROWS), :], grads)
+                score_grad = (shares * (share_grad - delta_ref[:, rows])).astype(jnp.bfloat16)
+                dv_sum[...] += jnp.dot(
+                    shares.astype(jnp.bfloat16), grads, preferred_element_type=jnp.float32
+                )
+                dk_sum[...] += jnp.dot(score_grad, queries, preferred_element_type=jnp.float32)
+                dq_ref[rows, :] += columns_times_columns(score_grad, keys)
+
+            start, full_from = meta[2 + 2 * part], meta[3 + 2 * part]
+            full = (block >= full_from) & ((block + 1) * KEY_ROWS <= first + 1)
+            needed = (block >= start) & (block * KEY_ROWS < first + QUERY_ROWS)
+
+            @pl.when(full)
+            def _(visit=visit):
+                visit(False)
+
+            @pl.when(needed & jnp.logical_not(full))
+            def _(visit=visit):
+                visit(True)
+
+        place = (block // per_chip) ^ chip
+        inner = pl.multiple_of((block % per_chip) * KEY_ROWS, KEY_ROWS)
+        dk_low = dk_sum[...].astype(jnp.bfloat16)
+        dv_low = dv_sum[...].astype(jnp.bfloat16)
+
+        @pl.when(meta[1] == 0)
+        def _():
+            keep_ref[place, pl.ds(inner, KEY_ROWS), :] = dk_low
+            send_ref[place, pl.ds(inner, KEY_ROWS), :] = dv_low
+
+        @pl.when(meta[1] != 0)
+        def _():
+            keep_ref[place, pl.ds(inner, KEY_ROWS), :] = dv_low
+            send_ref[place, pl.ds(inner, KEY_ROWS), :] = dk_low
+
+
+def in_vmem(count):
+    return [pl.BlockSpec(memory_space=pltpu.VMEM)] * count
+
+
+def attend_here(meta, q, lo, mine, theirs):
+    own, width = q.shape
+    row = own * CHIPS
+    return pl.pallas_call(
+        attend_kernel,
+        out_shape=(
+            jax.ShapeDtypeStruct((own, width), jnp.float32),
+            jax.ShapeDtypeStruct((own, 1), jnp.float32),
+        ),
+        in_specs=[pl.BlockSpec(memory_space=pltpu.SMEM)] + in_vmem(12),
+        out_specs=tuple(in_vmem(2)),
+        scratch_shapes=[
+            pltpu.VMEM((row, width), jnp.bfloat16),
+            pltpu.VMEM((row, width), jnp.bfloat16),
+            pltpu.VMEM((QUERY_ROWS, 128), jnp.float32),
+            pltpu.VMEM((QUERY_ROWS, width), jnp.float32),
+        ],
+        compiler_params=pltpu.CompilerParams(vmem_limit_bytes=40 << 20),
+        cost_estimate=pl.CostEstimate(
+            flops=2 * own * row * width, bytes_accessed=6 * row * width, transcendentals=own * row // 2
+        ),
+    )(meta, q, lo.reshape(own, 1), *mine, *theirs)
+
+
+def attend_back_here(meta, q, grad, lse, delta, lo, mine, theirs):
+    own, width = q.shape
+    row = own * CHIPS
+    return pl.pallas_call(
+        attend_back_kernel,
+        out_shape=(
+            jax.ShapeDtypeStruct((own, width), jnp.float32),
+            jax.ShapeDtypeStruct((CHIPS, own, width), jnp.bfloat16),
+            jax.ShapeDtypeStruct((CHIPS, own, width), jnp.bfloat16),
+        ),
+        in_specs=[pl.BlockSpec(memory_space=pltpu.SMEM)] + in_vmem(15),
+        out_specs=tuple(in_vmem(3)),
+        scratch_shapes=[
+            pltpu.VMEM((row, width), jnp.bfloat16),
+            pltpu.VMEM((row, width), jnp.bfloat16),
+            pltpu.VMEM((KEY_ROWS, width), jnp.float32),
+            pltpu.VMEM((KEY_ROWS, width), jnp.float32),
+        ],
+        compiler_params=pltpu.CompilerParams(vmem_limit_bytes=48 << 20),
+        cost_estimate=pl.CostEstimate(
+            flops=5 * own * row * width, bytes_accessed=12 * row * width, transcendentals=own * row // 2
+        ),
+    )(
+        meta, q, grad, lse.reshape(1, own), delta.reshape(1, own), lo.reshape(1, own), *mine, *theirs
+    )
+
+
+def predict_list(versions, gain_rows, router, coefficients):
+    table = jnp.dot(
+        modes(versions[0], gain_rows[0], router), coefficients[:, :16], precision=highest
+    )
+    predicted = []
+    for i in range(4):
+        value = versions[i]
+        for j in range(4):
+            value = value + table[:, 4 * i + j : 4 * i + j + 1] * versions[j]
+        predicted.append(value)
+    return (tuple(predicted), rms_norm_apply(predicted[0], gain_rows[1]))
+
+
+def correct_list(merged, fed, predicted, gain_rows, router, coefficients):
+    activated = merged + rms_norm_apply(fed, gain_rows[5])
+    scale = (
+        jnp.dot(modes(activated, gain_rows[0], router), coefficients[:, 16:], precision=highest)
+        + 1.0
+    )
+    change = activated - predicted[0]
+    corrected = tuple(predicted[i] + scale[:, i : i + 1] * change for i in range(4))
+    return (corrected, corrected[0] * gain_rows[6])
+
+
+def head_apply(x, gain, cosine, sine):
+    normed = x * lax.rsqrt(jnp.mean(x * x, axis=-1, keepdims=True) + epsilon) * gain
+    half = x.shape[-1] // 2
+    turned = jnp.concatenate([-normed[:, half:], normed[:, :half]], axis=-1)
+    return normed * cosine + turned * sine
+
+
+def chip_device(
+    versions,
+    layer_input,
+    positions,
+    documents,
+    cotangent,
+    norm_gains,
+    router_weight,
+    coefficients,
+    query_key_gains,
+    query_weight,
+    key_matrix,
+    value_matrix,
+    out_weight,
+    laurel_weight,
+    input_gate,
+    input_projection,
+    gate_weight,
+    up_weight,
+    down_weight,
+):
+    narrow = jnp.bfloat16
+    wide = jnp.float32
+    line = lax.axis_index("heads")
+    piece = lax.axis_index("blk")
+    core = piece % CORES
+    chip = piece // CORES
+    first_core = core == 0
+    tokens = versions.shape[1]
+    own = 8 * tokens
+    width = versions.shape[2]
+    rows_here = query_weight.shape[0]
+    hidden = gate_weight.shape[1] // CORES
+    head = CORES * line + core
+    group = head // (QUERY_HEAD_COUNT // KEY_VALUE_HEADS)
+
+    def head_columns(index, kv):
+        return jnp.concatenate(
+            [
+                pick(query_weight, index * HEAD_WIDTH, HEAD_WIDTH),
+                pick(kv, group * HEAD_WIDTH, HEAD_WIDTH),
+                pick(out_weight, index * HEAD_WIDTH, HEAD_WIDTH),
+            ],
+            axis=1,
+        )
+
+    kv_mine = jnp.where(first_core, key_matrix, value_matrix)
+    kv_theirs = jnp.where(first_core, value_matrix, key_matrix)
+    head_full = all_rows(
+        weight_rows(head_columns(head, kv_mine), head_columns(head ^ 1, kv_theirs), core)
+    )
+    small_full = lax.all_gather(
+        jnp.concatenate([laurel_weight, input_gate, input_projection], axis=1),
+        "blk",
+        axis=0,
+        tiled=True,
+    )
+
+    def hidden_columns(index):
+        return jnp.concatenate(
+            [pick(w, index * hidden, hidden) for w in (gate_weight, up_weight, down_weight)], axis=1
+        )
+
+    unit_full = all_rows(weight_rows(hidden_columns(core), hidden_columns(1 - core), core))
+    query_kv_full = head_full[:, : 2 * HEAD_WIDTH]
+    out_full = head_full[:, 2 * HEAD_WIDTH :]
+    laurel_full = small_full[:, : 2 * LAUREL_RANK]
+    gate_full = small_full[:, 2 * LAUREL_RANK : 2 * LAUREL_RANK + LAYER_INPUT_SIZE]
+    projection_full = small_full[:, 2 * LAUREL_RANK + LAYER_INPUT_SIZE :]
+    unit_gate = unit_full[:, :hidden]
+    unit_up = unit_full[:, hidden : 2 * hidden]
+    unit_down = unit_full[:, 2 * hidden :]
+
+    gain_rows = norm_gains.astype(wide)
+    router_wide = router_weight.astype(wide)
+    coef_wide = coefficients.astype(wide)
+    head_wide = query_key_gains.astype(wide)
+    (predicted, normed), pull_predict = jax.vjp(
+        predict_list,
+        tuple(versions[i].astype(wide) for i in range(4)),
+        gain_rows,
+        router_wide,
+        coef_wide,
+    )
+    normed_low = normed.astype(narrow)
+
+    digits = jnp.stack([positions // 128, positions % 128], axis=1).astype(narrow)
+    sent = jnp.concatenate([normed_low, jnp.pad(digits, ((0, 0), (0, 126)))], axis=1)
+    gathered = gather_chip(sent)
+    normed_rows = gathered[:, :width]
+    digits_all = natural(gathered[:, width : width + 2].astype(wide), core, line)
+    phase_position = digits_all[:, :1] * 128.0 + digits_all[:, 1:2]
+    frequency = rotary_base ** (-2.0 * jnp.arange(HEAD_WIDTH // 2, dtype=wide) / HEAD_WIDTH)
+    phase = phase_position * frequency[None, :]
+    phase = jnp.concatenate([phase, phase], axis=-1)
+    cosine, sine = jnp.cos(phase), jnp.sin(phase)
+    cosine_kv = jnp.where(first_core, cosine, 1.0)
+    sine_kv = jnp.where(first_core, sine, 0.0)
+
+    def kv_gain(gains):
+        return jnp.where(first_core, gains[1], 1.0)
+
+    query_kv = natural(forward_product(normed_rows, query_kv_full), core, line)
+    query_pre = query_kv[:, :HEAD_WIDTH]
+    kv_pre = query_kv[:, HEAD_WIDTH:]
+    rotated = head_apply(query_pre, head_wide[0], cosine, sine).astype(narrow)
+    kv_own = head_apply(kv_pre, kv_gain(head_wide), cosine_kv, sine_kv).astype(narrow)
+    mine = (kv_own, *gather_chips(kv_own))
+    theirs = tuple(other_core(part) for part in mine)
+
+    first_row = chip * own
+    row_docs = lax.dynamic_slice_in_dim(documents, first_row, own)
+    begin_one = jnp.sum(documents < 1)
+    begin_two = jnp.sum(documents < 2)
+    lo = jnp.where(row_docs == 0, 0, jnp.where(row_docs == 1, begin_one, begin_two)).astype(jnp.int32)
+    bounds = []
+    for part in range(own // QUERY_ROWS):
+        bounds.append(lo[part * QUERY_ROWS] // KEY_ROWS)
+        bounds.append((lo[(part + 1) * QUERY_ROWS - 1] + KEY_ROWS - 1) // KEY_ROWS)
+    meta = jnp.stack([chip, core, *bounds]).astype(jnp.int32)
+    attended, lse = attend_here(meta, rotated, lo, mine, theirs)
+    mixed_rows = arrival(attended.astype(narrow), core, line)
+    attention_out = scatter_chip(transposed_product(mixed_rows, out_full).astype(narrow))
+
+    down_low = forward_product(normed_low, laurel_full[:, :LAUREL_RANK]).astype(narrow)
+    lifted = transposed_product(down_low, laurel_full[:, LAUREL_RANK:])
+    (merged, feed_in), pull_combine = jax.vjp(
+        combine, predicted[0], attention_out, normed_low.astype(wide), lifted, gain_rows
+    )
+    unit_rows = gather_chip(feed_in.astype(narrow))
+    hidden_units, pull_activate = jax.vjp(
+        activate, forward_product(unit_rows, unit_gate), forward_product(unit_rows, unit_up)
+    )
+    hidden_low = hidden_units.astype(narrow)
+    fed = scatter_chip(transposed_product(hidden_low, unit_down).astype(narrow))
+    (corrected, first), pull_correct = jax.vjp(
+        correct_list, merged, fed, predicted, gain_rows, router_wide, coef_wide
+    )
+    first_low = first.astype(narrow)
+    gated, pull_gate = jax.vjp(
+        activate, forward_product(first_low, gate_full), layer_input.astype(wide)
+    )
+    gated_low = gated.astype(narrow)
+    projected = transposed_product(gated_low, projection_full)
+    extra, pull_extra = jax.vjp(rms_norm_apply, projected, gain_rows[7])
+    result = jnp.stack(
+        [corrected[0].astype(narrow)] + [(corrected[i] + extra).astype(narrow) for i in (1, 2, 3)]
+    )
+
+    corrected_grad = tuple(cotangent[i].astype(wide) for i in range(4))
+    projected_grad, gain_seven = pull_extra(
+        corrected_grad[1] + corrected_grad[2] + corrected_grad[3]
+    )
+    projected_low = projected_grad.astype(narrow)
+    gate_pre_grad, layer_grad = pull_gate(forward_product(projected_low, projection_full))
+    gate_pre_low = gate_pre_grad.astype(narrow)
+    merged_grad, fed_grad, predicted_grad, gains_correct, router_correct, coef_correct = (
+        pull_correct((corrected_grad, transposed_product(gate_pre_low, gate_full)))
+    )
+    fed_rows = gather_chip(fed_grad.astype(narrow))
+    gate_grad, up_grad = pull_activate(forward_product(fed_rows, unit_down))
+    gate_low = gate_grad.astype(narrow)
+    up_low = up_grad.astype(narrow)
+    feed_grad = scatter_chip(
+        (transposed_product(gate_low, unit_gate) + transposed_product(up_low, unit_up)).astype(narrow)
+    )
+    unit_sum = own_rows(
+        jnp.concatenate(
+            [
+                weight_product(unit_rows, gate_low).astype(narrow),
+                weight_product(unit_rows, up_low).astype(narrow),
+                weight_product(fed_rows, hidden_low).astype(narrow),
+            ],
+            axis=1,
+        )
+    )
+    active_grad, attention_grad, normed_combine, lifted_grad, gains_combine = pull_combine(
+        (merged_grad, feed_grad)
+    )
+    lifted_low = lifted_grad.astype(narrow)
+    down_grad_low = forward_product(lifted_low, laurel_full[:, LAUREL_RANK:]).astype(narrow)
+    attention_rows = gather_chip(attention_grad.astype(narrow))
+    mixed_grad_rows = forward_product(attention_rows, out_full).astype(narrow)
+    mixed_grad = natural(mixed_grad_rows, core, line)
+    delta = jnp.sum(mixed_grad.astype(wide) * attended, axis=-1)
+    query_grad, kv_keep, kv_send = attend_back_here(
+        meta, rotated, mixed_grad, lse, delta, lo, mine, theirs
+    )
+    kv_got = other_core(kv_send)
+    kv_sum = scatter_chips(
+        [(kv_keep[m].astype(wide) + kv_got[m].astype(wide)).astype(narrow) for m in range(CHIPS)]
+    )
+    half = own // 2
+    mine_first = line % 2 == 0
+    kv_sum_low = kv_sum.astype(narrow)
+    kv_away = jnp.where(mine_first, kv_sum_low[half:], kv_sum_low[:half])
+    kv_back = jnp.where(mine_first, kv_sum[:half], kv_sum[half:]) + lax.ppermute(
+        kv_away, "heads", [(i, i ^ 1) for i in range(LINE)]
+    ).astype(wide)
+
+    def own_half(x):
+        return jnp.where(mine_first, x[:half], x[half:])
+
+    _, pull_query = jax.vjp(
+        lambda x, g: head_apply(x, g, cosine, sine), query_pre, head_wide[0]
+    )
+    query_pre_grad, query_gain_grad = pull_query(query_grad.astype(narrow).astype(wide))
+    _, pull_kv = jax.vjp(
+        lambda x, g: head_apply(x, kv_gain(g), own_half(cosine_kv), own_half(sine_kv)),
+        own_half(kv_pre),
+        head_wide,
+    )
+    kv_pre_grad, kv_gain_grad = pull_kv(kv_back)
+    kv_low = kv_pre_grad.astype(narrow)
+    nothing = jnp.zeros_like(kv_low)
+    kv_both = jnp.concatenate(
+        [jnp.where(mine_first, kv_low, nothing), jnp.where(mine_first, nothing, kv_low)], axis=0
+    )
+    head_grads = arrival(
+        jnp.concatenate([query_pre_grad.astype(narrow), kv_both], axis=1), core, line
+    )
+    normed_sum = scatter_chip(transposed_product(head_grads, query_kv_full).astype(narrow))
+    normed_grad = (
+        normed_combine
+        + normed_sum
+        + transposed_product(down_grad_low, laurel_full[:, :LAUREL_RANK])
+    )
+    predicted_grad = (predicted_grad[0] + active_grad, *predicted_grad[1:])
+    version_grad, gains_predict, router_predict, coef_predict = pull_predict(
+        (predicted_grad, normed_grad)
+    )
+
+    gains_grad = (gains_correct + gains_combine + gains_predict).at[7].add(gain_seven)
+    head_gain_grad = kv_gain_grad.at[0].add(query_gain_grad)
+    coef_grad = coef_correct + coef_predict
+    packed = jnp.concatenate(
+        [
+            gains_grad,
+            router_correct + router_predict,
+            jnp.pad(
+                jnp.concatenate([head_gain_grad.reshape(1, -1), coef_grad.reshape(1, -1)], axis=1),
+                ((0, 3), (0, width - head_gain_grad.size - coef_grad.size)),
+            ),
+        ],
+        axis=0,
+    )
+    packed = butterfly(packed)
+    head_gain_sum = packed[12, : head_gain_grad.size].reshape(head_gain_grad.shape)
+    coef_sum = packed[12, head_gain_grad.size : head_gain_grad.size + coef_grad.size].reshape(
+        coef_grad.shape
+    )
+
+    small_sum = lax.psum(
+        lax.psum_scatter(
+            jnp.concatenate(
+                [
+                    weight_product(normed_low, down_grad_low),
+                    weight_product(lifted_low, down_low),
+                    weight_product(first_low, gate_pre_low),
+                    weight_product(projected_low, gated_low),
+                ],
+                axis=1,
+            ).astype(narrow),
+            "blk",
+            scatter_dimension=0,
+            tiled=True,
+        ),
+        "heads",
+    ).astype(wide)
+    head_sum = own_rows(
+        jnp.concatenate(
+            [
+                weight_product(normed_rows, head_grads).astype(narrow),
+                weight_product(attention_rows, mixed_rows).astype(narrow),
+            ],
+            axis=1,
+        )
+    )
+
+    def core_columns(x):
+        top, bottom = x[:rows_here], x[rows_here:]
+        keep = jnp.where(first_core, top, bottom)
+        got = other_core(jnp.where(first_core, bottom, top))
+        return jnp.where(first_core, keep, got), jnp.where(first_core, got, keep)
+
+    head_first, head_second = core_columns(head_sum)
+    unit_first, unit_second = core_columns(unit_sum)
+
+    def both(index):
+        columns = slice(index * HEAD_WIDTH, (index + 1) * HEAD_WIDTH)
+        return [head_first[:, columns], head_second[:, columns]]
+
+    line_all = lax.all_gather(
+        jnp.concatenate(both(0) + both(2) + both(1), axis=1), "heads", axis=0, tiled=False
+    ).astype(wide)
+    pair = CORES * HEAD_WIDTH
+    query_sum = jnp.concatenate([line_all[i, :, :pair] for i in range(LINE)], axis=1)
+    out_sum = jnp.concatenate([line_all[i, :, pair : 2 * pair] for i in range(LINE)], axis=1)
+    kv_lines = line_all[:, :, 2 * pair :]
+    kv_groups = [kv_lines[0] + kv_lines[1], kv_lines[2] + kv_lines[3]]
+    key_sum = jnp.concatenate([g[:, :HEAD_WIDTH] for g in kv_groups], axis=1)
+    value_sum = jnp.concatenate([g[:, HEAD_WIDTH:] for g in kv_groups], axis=1)
+
+    def unit(index):
+        columns = slice(index * hidden, (index + 1) * hidden)
+        return jnp.concatenate([unit_first[:, columns], unit_second[:, columns]], axis=1).astype(wide)
+
+    ranks = 2 * LAUREL_RANK
+    return (
+        result,
+        jnp.stack([g.astype(narrow) for g in version_grad]),
+        layer_grad.astype(narrow),
+        packed[:8],
+        packed[8:12],
+        coef_sum,
+        head_gain_sum,
+        query_sum,
+        key_sum,
+        value_sum,
+        out_sum,
+        small_sum[:, :ranks],
+        small_sum[:, ranks : ranks + LAYER_INPUT_SIZE],
+        small_sum[:, ranks + LAYER_INPUT_SIZE :],
+        unit(0),
+        unit(1),
+        unit(2),
+    )
+
+
 def solution(mesh):
+    by_chip = mesh.shape["heads"] == LINE and mesh.shape["blk"] == CORES * CHIPS
+    on_device = chip_device if by_chip else general_device
+
     in_specs = (
         P(None, ("blk", "heads"), None),
         P(("blk", "heads"), None),

time: 1510 us -> 939 us (0.62)
  waiting for transfers between devices: 947 us -> 449 us
  starting transfers between devices: 27.2 us -> 138 us
  blocking collectives: 108 us -> 0 us
  matrix products: 201 us -> 112 us
  other arithmetic: 73.1 us -> 120 us
  local copies, waits for them, and re-layouts: 116 us -> 75.6 us
    all_gather x13 -> x4, waiting for transfers between devices: 353 us -> 0.03 us  [the longest x2 0.02 us: all_rows(): lax.all_gather(x, 'blk', axis=0, tiled=True, axis_index_groups=chip_group...]
    ppermute x0 -> x88, waiting for transfers between devices: none -> 295 us  [the longest x32 228 us: along_heads(): lax.ppermute(x, 'heads', [(i, (i + step) % LINE) for i in range(LINE)])]
    reduce_scatter x5 -> x3, waiting for transfers between devices: 409 us -> 153 us  [the longest x2 108 us: own_rows(): lax.psum_scatter(x, 'blk', scatter_dimension=0, tiled=True, axis_index_gr...]
    psum x2 -> x1, waiting for transfers between devices: 145 us -> 0.01 us  [chip_device(): lax.psum(lax.psum_scatter(jnp.concatenate([weight_product(normed_low, dow...]
    ppermute x0 -> x88, starting transfers between devices: none -> 138 us  [the longest x32 78.6 us: along_heads(): lax.ppermute(x, 'heads', [(i, (i + step) % LINE) for i in range(LINE)])]
    dot_general x16 -> x6, matrix products: 56.1 us -> 1.59 us  [the longest x3 1.16 us: correct_list(): jnp.dot(modes(activated, gain_rows[0], router), coefficients[:, 16:], pre...]
    concatenate x1 -> x35, other arithmetic: 0.01 us -> 44.1 us  [the longest x1 21.4 us: chip_device(): jnp.concatenate([weight_product(unit_rows, gate_low).astype(narrow), weig...]
    psum x1 -> x0, blocking collectives: 43.5 us -> none  [on_device(): lax.psum((gains_finish + gains_correct + gains_combine + gains_predict, r...]
  transfers between devices with their start and end apart: 26 -> 96, of which waited for: 23 -> 58; matrix products, arithmetic and copies ran while one was open for 15% -> 21% of each run, Pallas kernels for 0% -> 0%
where the time goes in v1:
time: 939 us; the launch traced here: 932 us
  waiting for transfers between devices  449 us (48%)
  starting transfers between devices  138 us (15%)
  other arithmetic  120 us (13%)
  matrix products  112 us (12%)
  local copies, waits for them, and re-layouts  75.6 us (8%)
  between operations  24.7 us (3%)
  Pallas kernels  11.8 us (1%)
    ppermute x32, waiting for transfers between devices, along_heads(): lax.ppermute(x, 'heads', [(i, (i + step) % LINE) for i in range(LINE)])  228 us
    reduce_scatter x2, waiting for transfers between devices, own_rows(): lax.psum_scatter(x, 'blk', scatter_dimension=0, tiled=True, axis_index_gr...  108 us
    ppermute x32, starting transfers between devices, along_heads(): lax.ppermute(x, 'heads', [(i, (i + step) % LINE) for i in range(LINE)])  78.6 us
    ppermute x53, waiting for transfers between devices, across_blk(): return lax.ppermute(x, 'blk', [(i, i ^ mask) for i in range(CORES * CHIPS)])  57.7 us
    ppermute x53, starting transfers between devices, across_blk(): return lax.ppermute(x, 'blk', [(i, i ^ mask) for i in range(CORES * CHIPS)])  48.1 us
    unnamed x416, local copies, waits for them, and re-layouts  46.6 us
    reduce_scatter x1, waiting for transfers between devices, chip_device(): lax.psum_scatter(jnp.concatenate([weight_product(normed_low, down_grad_lo...  45.6 us
    dot_general x9, matrix products, forward_product(): return jnp.dot(left, right, preferred_element_type=jnp.float32)  42.8 us
  transfers between devices with their start and end apart: 96, of which 58 were waited for; matrix products, arithmetic and copies ran while one was open for 21% of the time, Pallas kernels for 0%

profile of v1, /device:TPU:0, one launch (start us, length us, event | category | flops | bytes accessed | tf_op | source)
XLA Modules:
  0.0 931.9 jit_solution(11357741755633341687)
XLA Ops:
  35.0 5.0 collective-permute-start.1
  45.0 8.4 collective-permute-done.1
  58.6 7.5 collective-permute-done
  72.1 5.1 collective-permute-done.2
  81.8 5.4 fusion.19
  97.2 12.9 %collective-permute-done.10.refs_2_ = bf16[1024,256]{1,0:T(8,128)(2,1)S(1)} collective-permute-done((bf16[1024,256]{1,0:T(8,128)(2,1)S(1)}, bf16[1024,256]{1,0:T(8,128)(2,1)S(1)}, u32[]{:S(2)}, u32[]{:S(2)}) %collective-permute-start.10) | collective-permute-done | bytes 524320 | tf_op jit(solution)/shard_map/ppermute | solution.py:445
  115.3 9.3 %collective-permute-done.12.refs_4_ = bf16[512,256]{1,0:T(8,128)(2,1)S(1)} collective-permute-done((bf16[512,256]{1,0:T(8,128)(2,1)S(1)}, bf16[512,256]{1,0:T(8,128)(2,1)S(1)}, u32[]{:S(2)}, u32[]{:S(2)}) %collective-permute-start.12) | collective-permute-done | bytes 262176 | tf_op jit(solution)/shard_map/ppermute | solution.py:445
  157.9 6.5 collective-permute-done.24
  176.4 6.2 collective-permute-done.25
  182.6 10.4 %collective-permute-done.22 = bf16[128,2048]{1,0:T(8,128)(2,1)} collective-permute-done((bf16[128,2048]{1,0:T(8,128)(2,1)}, bf16[128,2048]{1,0:T(8,128)(2,1)}, u32[]{:S(2)}, u32[]{:S(2)}) %collective-permute-start.22) | collective-permute-done | bytes 524320 | tf_op jit(solution)/shard_map/ppermute | solution.py:441
  199.9 12.3 %collective-permute-done.27 = bf16[128,2048]{1,0:T(8,128)(2,1)S(1)} collective-permute-done((bf16[128,2048]{1,0:T(8,128)(2,1)S(1)}, bf16[128,2048]{1,0:T(8,128)(2,1)S(1)}, u32[]{:S(2)}, u32[]{:S(2)}) %collective-permute-start.27) | collective-permute-done | bytes 524320 | tf_op jit(solution)/shard_map/ppermute | solution.py:441
  216.6 7.9 collective-permute-done.26
  229.9 4.9 collective-permute-done.28
  239.8 7.7 fusion.15
  247.5 10.7 %multiply_convert_fusion.1 = (bf16[1024,1024]{1,0:T(8,128)(2,1)S(1)}, f32[1024,1024]{1,0:T(8,128)}) fusion(f32[1024,1024]{1,0:T(8,128)S(1)} %fusion.15, bf16[1024,2048]{1,0:T(8,128)(2,1)} %constant_dynamic-update-slice_fusion.9, bf16[2048,3072]{0,1:T(8,128)(2,1)S(1)} %copy-done.163), kind=kOutput, calls=%fused_computation.25 | convolution fusion | flops 4305453056 | bytes 18874368 | tf_op jit(solution)/shard_map/dot_general | solution.py:111
  270.6 6.5 collective-permute-done.41
  285.6 9.6 %collective-permute-done.42 = bf16[128,2048]{1,0:T(8,128)(2,1)S(1)} collective-permute-done((bf16[128,2048]{1,0:T(8,128)(2,1)S(1)}, bf16[128,2048]{1,0:T(8,128)(2,1)S(1)}, u32[]{:S(2)}, u32[]{:S(2)}) %collective-permute-start.42) | collective-permute-done | bytes 524320 | tf_op jit(solution)/shard_map/ppermute | solution.py:441
  295.2 10.8 %collective-permute-done.39 = bf16[128,2048]{1,0:T(8,128)(2,1)S(1)} collective-permute-done((bf16[128,2048]{1,0:T(8,128)(2,1)S(1)}, bf16[128,2048]{1,0:T(8,128)(2,1)S(1)}, u32[]{:S(2)}, u32[]{:S(2)}) %collective-permute-start.39) | collective-permute-done | bytes 524320 | tf_op jit(solution)/shard_map/ppermute | solution.py:441
  325.7 12.3 %collective-permute-done.44 = bf16[128,2048]{1,0:T(8,128)(2,1)S(1)} collective-permute-done((bf16[128,2048]{1,0:T(8,128)(2,1)S(1)}, bf16[128,2048]{1,0:T(8,128)(2,1)S(1)}, u32[]{:S(2)}, u32[]{:S(2)}) %collective-permute-start.44) | collective-permute-done | bytes 524320 | tf_op jit(solution)/shard_map/ppermute | solution.py:441
  342.3 7.9 collective-permute-done.43
  355.7 4.9 collective-permute-done.45
  362.6 12.2 %multiply_convert_fusion = (bf16[1024,1024]{1,0:T(8,128)(2,1)}, bf16[1024,1024]{1,0:T(8,128)(2,1)S(1)}) fusion(f32[1024,1024]{1,0:T(8,128)} %copy-done.173, f32[1024,1024]{1,0:T(8,128)} %get-tuple-element.342, bf16[1024,2048]{1,0:T(8,128)(2,1)S(1)} %constant_dynamic-update-slice_fusion.18, bf16[2048,3072]{0,1:T(8,128)(2,1)S(1)} %copy-done.163), kind=kOutput, calls=%fused_computation.24 | convolution fusion | flops 4320133120 | bytes 20971520 | tf_op jit(solution)/shard_map/dot_general | solution.py:111
  374.8 6.8 fusion.13
  381.6 7.6 add_convert_fusion
  396.6 6.5 collective-permute-done.57
  411.4 9.8 %collective-permute-done.58 = bf16[128,2048]{1,0:T(8,128)(2,1)S(1)} collective-permute-done((bf16[128,2048]{1,0:T(8,128)(2,1)S(1)}, bf16[128,2048]{1,0:T(8,128)(2,1)S(1)}, u32[]{:S(2)}, u32[]{:S(2)}) %collective-permute-start.58) | collective-permute-done | bytes 524320 | tf_op jit(solution)/shard_map/ppermute | solution.py:441
  421.2 10.5 %collective-permute-done.55 = bf16[128,2048]{1,0:T(8,128)(2,1)S(1)} collective-permute-done((bf16[128,2048]{1,0:T(8,128)(2,1)S(1)}, bf16[128,2048]{1,0:T(8,128)(2,1)S(1)}, u32[]{:S(2)}, u32[]{:S(2)}) %collective-permute-start.55) | collective-permute-done | bytes 524320 | tf_op jit(solution)/shard_map/ppermute | solution.py:441
  439.3 12.2 %collective-permute-done.60 = bf16[128,2048]{1,0:T(8,128)(2,1)} collective-permute-done((bf16[128,2048]{1,0:T(8,128)(2,1)}, bf16[128,2048]{1,0:T(8,128)(2,1)}, u32[]{:S(2)}, u32[]{:S(2)}) %collective-permute-start.60) | collective-permute-done | bytes 524320 | tf_op jit(solution)/shard_map/ppermute | solution.py:441
  456.8 7.0 collective-permute-done.59
  481.9 7.7 shard_map.315
  495.7 8.7 collective-permute-start.68
  504.5 13.0 %collective-permute-start.70 = (bf16[1024,256]{1,0:T(8,128)(2,1)S(1)}, bf16[1024,256]{1,0:T(8,128)(2,1)S(1)}, u32[]{:S(2)}, u32[]{:S(2)}) collective-permute-start(bf16[1024,256]{1,0:T(8,128)(2,1)S(1)} %pad_maximum_fusion.29), channel_id=1, source_target_pairs={{0,4},{1,5},{2,6},{3,7},{4,0},{5,1},{6,2},{7,3},{8,12},{9,13},{10,... | collective-permute-start | bytes 1572872 | tf_op jit(solution)/shard_map/ppermute | solution.py:445
  521.0 8.9 collective-permute-start.69
  539.9 5.0 collective-permute-done.72
  559.4 37.3 %reduce-scatter.4.cloned.1.call-done = bf16[512,768]{0,1:T(8,128)(2,1)} async-done(((bf16[2048,768]{0,1:T(8,128)(2,1)}), bf16[512,768]{0,1:T(8,128)(2,1)}) %reduce-scatter.4.cloned.1.call-update) | async-done | bytes 786448 | tf_op jit(solution)/shard_map/reduce_scatter | solution.py:540
  598.0 45.6 %reduce-scatter.6.cloned.1.call-done = bf16[256,640]{0,1:T(8,128)(2,1)} async-done(((bf16[2048,640]{0,1:T(8,128)(2,1)}), bf16[256,640]{0,1:T(8,128)(2,1)}) %reduce-scatter.6.cloned.1.call-update) | async-done | bytes 327696 | tf_op jit(solution)/shard_map/reduce_scatter | solution.py:1045
  645.9 7.2 convolution_convert_fusion.2
  653.1 7.2 convolution_convert_fusion.3
  660.3 7.0 convolution_convert_fusion.4
  667.3 21.4 %pad_maximum_fusion = bf16[2048,3072]{0,1:T(8,128)(2,1)} fusion(bf16[2048,1024]{0,1:T(8,128)(2,1)S(1)} %convolution_convert_fusion.2, bf16[2048,1024]{0,1:T(8,128)(2,1)S(1)} %convolution_convert_fusion.3, bf16[2048,1024]{0,1:T(8,128)(2,1)S(1)} %convolution_convert_fusion.4), kind=kLoop, calls=%fused_computation | loop fusion | flops 37748736 | bytes 25165824 | tf_op jit(solution)/shard_map/concatenate | solution.py:959
  709.1 16.0 %collective-permute-done.79 = bf16[64,2048]{1,0:T(8,128)(2,1)} collective-permute-done((bf16[64,2048]{1,0:T(8,128)(2,1)}, bf16[64,2048]{1,0:T(8,128)(2,1)}, u32[]{:S(2)}, u32[]{:S(2)}) %collective-permute-start.79) | collective-permute-done | bytes 262176 | tf_op jit(solution)/shard_map/ppermute | solution.py:441
  728.9 9.4 %collective-permute-start.77 = (bf16[128,2048]{1,0:T(8,128)(2,1)}, bf16[128,2048]{1,0:T(8,128)(2,1)}, u32[]{:S(2)}, u32[]{:S(2)}) collective-permute-start(bf16[128,2048]{1,0:T(8,128)(2,1)} %pad_maximum_fusion.30), channel_id=1, source_target_pairs={{0,8},{8,16},{16,24},{24,0},{1,9},{9,17},{17,25},{25,1},{2,10},{10... | collective-permute-start | bytes 1572872 | tf_op jit(solution)/shard_map/ppermute | solution.py:441
  742.8 21.6 %collective-permute-done.80 = bf16[128,2048]{1,0:T(8,128)(2,1)} collective-permute-done((bf16[128,2048]{1,0:T(8,128)(2,1)}, bf16[128,2048]{1,0:T(8,128)(2,1)}, u32[]{:S(2)}, u32[]{:S(2)}) %collective-permute-start.80) | collective-permute-done | bytes 524320 | tf_op jit(solution)/shard_map/ppermute | solution.py:441
  764.4 8.4 collective-permute-done.77
  794.9 5.9 collective-permute-done.82
  803.0 6.7 collective-permute-done.83
  829.9 5.5 copy.140
  835.4 70.4 %reduce-scatter.8.cloned.1.call-done = bf16[512,3072]{0,1:T(8,128)(2,1)} async-done(((bf16[2048,3072]{0,1:T(8,128)(2,1)}), bf16[512,3072]{0,1:T(8,128)(2,1)}) %reduce-scatter.8.cloned.1.call-update) | async-done | bytes 3145744 | tf_op jit(solution)/shard_map/reduce_scatter | solution.py:540
  (830 shorter events, 349.6 us)
Async XLA Ops:
  7.2 74.6 %all-gather.6.cloned.1.call-start = ((), (), s32[]{:S(2)}) async-start(), calls=%async_computation.3 | async-start | bytes 3932160 | tf_op jit(solution)/shard_map/all_gather | solution.py:536
  13.1 160.2 %all-gather.8.cloned.1.call-start = ((), (), s32[]{:S(2)}) async-start(), calls=%async_computation.4 | async-start | bytes 2949120 | tf_op jit(solution)/shard_map/all_gather | solution.py:843
  14.0 225.8 %all-gather.10.cloned.1.call-start = ((), (), s32[]{:S(2)}) async-start(), calls=%async_computation.5 | async-start | bytes 15728640 | tf_op jit(solution)/shard_map/all_gather | solution.py:536
  25.8 14.9 %collective-permute-start.34 = (bf16[256,3072]{0,1:T(8,128)(2,1)}, bf16[256,3072]{0,1:T(8,128)(2,1)}, u32[]{:S(2)}, u32[]{:S(2)}) collective-permute-start(bf16[256,3072]{0,1:T(8,128)(2,1)} %pad_maximum_fusion.9), channel_id=1, source_target_pairs={{0,1},{1,0},{2,3},{3,2},{4,5},{5,4},{6,7},{7,6},{8,9},{9,8},{10,11... | collective-permute-start | bytes 4718600 | tf_op jit(solution)/shard_map/ppermute | solution.py:445
  34.9 42.6 %collective-permute-start.5 = (bf16[128,2176]{1,0:T(8,128)(2,1)}, bf16[128,2176]{1,0:T(8,128)(2,1)}, u32[]{:S(2)}, u32[]{:S(2)}) collective-permute-start(bf16[128,2176]{1,0:T(8,128)(2,1)} %fusion.134), channel_id=1, source_target_pairs={{0,1},{1,0},{2,3},{3,2},{4,5},{5,4},{6,7},{7,6},{8,9},{9,8},{10,11... | collective-permute-start | bytes 1671176 | tf_op jit(solution)/shard_map/ppermute | solution.py:445
  35.0 18.3 %collective-permute-start.1 = (bf16[128,2176]{1,0:T(8,128)(2,1)}, bf16[128,2176]{1,0:T(8,128)(2,1)}, u32[]{:S(2)}, u32[]{:S(2)}) collective-permute-start(bf16[128,2176]{1,0:T(8,128)(2,1)} %fusion.134), channel_id=1, source_target_pairs={{0,24},{8,0},{16,8},{24,16},{1,25},{9,1},{17,9},{25,17},{2,26},{10... | collective-permute-start | bytes 1671176 | tf_op jit(solution)/shard_map/ppermute | solution.py:441
  40.0 26.2 %collective-permute-start = (bf16[128,2176]{1,0:T(8,128)(2,1)}, bf16[128,2176]{1,0:T(8,128)(2,1)}, u32[]{:S(2)}, u32[]{:S(2)}) collective-permute-start(bf16[128,2176]{1,0:T(8,128)(2,1)} %fusion.134), channel_id=1, source_target_pairs={{0,8},{8,16},{16,24},{24,0},{1,9},{9,17},{17,25},{25,1},{2,10},{10... | collective-permute-start | bytes 1671176 | tf_op jit(solution)/shard_map/ppermute | solution.py:441
  44.8 551.9 %reduce-scatter.4.cloned.1.call-start = ((), (), s32[]{:S(2)}) async-start(), calls=%async_computation.6 | async-start | bytes 3932160 | tf_op jit(solution)/shard_map/reduce_scatter | solution.py:540
  54.3 17.8 %collective-permute-start.3 = (bf16[64,2176]{1,0:T(8,128)(2,1)S(1)}, bf16[64,2176]{1,0:T(8,128)(2,1)S(1)}, u32[]{:S(2)}, u32[]{:S(2)}) collective-permute-start(bf16[64,2176]{1,0:T(8,128)(2,1)S(1)} %slice.913), channel_id=1, source_target_pairs={{0,24},{8,0},{16,8},{24,16},{1,25},{9,1},{17,9},{25,17},{2,26},{10... | collective-permute-start | bytes 835592 | tf_op jit(solution)/shard_map/ppermute | solution.py:441
  94.1 16.0 %collective-permute-start.10 = (bf16[1024,256]{1,0:T(8,128)(2,1)S(1)}, bf16[1024,256]{1,0:T(8,128)(2,1)S(1)}, u32[]{:S(2)}, u32[]{:S(2)}) collective-permute-start(bf16[1024,256]{1,0:T(8,128)(2,1)S(1)} %get-tuple-element.291.refs_0_), channel_id=1, source_target_pairs={{0,4},{1,5},{2,6},{3,7},{4,0},{5,1},{6,2},{7,3},{8,12},{9,13},{10,... | collective-permute-start | bytes 1572872 | tf_op jit(solution)/shard_map/ppermute | solution.py:445
  95.7 18.8 %collective-permute-start.9 = (bf16[1024,256]{1,0:T(8,128)(2,1)S(1)}, bf16[1024,256]{1,0:T(8,128)(2,1)S(1)}, u32[]{:S(2)}, u32[]{:S(2)}) collective-permute-start(bf16[1024,256]{1,0:T(8,128)(2,1)S(1)} %get-tuple-element.291.refs_0_), channel_id=1, source_target_pairs={{0,2},{1,3},{2,0},{3,1},{4,6},{5,7},{6,4},{7,5},{8,10},{9,11},{10,... | collective-permute-start | bytes 1572872 | tf_op jit(solution)/shard_map/ppermute | solution.py:445
  114.6 22.5 %collective-permute-start.13 = (bf16[1024,256]{1,0:T(8,128)(2,1)S(1)}, bf16[1024,256]{1,0:T(8,128)(2,1)S(1)}, u32[]{:S(2)}, u32[]{:S(2)}) collective-permute-start(bf16[1024,256]{1,0:T(8,128)(2,1)S(1)} %get-tuple-element.291.refs_0_), channel_id=1, source_target_pairs={{0,1},{1,0},{2,3},{3,2},{4,5},{5,4},{6,7},{7,6},{8,9},{9,8},{10,11... | collective-permute-start | bytes 1572872 | tf_op jit(solution)/shard_map/ppermute | solution.py:445
  114.7 23.2 %collective-permute-start.15 = (bf16[1024,256]{1,0:T(8,128)(2,1)S(1)}, bf16[1024,256]{1,0:T(8,128)(2,1)}, u32[]{:S(2)}, u32[]{:S(2)}) collective-permute-start(bf16[1024,256]{1,0:T(8,128)(2,1)S(1)} %collective-permute-done.10.refs_2_), channel_id=1, source_target_pairs={{0,1},{1,0},{2,3},{3,2},{4,5},{5,4},{6,7},{7,6},{8,9},{9,8},{10,11... | collective-permute-start | bytes 1572872 | tf_op jit(solution)/shard_map/ppermute | solution.py:445
  115.2 22.7 %collective-permute-start.14 = (bf16[1024,256]{1,0:T(8,128)(2,1)S(1)}, bf16[1024,256]{1,0:T(8,128)(2,1)}, u32[]{:S(2)}, u32[]{:S(2)}) collective-permute-start(bf16[1024,256]{1,0:T(8,128)(2,1)S(1)} %collective-permute-done.9.refs_1_), channel_id=1, source_target_pairs={{0,1},{1,0},{2,3},{3,2},{4,5},{5,4},{6,7},{7,6},{8,9},{9,8},{10,11... | collective-permute-start | bytes 1572872 | tf_op jit(solution)/shard_map/ppermute | solution.py:445
  157.7 18.7 %collective-permute-start.18 = (bf16[128,2048]{1,0:T(8,128)(2,1)}, bf16[128,2048]{1,0:T(8,128)(2,1)}, u32[]{:S(2)}, u32[]{:S(2)}) collective-permute-start(bf16[128,2048]{1,0:T(8,128)(2,1)} %get-tuple-element.217), channel_id=1, source_target_pairs={{0,1},{1,0},{2,3},{3,2},{4,5},{5,4},{6,7},{7,6},{8,9},{9,8},{10,11... | collective-permute-start | bytes 1572872 | tf_op jit(solution)/shard_map/ppermute | solution.py:445
  165.3 17.4 %collective-permute-start.25 = (bf16[128,2048]{1,0:T(8,128)(2,1)}, bf16[128,2048]{1,0:T(8,128)(2,1)}, u32[]{:S(2)}, u32[]{:S(2)}) collective-permute-start(bf16[128,2048]{1,0:T(8,128)(2,1)} %pad_maximum_fusion.19), channel_id=1, source_target_pairs={{0,24},{8,0},{16,8},{24,16},{1,25},{9,1},{17,9},{25,17},{2,26},{10... | collective-permute-start | bytes 1572872 | tf_op jit(solution)/shard_map/ppermute | solution.py:441
  171.9 21.1 %collective-permute-start.22 = (bf16[128,2048]{1,0:T(8,128)(2,1)}, bf16[128,2048]{1,0:T(8,128)(2,1)}, u32[]{:S(2)}, u32[]{:S(2)}) collective-permute-start(bf16[128,2048]{1,0:T(8,128)(2,1)} %pad_maximum_fusion.18), channel_id=1, source_target_pairs={{0,8},{8,16},{16,24},{24,0},{1,9},{9,17},{17,25},{25,1},{2,10},{10... | collective-permute-start | bytes 1572872 | tf_op jit(solution)/shard_map/ppermute | solution.py:441
  196.5 15.7 %collective-permute-start.27 = (bf16[128,2048]{1,0:T(8,128)(2,1)S(1)}, bf16[128,2048]{1,0:T(8,128)(2,1)S(1)}, u32[]{:S(2)}, u32[]{:S(2)}) collective-permute-start(bf16[128,2048]{1,0:T(8,128)(2,1)S(1)} %multiply_convert_fusion.3), channel_id=1, source_target_pairs={{0,24},{8,0},{16,8},{24,16},{1,25},{9,1},{17,9},{25,17},{2,26},{10... | collective-permute-start | bytes 1572872 | tf_op jit(solution)/shard_map/ppermute | solution.py:441
  199.9 24.6 %collective-permute-start.26 = (bf16[128,2048]{1,0:T(8,128)(2,1)S(1)}, bf16[128,2048]{1,0:T(8,128)(2,1)S(1)}, u32[]{:S(2)}, u32[]{:S(2)}) collective-permute-start(bf16[128,2048]{1,0:T(8,128)(2,1)S(1)} %multiply_convert_fusion.3), channel_id=1, source_target_pairs={{0,8},{8,16},{16,24},{24,0},{1,9},{9,17},{17,25},{25,1},{2,10},{10... | collective-permute-start | bytes 1572872 | tf_op jit(solution)/shard_map/ppermute | solution.py:441
  199.9 37.4 %collective-permute-start.31 = (bf16[128,2048]{1,0:T(8,128)(2,1)S(1)}, bf16[128,2048]{1,0:T(8,128)(2,1)S(1)}, u32[]{:S(2)}, u32[]{:S(2)}) collective-permute-start(bf16[128,2048]{1,0:T(8,128)(2,1)S(1)} %multiply_convert_fusion.3), channel_id=1, source_target_pairs={{0,1},{1,0},{2,3},{3,2},{4,5},{5,4},{6,7},{7,6},{8,9},{9,8},{10,11... | collective-permute-start | bytes 1572872 | tf_op jit(solution)/shard_map/ppermute | solution.py:445
  212.2 17.7 %collective-permute-start.29 = (bf16[64,2048]{1,0:T(8,128)(2,1)S(1)}, bf16[64,2048]{1,0:T(8,128)(2,1)S(1)}, u32[]{:S(2)}, u32[]{:S(2)}) collective-permute-start(bf16[64,2048]{1,0:T(8,128)(2,1)S(1)} %slice.956), channel_id=1, source_target_pairs={{0,24},{8,0},{16,8},{24,16},{1,25},{9,1},{17,9},{25,17},{2,26},{10... | collective-permute-start | bytes 786440 | tf_op jit(solution)/shard_map/ppermute | solution.py:441
  270.4 15.2 %collective-permute-start.35 = (bf16[128,2048]{1,0:T(8,128)(2,1)S(1)}, bf16[128,2048]{1,0:T(8,128)(2,1)S(1)}, u32[]{:S(2)}, u32[]{:S(2)}) collective-permute-start(bf16[128,2048]{1,0:T(8,128)(2,1)S(1)} %get-tuple-element.210), channel_id=1, source_target_pairs={{0,1},{1,0},{2,3},{3,2},{4,5},{5,4},{6,7},{7,6},{8,9},{9,8},{10,11... | collective-permute-start | bytes 1572872 | tf_op jit(solution)/shard_map/ppermute | solution.py:445
  277.2 18.0 %collective-permute-start.42 = (bf16[128,2048]{1,0:T(8,128)(2,1)S(1)}, bf16[128,2048]{1,0:T(8,128)(2,1)S(1)}, u32[]{:S(2)}, u32[]{:S(2)}) collective-permute-start(bf16[128,2048]{1,0:T(8,128)(2,1)S(1)} %pad_maximum_fusion.22), channel_id=1, source_target_pairs={{0,24},{8,0},{16,8},{24,16},{1,25},{9,1},{17,9},{25,17},{2,26},{10... | collective-permute-start | bytes 1572872 | tf_op jit(solution)/shard_map/ppermute | solution.py:441
  284.2 21.8 %collective-permute-start.39 = (bf16[128,2048]{1,0:T(8,128)(2,1)S(1)}, bf16[128,2048]{1,0:T(8,128)(2,1)S(1)}, u32[]{:S(2)}, u32[]{:S(2)}) collective-permute-start(bf16[128,2048]{1,0:T(8,128)(2,1)S(1)} %pad_maximum_fusion.21), channel_id=1, source_target_pairs={{0,8},{8,16},{16,24},{24,0},{1,9},{9,17},{17,25},{25,1},{2,10},{10... | collective-permute-start | bytes 1572872 | tf_op jit(solution)/shard_map/ppermute | solution.py:441
  322.7 15.3 %collective-permute-start.44 = (bf16[128,2048]{1,0:T(8,128)(2,1)S(1)}, bf16[128,2048]{1,0:T(8,128)(2,1)S(1)}, u32[]{:S(2)}, u32[]{:S(2)}) collective-permute-start(bf16[128,2048]{1,0:T(8,128)(2,1)S(1)} %fusion.39), channel_id=1, source_target_pairs={{0,24},{8,0},{16,8},{24,16},{1,25},{9,1},{17,9},{25,17},{2,26},{10... | collective-permute-start | bytes 1572872 | tf_op jit(solution)/shard_map/ppermute | solution.py:441
  325.6 24.6 %collective-permute-start.43 = (bf16[128,2048]{1,0:T(8,128)(2,1)S(1)}, bf16[128,2048]{1,0:T(8,128)(2,1)S(1)}, u32[]{:S(2)}, u32[]{:S(2)}) collective-permute-start(bf16[128,2048]{1,0:T(8,128)(2,1)S(1)} %fusion.39), channel_id=1, source_target_pairs={{0,8},{8,16},{16,24},{24,0},{1,9},{9,17},{17,25},{25,1},{2,10},{10... | collective-permute-start | bytes 1572872 | tf_op jit(solution)/shard_map/ppermute | solution.py:441
  325.7 35.1 %collective-permute-start.48 = (bf16[128,2048]{1,0:T(8,128)(2,1)S(1)}, bf16[128,2048]{1,0:T(8,128)(2,1)S(1)}, u32[]{:S(2)}, u32[]{:S(2)}) collective-permute-start(bf16[128,2048]{1,0:T(8,128)(2,1)S(1)} %fusion.39), channel_id=1, source_target_pairs={{0,1},{1,0},{2,3},{3,2},{4,5},{5,4},{6,7},{7,6},{8,9},{9,8},{10,11... | collective-permute-start | bytes 1572872 | tf_op jit(solution)/shard_map/ppermute | solution.py:445
  338.0 17.7 %collective-permute-start.46 = (bf16[64,2048]{1,0:T(8,128)(2,1)S(1)}, bf16[64,2048]{1,0:T(8,128)(2,1)S(1)}, u32[]{:S(2)}, u32[]{:S(2)}) collective-permute-start(bf16[64,2048]{1,0:T(8,128)(2,1)S(1)} %slice.992), channel_id=1, source_target_pairs={{0,24},{8,0},{16,8},{24,16},{1,25},{9,1},{17,9},{25,17},{2,26},{10... | collective-permute-start | bytes 786440 | tf_op jit(solution)/shard_map/ppermute | solution.py:441
  396.4 15.0 %collective-permute-start.51 = (bf16[128,2048]{1,0:T(8,128)(2,1)S(1)}, bf16[128,2048]{1,0:T(8,128)(2,1)S(1)}, u32[]{:S(2)}, u32[]{:S(2)}) collective-permute-start(bf16[128,2048]{1,0:T(8,128)(2,1)S(1)} %get-tuple-element.203), channel_id=1, source_target_pairs={{0,1},{1,0},{2,3},{3,2},{4,5},{5,4},{6,7},{7,6},{8,9},{9,8},{10,11... | collective-permute-start | bytes 1572872 | tf_op jit(solution)/shard_map/ppermute | solution.py:445
  403.3 17.9 %collective-permute-start.58 = (bf16[128,2048]{1,0:T(8,128)(2,1)S(1)}, bf16[128,2048]{1,0:T(8,128)(2,1)S(1)}, u32[]{:S(2)}, u32[]{:S(2)}) collective-permute-start(bf16[128,2048]{1,0:T(8,128)(2,1)S(1)} %pad_maximum_fusion.25), channel_id=1, source_target_pairs={{0,24},{8,0},{16,8},{24,16},{1,25},{9,1},{17,9},{25,17},{2,26},{10... | collective-permute-start | bytes 1572872 | tf_op jit(solution)/shard_map/ppermute | solution.py:441
  410.2 21.6 %collective-permute-start.55 = (bf16[128,2048]{1,0:T(8,128)(2,1)S(1)}, bf16[128,2048]{1,0:T(8,128)(2,1)S(1)}, u32[]{:S(2)}, u32[]{:S(2)}) collective-permute-start(bf16[128,2048]{1,0:T(8,128)(2,1)S(1)} %pad_maximum_fusion.24), channel_id=1, source_target_pairs={{0,8},{8,16},{16,24},{24,0},{1,9},{9,17},{17,25},{25,1},{2,10},{10... | collective-permute-start | bytes 1572872 | tf_op jit(solution)/shard_map/ppermute | solution.py:441
  435.8 15.7 %collective-permute-start.60 = (bf16[128,2048]{1,0:T(8,128)(2,1)}, bf16[128,2048]{1,0:T(8,128)(2,1)}, u32[]{:S(2)}, u32[]{:S(2)}) collective-permute-start(bf16[128,2048]{1,0:T(8,128)(2,1)} %get-tuple-element.249), channel_id=1, source_target_pairs={{0,24},{8,0},{16,8},{24,16},{1,25},{9,1},{17,9},{25,17},{2,26},{10... | collective-permute-start | bytes 1572872 | tf_op jit(solution)/shard_map/ppermute | solution.py:441
  438.9 24.9 %collective-permute-start.59 = (bf16[128,2048]{1,0:T(8,128)(2,1)}, bf16[128,2048]{1,0:T(8,128)(2,1)}, u32[]{:S(2)}, u32[]{:S(2)}) collective-permute-start(bf16[128,2048]{1,0:T(8,128)(2,1)} %get-tuple-element.249), channel_id=1, source_target_pairs={{0,8},{8,16},{16,24},{24,0},{1,9},{9,17},{17,25},{25,1},{2,10},{10... | collective-permute-start | bytes 1572872 | tf_op jit(solution)/shard_map/ppermute | solution.py:441
  439.2 35.0 %collective-permute-start.64 = (bf16[128,2048]{1,0:T(8,128)(2,1)}, bf16[128,2048]{1,0:T(8,128)(2,1)S(1)}, u32[]{:S(2)}, u32[]{:S(2)}) collective-permute-start(bf16[128,2048]{1,0:T(8,128)(2,1)} %get-tuple-element.249), channel_id=1, source_target_pairs={{0,1},{1,0},{2,3},{3,2},{4,5},{5,4},{6,7},{7,6},{8,9},{9,8},{10,11... | collective-permute-start | bytes 1572872 | tf_op jit(solution)/shard_map/ppermute | solution.py:445
  452.5 17.6 %collective-permute-start.62 = (bf16[64,2048]{1,0:T(8,128)(2,1)S(1)}, bf16[64,2048]{1,0:T(8,128)(2,1)S(1)}, u32[]{:S(2)}, u32[]{:S(2)}) collective-permute-start(bf16[64,2048]{1,0:T(8,128)(2,1)S(1)} %slice.1008), channel_id=1, source_target_pairs={{0,24},{8,0},{16,8},{24,16},{1,25},{9,1},{17,9},{25,17},{2,26},{10... | collective-permute-start | bytes 786440 | tf_op jit(solution)/shard_map/ppermute | solution.py:441
  495.7 25.3 %collective-permute-start.68 = (bf16[1024,256]{1,0:T(8,128)(2,1)S(1)}, bf16[1024,256]{1,0:T(8,128)(2,1)S(1)}, u32[]{:S(2)}, u32[]{:S(2)}) collective-permute-start(bf16[1024,256]{1,0:T(8,128)(2,1)S(1)} %pad_maximum_fusion.28), channel_id=1, source_target_pairs={{0,2},{1,3},{2,0},{3,1},{4,6},{5,7},{6,4},{7,5},{8,10},{9,11},{10,... | collective-permute-start | bytes 1572872 | tf_op jit(solution)/shard_map/ppermute | solution.py:445
  504.5 25.4 %collective-permute-start.70 = (bf16[1024,256]{1,0:T(8,128)(2,1)S(1)}, bf16[1024,256]{1,0:T(8,128)(2,1)S(1)}, u32[]{:S(2)}, u32[]{:S(2)}) collective-permute-start(bf16[1024,256]{1,0:T(8,128)(2,1)S(1)} %pad_maximum_fusion.29), channel_id=1, source_target_pairs={{0,4},{1,5},{2,6},{3,7},{4,0},{5,1},{6,2},{7,3},{8,12},{9,13},{10,... | collective-permute-start | bytes 1572872 | tf_op jit(solution)/shard_map/ppermute | solution.py:445
  521.0 15.1 %collective-permute-start.69 = (bf16[512,256]{1,0:T(8,128)(2,1)S(1)}, bf16[512,256]{1,0:T(8,128)(2,1)S(1)}, u32[]{:S(2)}, u32[]{:S(2)}) collective-permute-start(bf16[512,256]{1,0:T(8,128)(2,1)S(1)} %fusion.157), channel_id=1, source_target_pairs={{0,4},{1,5},{2,6},{3,7},{4,0},{5,1},{6,2},{7,3},{8,12},{9,13},{10,... | collective-permute-start | bytes 786440 | tf_op jit(solution)/shard_map/ppermute | solution.py:445
  552.9 90.6 %reduce-scatter.6.cloned.1.call-start = ((), (), s32[]{:S(2)}) async-start(), calls=%async_computation.7 | async-start | bytes 2949120 | tf_op jit(solution)/shard_map/reduce_scatter | solution.py:1045
  558.9 146.7 %all-reduce.38.cloned.1.call-start = ((), (), s32[]{:S(2)}) async-start(), calls=%async_computation.8 | async-start | bytes 655360 | tf_op jit(solution)/shard_map/psum | solution.py:1044
  597.9 45.8 %collective-permute-start.86 = (bf16[256,768]{0,1:T(8,128)(2,1)S(1)}, bf16[256,768]{0,1:T(8,128)(2,1)S(1)}, u32[]{:S(2)}, u32[]{:S(2)}) collective-permute-start(bf16[256,768]{0,1:T(8,128)(2,1)S(1)} %broadcast_select_fusion.12), channel_id=1, source_target_pairs={{0,1},{1,0},{2,3},{3,2},{4,5},{5,4},{6,7},{7,6},{8,9},{9,8},{10,11... | collective-permute-start | bytes 1179656 | tf_op jit(solution)/shard_map/ppermute | solution.py:445
  643.6 186.3 %all-gather.12.cloned.1.call-start = ((), (), s32[]{:S(2)}) async-start(), calls=%async_computation.10 | async-start | bytes 3932160 | tf_op jit(solution)/shard_map/all_gather | solution.py:1084
  645.9 260.0 %reduce-scatter.8.cloned.1.call-start = ((), (), s32[]{:S(2)}) async-start(), calls=%async_computation.9 | async-start | bytes 15728640 | tf_op jit(solution)/shard_map/reduce_scatter | solution.py:540
  700.0 25.1 %collective-permute-start.79 = (bf16[64,2048]{1,0:T(8,128)(2,1)}, bf16[64,2048]{1,0:T(8,128)(2,1)}, u32[]{:S(2)}, u32[]{:S(2)}) collective-permute-start(bf16[64,2048]{1,0:T(8,128)(2,1)} %get-tuple-element.272), channel_id=1, source_target_pairs={{0,24},{8,0},{16,8},{24,16},{1,25},{9,1},{17,9},{25,17},{2,26},{10... | collective-permute-start | bytes 786440 | tf_op jit(solution)/shard_map/ppermute | solution.py:441
  709.0 33.8 %collective-permute-start.73 = (bf16[128,2048]{1,0:T(8,128)(2,1)}, bf16[128,2048]{1,0:T(8,128)(2,1)}, u32[]{:S(2)}, u32[]{:S(2)}) collective-permute-start(bf16[128,2048]{1,0:T(8,128)(2,1)} %get-tuple-element.192), channel_id=1, source_target_pairs={{0,1},{1,0},{2,3},{3,2},{4,5},{5,4},{6,7},{7,6},{8,9},{9,8},{10,11... | collective-permute-start | bytes 1572872 | tf_op jit(solution)/shard_map/ppermute | solution.py:445
  709.0 19.0 %collective-permute-start.76 = (bf16[64,2048]{1,0:T(8,128)(2,1)}, bf16[64,2048]{1,0:T(8,128)(2,1)S(1)}, u32[]{:S(2)}, u32[]{:S(2)}) collective-permute-start(bf16[64,2048]{1,0:T(8,128)(2,1)} %get-tuple-element.271), channel_id=1, source_target_pairs={{0,8},{8,16},{16,24},{24,0},{1,9},{9,17},{17,25},{25,1},{2,10},{10... | collective-permute-start | bytes 786440 | tf_op jit(solution)/shard_map/ppermute | solution.py:441
  726.9 37.5 %collective-permute-start.80 = (bf16[128,2048]{1,0:T(8,128)(2,1)}, bf16[128,2048]{1,0:T(8,128)(2,1)}, u32[]{:S(2)}, u32[]{:S(2)}) collective-permute-start(bf16[128,2048]{1,0:T(8,128)(2,1)} %pad_maximum_fusion.31), channel_id=1, source_target_pairs={{0,24},{8,0},{16,8},{24,16},{1,25},{9,1},{17,9},{25,17},{2,26},{10... | collective-permute-start | bytes 1572872 | tf_op jit(solution)/shard_map/ppermute | solution.py:441
  728.9 43.9 %collective-permute-start.77 = (bf16[128,2048]{1,0:T(8,128)(2,1)}, bf16[128,2048]{1,0:T(8,128)(2,1)}, u32[]{:S(2)}, u32[]{:S(2)}) collective-permute-start(bf16[128,2048]{1,0:T(8,128)(2,1)} %pad_maximum_fusion.30), channel_id=1, source_target_pairs={{0,8},{8,16},{16,24},{24,0},{1,9},{9,17},{17,25},{25,1},{2,10},{10... | collective-permute-start | bytes 1572872 | tf_op jit(solution)/shard_map/ppermute | solution.py:441
  (229 other events, 3396.3 us)
Sparse Core Ops, SparseCore 0:
  13.2 46.4 all-gather.5
  61.6 30.1 all-gather.7
  93.6 130.3 all-gather.9
  553.1 43.6 reduce-scatter.3
  599.9 43.6 reduce-scatter.5
  645.8 36.2 all-reduce.37
  684.2 96.8 all-gather.11
  784.1 121.6 reduce-scatter.7

commit v2 on v1

--- a/solution.py
+++ b/solution.py
@@ -474,6 +474,31 @@
     return own + along_heads(after, 1).astype(wide) + along_heads(before, -1).astype(wide)
 
 
+def in_line(parts):
+    line = lax.axis_index("heads")
+    rows = parts[0].shape[0]
+    turned = turn(jnp.concatenate(parts, axis=0), (1 - line) % LINE)
+    return [turned[k * rows : (k + 1) * rows] for k in range(LINE)]
+
+
+def gather_line(x):
+    half = x.shape[0] // 2
+    before = along_heads(x, 1)
+    after_ = along_heads(x, -1)
+    far = jnp.concatenate([along_heads(before[:half], 1), along_heads(after_[half:], -1)], axis=0)
+    return in_line([before, x, after_, far])
+
+
+def share_line(x):
+    line = lax.axis_index("heads")
+    rows = x.shape[0] // LINE
+    total = lax.dynamic_slice_in_dim(x, line * rows, rows).astype(jnp.float32)
+    for step in range(1, LINE):
+        piece = lax.dynamic_slice_in_dim(x, ((line + step) % LINE) * rows, rows)
+        total = total + along_heads(piece, step).astype(jnp.float32)
+    return total
+
+
 def turn(x, blocks):
     rows = x.shape[0] // LINE
     twice = jnp.concatenate([x, x], axis=0)
@@ -501,7 +526,7 @@
     return side, front, across_blk(side[:half], 4), across_blk(front[half:], 2)
 
 
-def scatter_chips(parts):
+def scatter_chips(parts, *others):
     wide = jnp.float32
     half = parts[0].shape[0] // 2
     own, side, front, far = parts
@@ -509,9 +534,10 @@
     high = across_blk(jnp.concatenate([front[half:], far[half:]], axis=0), 4)
     front_sum = (front[:half].astype(wide) + low[half:].astype(wide)).astype(jnp.bfloat16)
     side_sum = (side[half:].astype(wide) + high[half:].astype(wide)).astype(jnp.bfloat16)
+    front_sum, side_sum, *others = together(front_sum, side_sum, *others)
     upper = own[:half].astype(wide) + low[:half].astype(wide) + across_blk(front_sum, 4).astype(wide)
     lower = own[half:].astype(wide) + high[:half].astype(wide) + across_blk(side_sum, 2).astype(wide)
-    return jnp.concatenate([upper, lower], axis=0)
+    return jnp.concatenate([upper, lower], axis=0), *others
 
 
 def butterfly(x):
@@ -540,6 +566,10 @@
     return lax.psum_scatter(
         x, "blk", scatter_dimension=0, tiled=True, axis_index_groups=chip_groups()
     )
+
+
+def together(*values):
+    return lax.optimization_barrier(values)
 
 
 def pick(x, start, size):
@@ -847,21 +877,11 @@
         tiled=True,
     )
 
-    def hidden_columns(index):
-        return jnp.concatenate(
-            [pick(w, index * hidden, hidden) for w in (gate_weight, up_weight, down_weight)], axis=1
-        )
-
-    unit_full = all_rows(weight_rows(hidden_columns(core), hidden_columns(1 - core), core))
     query_kv_full = head_full[:, : 2 * HEAD_WIDTH]
     out_full = head_full[:, 2 * HEAD_WIDTH :]
     laurel_full = small_full[:, : 2 * LAUREL_RANK]
     gate_full = small_full[:, 2 * LAUREL_RANK : 2 * LAUREL_RANK + LAYER_INPUT_SIZE]
     projection_full = small_full[:, 2 * LAUREL_RANK + LAYER_INPUT_SIZE :]
-    unit_gate = unit_full[:, :hidden]
-    unit_up = unit_full[:, hidden : 2 * hidden]
-    unit_down = unit_full[:, 2 * hidden :]
-
     gain_rows = norm_gains.astype(wide)
     router_wide = router_weight.astype(wide)
     coef_wide = coefficients.astype(wide)
@@ -874,6 +894,16 @@
         coef_wide,
     )
     normed_low = normed.astype(narrow)
+    *unit_weights, normed_low = together(gate_weight, up_weight, down_weight, normed_low)
+
+    def hidden_columns(index):
+        return jnp.concatenate([pick(w, index * hidden, hidden) for w in unit_weights], axis=1)
+
+    unit_full = all_rows(weight_rows(hidden_columns(core), hidden_columns(1 - core), core))
+    unit_two = unit_full[:, : 2 * hidden]
+    unit_gate = unit_full[:, :hidden]
+    unit_up = unit_full[:, hidden : 2 * hidden]
+    unit_down = unit_full[:, 2 * hidden :]
 
     digits = jnp.stack([positions // 128, positions % 128], axis=1).astype(narrow)
     sent = jnp.concatenate([normed_low, jnp.pad(digits, ((0, 0), (0, 126)))], axis=1)
@@ -938,6 +968,20 @@
         [corrected[0].astype(narrow)] + [(corrected[i] + extra).astype(narrow) for i in (1, 2, 3)]
     )
 
+    def core_columns(x):
+        top, bottom = x[:rows_here], x[rows_here:]
+        keep = jnp.where(first_core, top, bottom)
+        got = other_core(jnp.where(first_core, bottom, top))
+        return jnp.where(first_core, keep, got), jnp.where(first_core, got, keep)
+
+    def pairs(x, count):
+        first, second = core_columns(x)
+        parts = []
+        for index in range(count):
+            columns = slice(index * HEAD_WIDTH, (index + 1) * HEAD_WIDTH)
+            parts += [first[:, columns], second[:, columns]]
+        return jnp.concatenate(parts, axis=1)
+
     corrected_grad = tuple(cotangent[i].astype(wide) for i in range(4))
     projected_grad, gain_seven = pull_extra(
         corrected_grad[1] + corrected_grad[2] + corrected_grad[3]
@@ -948,69 +992,77 @@
     merged_grad, fed_grad, predicted_grad, gains_correct, router_correct, coef_correct = (
         pull_correct((corrected_grad, transposed_product(gate_pre_low, gate_full)))
     )
+    io_sum = lax.psum_scatter(
+        jnp.concatenate(
+            [weight_product(first_low, gate_pre_low), weight_product(projected_low, gated_low)],
+            axis=1,
+        ).astype(narrow),
+        "blk",
+        scatter_dimension=0,
+        tiled=True,
+    )
     fed_rows = gather_chip(fed_grad.astype(narrow))
+    fed_rows, io_sum = together(fed_rows, io_sum)
+    io_share = share_line(io_sum).astype(narrow)
     gate_grad, up_grad = pull_activate(forward_product(fed_rows, unit_down))
-    gate_low = gate_grad.astype(narrow)
-    up_low = up_grad.astype(narrow)
-    feed_grad = scatter_chip(
-        (transposed_product(gate_low, unit_gate) + transposed_product(up_low, unit_up)).astype(narrow)
-    )
-    unit_sum = own_rows(
-        jnp.concatenate(
-            [
-                weight_product(unit_rows, gate_low).astype(narrow),
-                weight_product(unit_rows, up_low).astype(narrow),
-                weight_product(fed_rows, hidden_low).astype(narrow),
-            ],
-            axis=1,
-        )
-    )
+    two_low = jnp.concatenate([gate_grad.astype(narrow), up_grad.astype(narrow)], axis=1)
+    feed_grad = scatter_chip(transposed_product(two_low, unit_two).astype(narrow))
+    down_part = weight_product(fed_rows, hidden_low).astype(narrow)
+    two_part = weight_product(unit_rows, two_low).astype(narrow)
+    down_sum = own_rows(down_part)
+    two_sum = own_rows(two_part)
     active_grad, attention_grad, normed_combine, lifted_grad, gains_combine = pull_combine(
         (merged_grad, feed_grad)
     )
+    attention_low = attention_grad.astype(narrow)
     lifted_low = lifted_grad.astype(narrow)
     down_grad_low = forward_product(lifted_low, laurel_full[:, LAUREL_RANK:]).astype(narrow)
-    attention_rows = gather_chip(attention_grad.astype(narrow))
+    laurel_part = jnp.concatenate(
+        [weight_product(normed_low, down_grad_low), weight_product(lifted_low, down_low)], axis=1
+    ).astype(narrow)
+    laurel_part = laurel_part + other_core(laurel_part)
+    attention_rows = gather_chip(attention_low)
+    out_part = jnp.concatenate(
+        [weight_product(attention_rows, mixed_rows).astype(narrow), laurel_part], axis=1
+    )
     mixed_grad_rows = forward_product(attention_rows, out_full).astype(narrow)
+    mixed_grad_rows, down_sum, two_sum, io_share, out_part = together(
+        mixed_grad_rows, down_sum, two_sum, io_share, out_part
+    )
+    out_sum = own_rows(out_part)
     mixed_grad = natural(mixed_grad_rows, core, line)
     delta = jnp.sum(mixed_grad.astype(wide) * attended, axis=-1)
     query_grad, kv_keep, kv_send = attend_back_here(
         meta, rotated, mixed_grad, lse, delta, lo, mine, theirs
     )
-    kv_got = other_core(kv_send)
-    kv_sum = scatter_chips(
-        [(kv_keep[m].astype(wide) + kv_got[m].astype(wide)).astype(narrow) for m in range(CHIPS)]
-    )
-    half = own // 2
-    mine_first = line % 2 == 0
-    kv_sum_low = kv_sum.astype(narrow)
-    kv_away = jnp.where(mine_first, kv_sum_low[half:], kv_sum_low[:half])
-    kv_back = jnp.where(mine_first, kv_sum[:half], kv_sum[half:]) + lax.ppermute(
-        kv_away, "heads", [(i, i ^ 1) for i in range(LINE)]
-    ).astype(wide)
-
-    def own_half(x):
-        return jnp.where(mine_first, x[:half], x[half:])
-
     _, pull_query = jax.vjp(
         lambda x, g: head_apply(x, g, cosine, sine), query_pre, head_wide[0]
     )
     query_pre_grad, query_gain_grad = pull_query(query_grad.astype(narrow).astype(wide))
+    query_rows_grad = arrival(query_pre_grad.astype(narrow), core, line)
+    query_part = weight_product(normed_rows, query_rows_grad).astype(narrow)
+    kv_got = other_core(kv_send)
+    *kv_parts, out_sum = together(
+        *[(kv_keep[m].astype(wide) + kv_got[m].astype(wide)).astype(narrow) for m in range(CHIPS)],
+        out_sum,
+    )
+    kv_grad, query_part = scatter_chips(kv_parts, query_part)
+    query_sum = own_rows(query_part)
+
     _, pull_kv = jax.vjp(
-        lambda x, g: head_apply(x, kv_gain(g), own_half(cosine_kv), own_half(sine_kv)),
-        own_half(kv_pre),
-        head_wide,
-    )
-    kv_pre_grad, kv_gain_grad = pull_kv(kv_back)
-    kv_low = kv_pre_grad.astype(narrow)
-    nothing = jnp.zeros_like(kv_low)
-    kv_both = jnp.concatenate(
-        [jnp.where(mine_first, kv_low, nothing), jnp.where(mine_first, nothing, kv_low)], axis=0
-    )
-    head_grads = arrival(
-        jnp.concatenate([query_pre_grad.astype(narrow), kv_both], axis=1), core, line
-    )
-    normed_sum = scatter_chip(transposed_product(head_grads, query_kv_full).astype(narrow))
+        lambda x, g: head_apply(x, kv_gain(g), cosine_kv, sine_kv), kv_pre, head_wide
+    )
+    kv_pre_grad, kv_gain_grad = pull_kv(kv_grad)
+    kv_rows_grad = arrival(kv_pre_grad.astype(narrow), core, line)
+    head_grads = jnp.concatenate([query_rows_grad, kv_rows_grad], axis=1)
+    kv_part = weight_product(normed_rows, kv_rows_grad).astype(narrow)
+    normed_part = transposed_product(head_grads, query_kv_full).astype(narrow)
+    normed_part, kv_part, query_sum, down_sum, two_sum = together(
+        normed_part, kv_part, query_sum, down_sum, two_sum
+    )
+    kv_weight_sum = own_rows(kv_part)
+    normed_sum = scatter_chip(normed_part)
+    normed_sum, query_sum = together(normed_sum, query_sum)
     normed_grad = (
         normed_combine
         + normed_sum
@@ -1041,62 +1093,38 @@
         coef_grad.shape
     )
 
-    small_sum = lax.psum(
-        lax.psum_scatter(
-            jnp.concatenate(
-                [
-                    weight_product(normed_low, down_grad_low),
-                    weight_product(lifted_low, down_low),
-                    weight_product(first_low, gate_pre_low),
-                    weight_product(projected_low, gated_low),
-                ],
-                axis=1,
-            ).astype(narrow),
-            "blk",
-            scatter_dimension=0,
-            tiled=True,
-        ),
-        "heads",
+    down_first, down_second = core_columns(down_sum)
+    two_first, two_second = core_columns(two_sum)
+    pair = CORES * HEAD_WIDTH
+    ranks = 2 * LAUREL_RANK
+    laurel_here = jnp.where(
+        first_core, out_sum[:rows_here, HEAD_WIDTH:], out_sum[rows_here:, HEAD_WIDTH:]
+    )
+    out_lines = gather_line(
+        jnp.concatenate([pairs(out_sum, 1), laurel_here, io_share.reshape(rows_here, -1)], axis=1)
+    )
+    query_lines = gather_line(pairs(query_sum, 1))
+    kv_lines = gather_line(pairs(kv_weight_sum, 1))
+    query_all = jnp.concatenate(query_lines, axis=1).astype(wide)
+    out_all = jnp.concatenate([part[:, :pair] for part in out_lines], axis=1).astype(wide)
+    laurel_all = sum(part[:, pair : pair + ranks].astype(wide) for part in out_lines)
+    io_all = jnp.concatenate(
+        [
+            part[:, pair + ranks :].reshape(rows_here // LINE, 2 * LAYER_INPUT_SIZE)
+            for part in out_lines
+        ],
+        axis=0,
     ).astype(wide)
-    head_sum = own_rows(
-        jnp.concatenate(
-            [
-                weight_product(normed_rows, head_grads).astype(narrow),
-                weight_product(attention_rows, mixed_rows).astype(narrow),
-            ],
-            axis=1,
-        )
-    )
-
-    def core_columns(x):
-        top, bottom = x[:rows_here], x[rows_here:]
-        keep = jnp.where(first_core, top, bottom)
-        got = other_core(jnp.where(first_core, bottom, top))
-        return jnp.where(first_core, keep, got), jnp.where(first_core, got, keep)
-
-    head_first, head_second = core_columns(head_sum)
-    unit_first, unit_second = core_columns(unit_sum)
-
-    def both(index):
-        columns = slice(index * HEAD_WIDTH, (index + 1) * HEAD_WIDTH)
-        return [head_first[:, columns], head_second[:, columns]]
-
-    line_all = lax.all_gather(
-        jnp.concatenate(both(0) + both(2) + both(1), axis=1), "heads", axis=0, tiled=False
-    ).astype(wide)
-    pair = CORES * HEAD_WIDTH
-    query_sum = jnp.concatenate([line_all[i, :, :pair] for i in range(LINE)], axis=1)
-    out_sum = jnp.concatenate([line_all[i, :, pair : 2 * pair] for i in range(LINE)], axis=1)
-    kv_lines = line_all[:, :, 2 * pair :]
-    kv_groups = [kv_lines[0] + kv_lines[1], kv_lines[2] + kv_lines[3]]
+    kv_groups = [
+        kv_lines[k].astype(wide) + kv_lines[k + 1].astype(wide) for k in range(0, LINE, 2)
+    ]
     key_sum = jnp.concatenate([g[:, :HEAD_WIDTH] for g in kv_groups], axis=1)
     value_sum = jnp.concatenate([g[:, HEAD_WIDTH:] for g in kv_groups], axis=1)
 
     def unit(index):
         columns = slice(index * hidden, (index + 1) * hidden)
-        return jnp.concatenate([unit_first[:, columns], unit_second[:, columns]], axis=1).astype(wide)
-
-    ranks = 2 * LAUREL_RANK
+        return jnp.concatenate([two_first[:, columns], two_second[:, columns]], axis=1).astype(wide)
+
     return (
         result,
         jnp.stack([g.astype(narrow) for g in version_grad]),
@@ -1105,16 +1133,16 @@
         packed[8:12],
         coef_sum,
         head_gain_sum,
-        query_sum,
+        query_all,
         key_sum,
         value_sum,
-        out_sum,
-        small_sum[:, :ranks],
-        small_sum[:, ranks : ranks + LAYER_INPUT_SIZE],
-        small_sum[:, ranks + LAYER_INPUT_SIZE :],
+        out_all,
+        laurel_all,
+        io_all[:, :LAYER_INPUT_SIZE],
+        io_all[:, LAYER_INPUT_SIZE:],
         unit(0),
         unit(1),
-        unit(2),
+        jnp.concatenate([down_first, down_second], axis=1).astype(wide),
     )
 
 

time: 939 us -> 751 us (0.80)
  waiting for transfers between devices: 449 us -> 280 us
  local copies, waits for them, and re-layouts: 75.6 us -> 61 us
  matrix products: 112 us -> 123 us
    reduce_scatter x2 -> x5, waiting for transfers between devices: 108 us -> 7.46 us  [own_rows(): lax.psum_scatter(x, 'blk', scatter_dimension=0, tiled=True, axis_index_gr...]
    reduce_scatter x1, waiting for transfers between devices: 45.6 us -> 0.01 us  [chip_device(): lax.psum_scatter(jnp.concatenate([weight_product(first_low, gate_pre_low)...]
    concatenate x6, other arithmetic: 29.2 us -> 4.89 us  [the longest x1 1.57 us: chip_device(): jnp.concatenate([weight_product(first_low, gate_pre_low), weight_product(...]
    ppermute x32 -> x47, starting transfers between devices: 78.6 us -> 97.8 us  [along_heads(): lax.ppermute(x, 'heads', [(i, (i + step) % LINE) for i in range(LINE)])]
    ppermute x53 -> x57, starting transfers between devices: 48.1 us -> 29.4 us  [across_blk(): return lax.ppermute(x, 'blk', [(i, i ^ mask) for i in range(CORES * CHIPS)])]
    unnamed x416 -> x460, local copies, waits for them, and re-layouts: 46.6 us -> 33.7 us
    ppermute x53 -> x57, waiting for transfers between devices: 57.7 us -> 48.4 us  [across_blk(): return lax.ppermute(x, 'blk', [(i, i ^ mask) for i in range(CORES * CHIPS)])]
    ppermute x32 -> x47, waiting for transfers between devices: 228 us -> 224 us  [along_heads(): lax.ppermute(x, 'heads', [(i, (i + step) % LINE) for i in range(LINE)])]
  transfers between devices with their start and end apart: 96 -> 115, of which waited for: 58 -> 62; matrix products, arithmetic and copies ran while one was open for 21% -> 30% of each run, Pallas kernels for 0% -> 2%
where the time goes in v2:
time: 751 us; the launch traced here: 745 us
  waiting for transfers between devices  280 us (37%)
  starting transfers between devices  130 us (17%)
  matrix products  123 us (16%)
  other arithmetic  114 us (15%)
  local copies, waits for them, and re-layouts  61 us (8%)
  between operations  24.9 us (3%)
  Pallas kernels  11.8 us (2%)
    ppermute x47, waiting for transfers between devices, along_heads(): lax.ppermute(x, 'heads', [(i, (i + step) % LINE) for i in range(LINE)])  224 us
    ppermute x47, starting transfers between devices, along_heads(): lax.ppermute(x, 'heads', [(i, (i + step) % LINE) for i in range(LINE)])  97.8 us
    ppermute x57, waiting for transfers between devices, across_blk(): return lax.ppermute(x, 'blk', [(i, i ^ mask) for i in range(CORES * CHIPS)])  48.4 us
    dot_general x9, matrix products, forward_product(): return jnp.dot(left, right, preferred_element_type=jnp.float32)  45.3 us
    dot_general x8, matrix products, transposed_product(): lax.dot_general(left, right, (((1,), (1,)), ((), ())), preferred_element_...  34.2 us
    unnamed x460, local copies, waits for them, and re-layouts  33.7 us
    dot_general x9, matrix products, weight_product(): lax.dot_general(left, right, (((0,), (0,)), ((), ())), preferred_element_...  33.6 us
    ppermute x57, starting transfers between devices, across_blk(): return lax.ppermute(x, 'blk', [(i, i ^ mask) for i in range(CORES * CHIPS)])  29.4 us
  transfers between devices with their start and end apart: 115, of which 62 were waited for; matrix products, arithmetic and copies ran while one was open for 30% of the time, Pallas kernels for 2%

profile of v2, /device:TPU:0, one launch (start us, length us, event | category | flops | bytes accessed | tf_op | source)
XLA Modules:
  0.0 745.4 jit_solution(13339473918807892325)
XLA Ops:
  25.7 5.0 collective-permute-start.1
  34.9 9.2 %collective-permute-done.1 = bf16[128,2176]{1,0:T(8,128)(2,1)S(1)} collective-permute-done((bf16[128,2176]{1,0:T(8,128)(2,1)}, bf16[128,2176]{1,0:T(8,128)(2,1)S(1)}, u32[]{:S(2)}, u32[]{:S(2)}) %collective-permute-start.1) | collective-permute-done | bytes 557088 | tf_op jit(solution)/shard_map/ppermute | solution.py:441
  48.3 8.5 %collective-permute-done = bf16[128,2176]{1,0:T(8,128)(2,1)S(1)} collective-permute-done((bf16[128,2176]{1,0:T(8,128)(2,1)}, bf16[128,2176]{1,0:T(8,128)(2,1)S(1)}, u32[]{:S(2)}, u32[]{:S(2)}) %collective-permute-start) | collective-permute-done | bytes 557088 | tf_op jit(solution)/shard_map/ppermute | solution.py:441
  62.7 5.2 collective-permute-done.2
  72.6 5.3 fusion.23
  80.4 4.9 fusion.126
  88.4 13.3 %collective-permute-done.10.refs_2_ = bf16[1024,256]{1,0:T(8,128)(2,1)S(1)} collective-permute-done((bf16[1024,256]{1,0:T(8,128)(2,1)S(1)}, bf16[1024,256]{1,0:T(8,128)(2,1)S(1)}, u32[]{:S(2)}, u32[]{:S(2)}) %collective-permute-start.10) | collective-permute-done | bytes 524320 | tf_op jit(solution)/shard_map/ppermute | solution.py:445
  104.4 6.9 collective-permute-done.12.refs_4_
  141.0 6.5 collective-permute-done.24
  159.5 6.2 collective-permute-done.25
  165.7 10.4 %collective-permute-done.22 = bf16[128,2048]{1,0:T(8,128)(2,1)} collective-permute-done((bf16[128,2048]{1,0:T(8,128)(2,1)}, bf16[128,2048]{1,0:T(8,128)(2,1)}, u32[]{:S(2)}, u32[]{:S(2)}) %collective-permute-start.22) | collective-permute-done | bytes 524320 | tf_op jit(solution)/shard_map/ppermute | solution.py:441
  183.3 12.3 %collective-permute-done.27 = bf16[128,2048]{1,0:T(8,128)(2,1)S(1)} collective-permute-done((bf16[128,2048]{1,0:T(8,128)(2,1)S(1)}, bf16[128,2048]{1,0:T(8,128)(2,1)S(1)}, u32[]{:S(2)}, u32[]{:S(2)}) %collective-permute-start.27) | collective-permute-done | bytes 524320 | tf_op jit(solution)/shard_map/ppermute | solution.py:441
  195.6 4.3 collective-permute-start.29
  200.0 7.9 %collective-permute-done.26 = bf16[128,2048]{1,0:T(8,128)(2,1)S(1)} collective-permute-done((bf16[128,2048]{1,0:T(8,128)(2,1)S(1)}, bf16[128,2048]{1,0:T(8,128)(2,1)S(1)}, u32[]{:S(2)}, u32[]{:S(2)}) %collective-permute-start.26) | collective-permute-done | bytes 524320 | tf_op jit(solution)/shard_map/ppermute | solution.py:441
  213.3 4.9 collective-permute-done.28
  223.2 7.8 %fusion.11 = f32[1024,1024]{0,1:T(8,128)S(1)} fusion(bf16[1024,2048]{1,0:T(8,128)(2,1)} %constant_dynamic-update-slice_fusion.9, bf16[2048,3072]{1,0:T(8,128)(2,1)} %all-gather.8.cloned.1.call-done), kind=kOutput, calls=%fused_computation.14 | convolution fusion | flops 4294967296 | bytes 12582912 | tf_op jit(solution)/shard_map/dot_general | solution.py:111
  231.0 10.9 %multiply_convert_fusion.1 = (bf16[1024,1024]{0,1:T(8,128)(2,1)}, f32[1024,1024]{0,1:T(8,128)}) fusion(f32[1024,1024]{0,1:T(8,128)S(1)} %fusion.11, bf16[1024,2048]{1,0:T(8,128)(2,1)} %constant_dynamic-update-slice_fusion.9, bf16[2048,3072]{1,0:T(8,128)(2,1)S(1)} %copy-done.188), kind=kOutput, calls=%fused_computation.31 | convolution fusion | flops 4305453056 | bytes 18874368 | tf_op jit(solution)/shard_map/dot_general | solution.py:111
  241.9 6.4 convolution_convert_fusion.4
  255.9 6.5 collective-permute-done.41
  262.5 4.3 collective-permute-start.42
  270.9 9.6 %collective-permute-done.42 = bf16[128,2048]{1,0:T(8,128)(2,1)S(1)} collective-permute-done((bf16[128,2048]{1,0:T(8,128)(2,1)S(1)}, bf16[128,2048]{1,0:T(8,128)(2,1)S(1)}, u32[]{:S(2)}, u32[]{:S(2)}) %collective-permute-start.42) | collective-permute-done | bytes 524320 | tf_op jit(solution)/shard_map/ppermute | solution.py:441
  280.4 10.8 %collective-permute-done.39 = bf16[128,2048]{1,0:T(8,128)(2,1)S(1)} collective-permute-done((bf16[128,2048]{1,0:T(8,128)(2,1)S(1)}, bf16[128,2048]{1,0:T(8,128)(2,1)S(1)}, u32[]{:S(2)}, u32[]{:S(2)}) %collective-permute-start.39) | collective-permute-done | bytes 524320 | tf_op jit(solution)/shard_map/ppermute | solution.py:441
  320.1 12.3 %collective-permute-done.44 = bf16[128,2048]{1,0:T(8,128)(2,1)S(1)} collective-permute-done((bf16[128,2048]{1,0:T(8,128)(2,1)S(1)}, bf16[128,2048]{1,0:T(8,128)(2,1)S(1)}, u32[]{:S(2)}, u32[]{:S(2)}) %collective-permute-start.44) | collective-permute-done | bytes 524320 | tf_op jit(solution)/shard_map/ppermute | solution.py:441
  332.5 4.3 collective-permute-start.46
  336.8 7.9 %collective-permute-done.43 = bf16[128,2048]{1,0:T(8,128)(2,1)S(1)} collective-permute-done((bf16[128,2048]{1,0:T(8,128)(2,1)S(1)}, bf16[128,2048]{1,0:T(8,128)(2,1)S(1)}, u32[]{:S(2)}, u32[]{:S(2)}) %collective-permute-start.43) | collective-permute-done | bytes 524320 | tf_op jit(solution)/shard_map/ppermute | solution.py:441
  350.1 4.9 collective-permute-done.45
  360.0 9.4 %convolution_convert_fusion.3 = bf16[2048,1024]{1,0:T(8,128)(2,1)} fusion(bf16[1024,2048]{1,0:T(8,128)(2,1)} %constant_dynamic-update-slice_fusion.18, bf16[1024,1024]{0,1:T(8,128)(2,1)} %get-tuple-element.404), kind=kOutput, calls=%fused_computation.68 | convolution fusion | flops 4297064448 | bytes 10485760 | tf_op jit(solution)/shard_map/dot_general | solution.py:121
  369.5 12.2 %fusion.8 = (bf16[1024,1024]{0,1:T(8,128)(2,1)S(1)}, bf16[1024,1024]{0,1:T(8,128)(2,1)S(1)}) fusion(f32[1024,1024]{0,1:T(8,128)} %copy-done.198, f32[1024,1024]{0,1:T(8,128)} %get-tuple-element.405, bf16[1024,2048]{1,0:T(8,128)(2,1)} %constant_dynamic-update-slice_fusion.18, bf16[2048,3072]{1,0:T(8,128)(2,1)} %all-gather.8.cloned.1.call-done), kind=kOutput, calls=%fused_computation.11 | convolution fusion | flops 4320133120 | bytes 20971520 | tf_op jit(solution)/shard_map/dot_general | solution.py:111
  383.6 14.5 %convolution_convert_fusion = bf16[2048,2048]{1,0:T(8,128)(2,1)} fusion(bf16[1024,2048]{1,0:T(8,128)(2,1)} %constant_dynamic-update-slice_fusion.9, bf16[1024,1024]{0,1:T(8,128)(2,1)S(1)} %get-tuple-element.226, bf16[1024,1024]{0,1:T(8,128)(2,1)S(1)} %get-tuple-element.225), kind=kOutput, calls=%fused_computation.2 | convolution fusion | flops 8602517504 | bytes 16777216 | tf_op jit(solution)/shard_map/dot_general | solution.py:121
  398.7 12.7 %fusion.13 = bf16[1024,2048]{1,0:T(8,128)(2,1)S(1)} fusion(bf16[2048,3072]{1,0:T(8,128)(2,1)} %all-gather.8.cloned.1.call-done, bf16[1024,1024]{0,1:T(8,128)(2,1)} %copy-done.200, bf16[1024,1024]{0,1:T(8,128)(2,1)} %copy-done.199), kind=kOutput, calls=%fused_computation.65 | convolution fusion | flops 8600420352 | bytes 16777216 | tf_op jit(solution)/shard_map/dot_general | solution.py:115
  424.2 4.6 collective-permute-done.57
  448.2 11.2 %collective-permute-done.55 = bf16[128,2048]{1,0:T(8,128)(2,1)} collective-permute-done((bf16[128,2048]{1,0:T(8,128)(2,1)}, bf16[128,2048]{1,0:T(8,128)(2,1)}, u32[]{:S(2)}, u32[]{:S(2)}) %collective-permute-start.55) | collective-permute-done | bytes 524320 | tf_op jit(solution)/shard_map/ppermute | solution.py:441
  472.6 8.0 %collective-permute-done.60 = bf16[128,2048]{1,0:T(8,128)(2,1)S(1)} collective-permute-done((bf16[128,2048]{1,0:T(8,128)(2,1)S(1)}, bf16[128,2048]{1,0:T(8,128)(2,1)S(1)}, u32[]{:S(2)}, u32[]{:S(2)}) %collective-permute-start.60) | collective-permute-done | bytes 524320 | tf_op jit(solution)/shard_map/ppermute | solution.py:441
  485.0 7.9 %collective-permute-done.59 = bf16[128,2048]{1,0:T(8,128)(2,1)S(1)} collective-permute-done((bf16[128,2048]{1,0:T(8,128)(2,1)S(1)}, bf16[128,2048]{1,0:T(8,128)(2,1)S(1)}, u32[]{:S(2)}, u32[]{:S(2)}) %collective-permute-start.59) | collective-permute-done | bytes 524320 | tf_op jit(solution)/shard_map/ppermute | solution.py:441
  498.4 4.8 collective-permute-done.61
  508.5 4.7 convolution_convert_fusion.10
  518.7 7.7 %shard_map.315 = (f32[1024,256]{1,0:T(8,128)}, bf16[4,1024,256]{2,1,0:T(8,128)(2,1)}, bf16[4,1024,256]{2,1,0:T(8,128)(2,1)}) custom-call(s32[6]{0:T(128)S(1)} %copy-done.6, bf16[1024,256]{1,0:T(8,128)(2,1)S(1)} %get-tuple-element.346.q_ref, bf16[1024,256]{1,0:T(8,128)(2,1)S(1)} %pad_maximum_fusion.26.grad_ref, f32[1,1024]{1,0:T(1,128)S(1)} %bitcast.343, ...), custom_call_target="tpu_custom_call" | custom-call | flops 5368709120 | bytes 12582912 | tf_op jit(solution)/shard_map/pallas_call | solution.py:767
  526.5 4.6 convert_multiply_fusion.54
  538.1 4.6 fusion.25
  545.4 5.1 reduce-scatter.13.cloned.1.call-done
  553.3 9.7 %collective-permute-start.73 = (bf16[1024,256]{1,0:T(8,128)(2,1)S(1)}, bf16[1024,256]{1,0:T(8,128)(2,1)S(1)}, u32[]{:S(2)}, u32[]{:S(2)}) collective-permute-start(bf16[1024,256]{1,0:T(8,128)(2,1)S(1)} %pad_maximum_fusion.28), channel_id=1, source_target_pairs={{0,4},{1,5},{2,6},{3,7},{4,0},{5,1},{6,2},{7,3},{8,12},{9,13},{10,... | collective-permute-start | bytes 1572872 | tf_op jit(solution)/shard_map/ppermute | solution.py:445
  568.8 6.1 collective-permute-done.73
  611.4 4.3 convolution_convert_fusion.1
  629.6 8.5 %collective-permute-done.82 = bf16[64,2048]{1,0:T(8,128)(2,1)S(1)} collective-permute-done((bf16[64,2048]{1,0:T(8,128)(2,1)S(1)}, bf16[64,2048]{1,0:T(8,128)(2,1)S(1)}, u32[]{:S(2)}, u32[]{:S(2)}) %collective-permute-start.82) | collective-permute-done | bytes 262176 | tf_op jit(solution)/shard_map/ppermute | solution.py:441
  644.3 8.5 %collective-permute-done.83 = bf16[128,2048]{1,0:T(8,128)(2,1)S(1)} collective-permute-done((bf16[128,2048]{1,0:T(8,128)(2,1)S(1)}, bf16[128,2048]{1,0:T(8,128)(2,1)S(1)}, u32[]{:S(2)}, u32[]{:S(2)}) %collective-permute-start.83) | collective-permute-done | bytes 524320 | tf_op jit(solution)/shard_map/ppermute | solution.py:441
  652.8 11.7 %collective-permute-done.80 = bf16[128,2048]{1,0:T(8,128)(2,1)S(1)} collective-permute-done((bf16[128,2048]{1,0:T(8,128)(2,1)S(1)}, bf16[128,2048]{1,0:T(8,128)(2,1)S(1)}, u32[]{:S(2)}, u32[]{:S(2)}) %collective-permute-start.80) | collective-permute-done | bytes 524320 | tf_op jit(solution)/shard_map/ppermute | solution.py:441
  705.8 5.1 collective-permute-done.92
  731.3 5.2 collective-permute-done.97
  (951 shorter events, 352.7 us)
Async XLA Ops:
  7.2 65.4 %all-gather.4.cloned.1.call-start = ((), (), s32[]{:S(2)}) async-start(), calls=%async_computation.6 | async-start | bytes 3932160 | tf_op jit(solution)/shard_map/all_gather | solution.py:562
  12.7 143.7 %all-gather.6.cloned.1.call-start = ((), (), s32[]{:S(2)}) async-start(), calls=%async_computation.7 | async-start | bytes 2949120 | tf_op jit(solution)/shard_map/all_gather | solution.py:873
  13.6 209.6 %all-gather.8.cloned.1.call-start = ((), (), s32[]{:S(2)}) async-start(), calls=%async_computation.8 | async-start | bytes 15728640 | tf_op jit(solution)/shard_map/all_gather | solution.py:562
  25.6 42.6 %collective-permute-start.5 = (bf16[128,2176]{1,0:T(8,128)(2,1)}, bf16[128,2176]{1,0:T(8,128)(2,1)}, u32[]{:S(2)}, u32[]{:S(2)}) collective-permute-start(bf16[128,2176]{1,0:T(8,128)(2,1)} %fusion.150), channel_id=1, source_target_pairs={{0,1},{1,0},{2,3},{3,2},{4,5},{5,4},{6,7},{7,6},{8,9},{9,8},{10,11... | collective-permute-start | bytes 1671176 | tf_op jit(solution)/shard_map/ppermute | solution.py:445
  25.7 18.3 %collective-permute-start.1 = (bf16[128,2176]{1,0:T(8,128)(2,1)}, bf16[128,2176]{1,0:T(8,128)(2,1)S(1)}, u32[]{:S(2)}, u32[]{:S(2)}) collective-permute-start(bf16[128,2176]{1,0:T(8,128)(2,1)} %fusion.150), channel_id=1, source_target_pairs={{0,24},{8,0},{16,8},{24,16},{1,25},{9,1},{17,9},{25,17},{2,26},{10... | collective-permute-start | bytes 1671176 | tf_op jit(solution)/shard_map/ppermute | solution.py:441
  30.7 26.1 %collective-permute-start = (bf16[128,2176]{1,0:T(8,128)(2,1)}, bf16[128,2176]{1,0:T(8,128)(2,1)S(1)}, u32[]{:S(2)}, u32[]{:S(2)}) collective-permute-start(bf16[128,2176]{1,0:T(8,128)(2,1)} %fusion.150), channel_id=1, source_target_pairs={{0,8},{8,16},{16,24},{24,0},{1,9},{9,17},{17,25},{25,1},{2,10},{10... | collective-permute-start | bytes 1671176 | tf_op jit(solution)/shard_map/ppermute | solution.py:441
  34.8 325.2 %reduce-scatter.7.cloned.1.call-start = ((), (), s32[]{:S(2)}) async-start(), calls=%async_computation.9 | async-start | bytes 2359296 | tf_op jit(solution)/shard_map/reduce_scatter | solution.py:995
  44.1 18.6 %collective-permute-start.3 = (bf16[64,2176]{1,0:T(8,128)(2,1)S(1)}, bf16[64,2176]{1,0:T(8,128)(2,1)S(1)}, u32[]{:S(2)}, u32[]{:S(2)}) collective-permute-start(bf16[64,2176]{1,0:T(8,128)(2,1)S(1)} %slice.942), channel_id=1, source_target_pairs={{0,24},{8,0},{16,8},{24,16},{1,25},{9,1},{17,9},{25,17},{2,26},{10... | collective-permute-start | bytes 835592 | tf_op jit(solution)/shard_map/ppermute | solution.py:441
  85.3 16.4 %collective-permute-start.10 = (bf16[1024,256]{1,0:T(8,128)(2,1)S(1)}, bf16[1024,256]{1,0:T(8,128)(2,1)S(1)}, u32[]{:S(2)}, u32[]{:S(2)}) collective-permute-start(bf16[1024,256]{1,0:T(8,128)(2,1)S(1)} %get-tuple-element.345.refs_0_), channel_id=1, source_target_pairs={{0,4},{1,5},{2,6},{3,7},{4,0},{5,1},{6,2},{7,3},{8,12},{9,13},{10,... | collective-permute-start | bytes 1572872 | tf_op jit(solution)/shard_map/ppermute | solution.py:445
  86.9 16.3 %collective-permute-start.9 = (bf16[1024,256]{1,0:T(8,128)(2,1)S(1)}, bf16[1024,256]{1,0:T(8,128)(2,1)S(1)}, u32[]{:S(2)}, u32[]{:S(2)}) collective-permute-start(bf16[1024,256]{1,0:T(8,128)(2,1)S(1)} %get-tuple-element.345.refs_0_), channel_id=1, source_target_pairs={{0,2},{1,3},{2,0},{3,1},{4,6},{5,7},{6,4},{7,5},{8,10},{9,11},{10,... | collective-permute-start | bytes 1572872 | tf_op jit(solution)/shard_map/ppermute | solution.py:445
  103.9 18.9 %collective-permute-start.13 = (bf16[1024,256]{1,0:T(8,128)(2,1)S(1)}, bf16[1024,256]{1,0:T(8,128)(2,1)}, u32[]{:S(2)}, u32[]{:S(2)}) collective-permute-start(bf16[1024,256]{1,0:T(8,128)(2,1)S(1)} %get-tuple-element.345.refs_0_), channel_id=1, source_target_pairs={{0,1},{1,0},{2,3},{3,2},{4,5},{5,4},{6,7},{7,6},{8,9},{9,8},{10,11... | collective-permute-start | bytes 1572872 | tf_op jit(solution)/shard_map/ppermute | solution.py:445
  103.9 18.9 %collective-permute-start.15 = (bf16[1024,256]{1,0:T(8,128)(2,1)S(1)}, bf16[1024,256]{1,0:T(8,128)(2,1)}, u32[]{:S(2)}, u32[]{:S(2)}) collective-permute-start(bf16[1024,256]{1,0:T(8,128)(2,1)S(1)} %collective-permute-done.10.refs_2_), channel_id=1, source_target_pairs={{0,1},{1,0},{2,3},{3,2},{4,5},{5,4},{6,7},{7,6},{8,9},{9,8},{10,11... | collective-permute-start | bytes 1572872 | tf_op jit(solution)/shard_map/ppermute | solution.py:445
  104.4 18.4 %collective-permute-start.14 = (bf16[1024,256]{1,0:T(8,128)(2,1)S(1)}, bf16[1024,256]{1,0:T(8,128)(2,1)}, u32[]{:S(2)}, u32[]{:S(2)}) collective-permute-start(bf16[1024,256]{1,0:T(8,128)(2,1)S(1)} %collective-permute-done.9.refs_1_), channel_id=1, source_target_pairs={{0,1},{1,0},{2,3},{3,2},{4,5},{5,4},{6,7},{7,6},{8,9},{9,8},{10,11... | collective-permute-start | bytes 1572872 | tf_op jit(solution)/shard_map/ppermute | solution.py:445
  140.8 18.7 %collective-permute-start.18 = (bf16[128,2048]{1,0:T(8,128)(2,1)}, bf16[128,2048]{1,0:T(8,128)(2,1)}, u32[]{:S(2)}, u32[]{:S(2)}) collective-permute-start(bf16[128,2048]{1,0:T(8,128)(2,1)} %get-tuple-element.252), channel_id=1, source_target_pairs={{0,1},{1,0},{2,3},{3,2},{4,5},{5,4},{6,7},{7,6},{8,9},{9,8},{10,11... | collective-permute-start | bytes 1572872 | tf_op jit(solution)/shard_map/ppermute | solution.py:445
  148.4 17.4 %collective-permute-start.25 = (bf16[128,2048]{1,0:T(8,128)(2,1)}, bf16[128,2048]{1,0:T(8,128)(2,1)}, u32[]{:S(2)}, u32[]{:S(2)}) collective-permute-start(bf16[128,2048]{1,0:T(8,128)(2,1)} %pad_maximum_fusion.17), channel_id=1, source_target_pairs={{0,24},{8,0},{16,8},{24,16},{1,25},{9,1},{17,9},{25,17},{2,26},{10... | collective-permute-start | bytes 1572872 | tf_op jit(solution)/shard_map/ppermute | solution.py:441
  155.0 21.1 %collective-permute-start.22 = (bf16[128,2048]{1,0:T(8,128)(2,1)}, bf16[128,2048]{1,0:T(8,128)(2,1)}, u32[]{:S(2)}, u32[]{:S(2)}) collective-permute-start(bf16[128,2048]{1,0:T(8,128)(2,1)} %pad_maximum_fusion.16), channel_id=1, source_target_pairs={{0,8},{8,16},{16,24},{24,0},{1,9},{9,17},{17,25},{25,1},{2,10},{10... | collective-permute-start | bytes 1572872 | tf_op jit(solution)/shard_map/ppermute | solution.py:441
  183.3 24.6 %collective-permute-start.26 = (bf16[128,2048]{1,0:T(8,128)(2,1)S(1)}, bf16[128,2048]{1,0:T(8,128)(2,1)S(1)}, u32[]{:S(2)}, u32[]{:S(2)}) collective-permute-start(bf16[128,2048]{1,0:T(8,128)(2,1)S(1)} %multiply_convert_fusion.3), channel_id=1, source_target_pairs={{0,8},{8,16},{16,24},{24,0},{1,9},{9,17},{17,25},{25,1},{2,10},{10... | collective-permute-start | bytes 1572872 | tf_op jit(solution)/shard_map/ppermute | solution.py:441
  183.3 37.3 %collective-permute-start.31 = (bf16[128,2048]{1,0:T(8,128)(2,1)S(1)}, bf16[128,2048]{1,0:T(8,128)(2,1)S(1)}, u32[]{:S(2)}, u32[]{:S(2)}) collective-permute-start(bf16[128,2048]{1,0:T(8,128)(2,1)S(1)} %multiply_convert_fusion.3), channel_id=1, source_target_pairs={{0,1},{1,0},{2,3},{3,2},{4,5},{5,4},{6,7},{7,6},{8,9},{9,8},{10,11... | collective-permute-start | bytes 1572872 | tf_op jit(solution)/shard_map/ppermute | solution.py:445
  195.6 17.6 %collective-permute-start.29 = (bf16[64,2048]{1,0:T(8,128)(2,1)S(1)}, bf16[64,2048]{1,0:T(8,128)(2,1)S(1)}, u32[]{:S(2)}, u32[]{:S(2)}) collective-permute-start(bf16[64,2048]{1,0:T(8,128)(2,1)S(1)} %slice.985), channel_id=1, source_target_pairs={{0,24},{8,0},{16,8},{24,16},{1,25},{9,1},{17,9},{25,17},{2,26},{10... | collective-permute-start | bytes 786440 | tf_op jit(solution)/shard_map/ppermute | solution.py:441
  262.5 17.9 %collective-permute-start.42 = (bf16[128,2048]{1,0:T(8,128)(2,1)S(1)}, bf16[128,2048]{1,0:T(8,128)(2,1)S(1)}, u32[]{:S(2)}, u32[]{:S(2)}) collective-permute-start(bf16[128,2048]{1,0:T(8,128)(2,1)S(1)} %pad_maximum_fusion.20), channel_id=1, source_target_pairs={{0,24},{8,0},{16,8},{24,16},{1,25},{9,1},{17,9},{25,17},{2,26},{10... | collective-permute-start | bytes 1572872 | tf_op jit(solution)/shard_map/ppermute | solution.py:441
  269.4 21.8 %collective-permute-start.39 = (bf16[128,2048]{1,0:T(8,128)(2,1)S(1)}, bf16[128,2048]{1,0:T(8,128)(2,1)S(1)}, u32[]{:S(2)}, u32[]{:S(2)}) collective-permute-start(bf16[128,2048]{1,0:T(8,128)(2,1)S(1)} %pad_maximum_fusion.19), channel_id=1, source_target_pairs={{0,8},{8,16},{16,24},{24,0},{1,9},{9,17},{17,25},{25,1},{2,10},{10... | collective-permute-start | bytes 1572872 | tf_op jit(solution)/shard_map/ppermute | solution.py:441
  308.7 204.6 %reduce-scatter.9.cloned.1.call-start = ((), (), s32[]{:S(2)}) async-start(), calls=%async_computation.10 | async-start | bytes 5242880 | tf_op jit(solution)/shard_map/reduce_scatter | solution.py:566
  320.1 24.6 %collective-permute-start.43 = (bf16[128,2048]{1,0:T(8,128)(2,1)S(1)}, bf16[128,2048]{1,0:T(8,128)(2,1)S(1)}, u32[]{:S(2)}, u32[]{:S(2)}) collective-permute-start(bf16[128,2048]{1,0:T(8,128)(2,1)S(1)} %fusion.46), channel_id=1, source_target_pairs={{0,8},{8,16},{16,24},{24,0},{1,9},{9,17},{17,25},{25,1},{2,10},{10... | collective-permute-start | bytes 1572872 | tf_op jit(solution)/shard_map/ppermute | solution.py:441
  320.1 37.3 %collective-permute-start.48 = (bf16[128,2048]{1,0:T(8,128)(2,1)S(1)}, bf16[128,2048]{1,0:T(8,128)(2,1)S(1)}, u32[]{:S(2)}, u32[]{:S(2)}) collective-permute-start(bf16[128,2048]{1,0:T(8,128)(2,1)S(1)} %fusion.46), channel_id=1, source_target_pairs={{0,1},{1,0},{2,3},{3,2},{4,5},{5,4},{6,7},{7,6},{8,9},{9,8},{10,11... | collective-permute-start | bytes 1572872 | tf_op jit(solution)/shard_map/ppermute | solution.py:445
  332.5 17.7 %collective-permute-start.46 = (bf16[64,2048]{1,0:T(8,128)(2,1)S(1)}, bf16[64,2048]{1,0:T(8,128)(2,1)S(1)}, u32[]{:S(2)}, u32[]{:S(2)}) collective-permute-start(bf16[64,2048]{1,0:T(8,128)(2,1)S(1)} %slice.1021), channel_id=1, source_target_pairs={{0,24},{8,0},{16,8},{24,16},{1,25},{9,1},{17,9},{25,17},{2,26},{10... | collective-permute-start | bytes 786440 | tf_op jit(solution)/shard_map/ppermute | solution.py:441
  369.4 146.2 %reduce-scatter.11.cloned.1.call-start = ((), (), s32[]{:S(2)}) async-start(), calls=%async_computation.11 | async-start | bytes 10485760 | tf_op jit(solution)/shard_map/reduce_scatter | solution.py:566
  398.2 152.3 %reduce-scatter.13.cloned.1.call-start = ((), (), s32[]{:S(2)}) async-start(), calls=%async_computation.12 | async-start | bytes 1966080 | tf_op jit(solution)/shard_map/reduce_scatter | solution.py:566
  421.8 23.4 %collective-permute-start.51 = (bf16[128,2048]{1,0:T(8,128)(2,1)}, bf16[128,2048]{1,0:T(8,128)(2,1)}, u32[]{:S(2)}, u32[]{:S(2)}) collective-permute-start(bf16[128,2048]{1,0:T(8,128)(2,1)} %get-tuple-element.238), channel_id=1, source_target_pairs={{0,1},{1,0},{2,3},{3,2},{4,5},{5,4},{6,7},{7,6},{8,9},{9,8},{10,11... | collective-permute-start | bytes 1572872 | tf_op jit(solution)/shard_map/ppermute | solution.py:445
  430.8 17.5 %collective-permute-start.58 = (bf16[128,2048]{1,0:T(8,128)(2,1)}, bf16[128,2048]{1,0:T(8,128)(2,1)}, u32[]{:S(2)}, u32[]{:S(2)}) collective-permute-start(bf16[128,2048]{1,0:T(8,128)(2,1)} %pad_maximum_fusion.23), channel_id=1, source_target_pairs={{0,24},{8,0},{16,8},{24,16},{1,25},{9,1},{17,9},{25,17},{2,26},{10... | collective-permute-start | bytes 1572872 | tf_op jit(solution)/shard_map/ppermute | solution.py:441
  436.1 23.4 %collective-permute-start.55 = (bf16[128,2048]{1,0:T(8,128)(2,1)}, bf16[128,2048]{1,0:T(8,128)(2,1)}, u32[]{:S(2)}, u32[]{:S(2)}) collective-permute-start(bf16[128,2048]{1,0:T(8,128)(2,1)} %pad_maximum_fusion.22), channel_id=1, source_target_pairs={{0,8},{8,16},{16,24},{24,0},{1,9},{9,17},{17,25},{25,1},{2,10},{10... | collective-permute-start | bytes 1572872 | tf_op jit(solution)/shard_map/ppermute | solution.py:441
  441.3 29.2 %collective-permute-start.67 = (bf16[64,512]{0,1:T(8,128)(2,1)S(1)}, bf16[64,512]{0,1:T(8,128)(2,1)S(1)}, u32[]{:S(2)}, u32[]{:S(2)}) collective-permute-start(bf16[64,512]{0,1:T(8,128)(2,1)S(1)} %get-tuple-element.359), channel_id=1, source_target_pairs={{0,8},{8,16},{16,24},{24,0},{1,9},{9,17},{17,25},{25,1},{2,10},{10... | collective-permute-start | bytes 196616 | tf_op jit(solution)/shard_map/ppermute | solution.py:441
  442.8 28.5 %collective-permute-start.69 = (bf16[64,512]{0,1:T(8,128)(2,1)S(1)}, bf16[64,512]{0,1:T(8,128)(2,1)S(1)}, u32[]{:S(2)}, u32[]{:S(2)}) collective-permute-start(bf16[64,512]{0,1:T(8,128)(2,1)S(1)} %get-tuple-element.360), channel_id=1, source_target_pairs={{0,24},{8,0},{16,8},{24,16},{1,25},{9,1},{17,9},{25,17},{2,26},{10... | collective-permute-start | bytes 196616 | tf_op jit(solution)/shard_map/ppermute | solution.py:441
  445.2 26.1 %collective-permute-start.68 = (bf16[64,512]{0,1:T(8,128)(2,1)S(1)}, bf16[64,512]{0,1:T(8,128)(2,1)S(1)}, u32[]{:S(2)}, u32[]{:S(2)}) collective-permute-start(bf16[64,512]{0,1:T(8,128)(2,1)S(1)} %get-tuple-element.361), channel_id=1, source_target_pairs={{0,16},{8,24},{16,0},{24,8},{1,17},{9,25},{17,1},{25,9},{2,18},{10... | collective-permute-start | bytes 196616 | tf_op jit(solution)/shard_map/ppermute | solution.py:441
  468.3 24.6 %collective-permute-start.59 = (bf16[128,2048]{1,0:T(8,128)(2,1)S(1)}, bf16[128,2048]{1,0:T(8,128)(2,1)S(1)}, u32[]{:S(2)}, u32[]{:S(2)}) collective-permute-start(bf16[128,2048]{1,0:T(8,128)(2,1)S(1)} %get-tuple-element.299), channel_id=1, source_target_pairs={{0,8},{8,16},{16,24},{24,0},{1,9},{9,17},{17,25},{25,1},{2,10},{10... | collective-permute-start | bytes 1572872 | tf_op jit(solution)/shard_map/ppermute | solution.py:441
  470.5 24.2 %collective-permute-start.70 = (bf16[2048,128]{0,1:T(8,128)(2,1)S(1)}, bf16[2048,128]{0,1:T(8,128)(2,1)S(1)}, u32[]{:S(2)}, u32[]{:S(2)}) collective-permute-start(bf16[2048,128]{0,1:T(8,128)(2,1)S(1)} %pad_maximum_fusion.25), channel_id=1, source_target_pairs={{0,1},{1,0},{2,3},{3,2},{4,5},{5,4},{6,7},{7,6},{8,9},{9,8},{10,11... | collective-permute-start | bytes 1572872 | tf_op jit(solution)/shard_map/ppermute | solution.py:445
  472.2 31.3 %collective-permute-start.64 = (bf16[128,2048]{1,0:T(8,128)(2,1)S(1)}, bf16[128,2048]{1,0:T(8,128)(2,1)S(1)}, u32[]{:S(2)}, u32[]{:S(2)}) collective-permute-start(bf16[128,2048]{1,0:T(8,128)(2,1)S(1)} %get-tuple-element.299), channel_id=1, source_target_pairs={{0,1},{1,0},{2,3},{3,2},{4,5},{5,4},{6,7},{7,6},{8,9},{9,8},{10,11... | collective-permute-start | bytes 1572872 | tf_op jit(solution)/shard_map/ppermute | solution.py:445
  480.7 17.8 %collective-permute-start.62 = (bf16[64,2048]{1,0:T(8,128)(2,1)S(1)}, bf16[64,2048]{1,0:T(8,128)(2,1)S(1)}, u32[]{:S(2)}, u32[]{:S(2)}) collective-permute-start(bf16[64,2048]{1,0:T(8,128)(2,1)S(1)} %slice.1038), channel_id=1, source_target_pairs={{0,24},{8,0},{16,8},{24,16},{1,25},{9,1},{17,9},{25,17},{2,26},{10... | collective-permute-start | bytes 786440 | tf_op jit(solution)/shard_map/ppermute | solution.py:441
  517.7 100.4 %reduce-scatter.15.cloned.1.call-start = ((), (), s32[]{:S(2)}) async-start(), calls=%async_computation.13 | async-start | bytes 1310720 | tf_op jit(solution)/shard_map/reduce_scatter | solution.py:566
  526.4 16.3 %collective-permute-start.71 = (bf16[4,1024,256]{2,1,0:T(8,128)(2,1)}, bf16[4,1024,256]{2,1,0:T(8,128)(2,1)}, u32[]{:S(2)}, u32[]{:S(2)}) collective-permute-start(bf16[4,1024,256]{2,1,0:T(8,128)(2,1)} %get-tuple-element.83), channel_id=1, source_target_pairs={{0,1},{1,0},{2,3},{3,2},{4,5},{5,4},{6,7},{7,6},{8,9},{9,8},{10,11... | collective-permute-start | bytes 6291464 | tf_op jit(solution)/shard_map/ppermute | solution.py:445
  551.8 16.1 %collective-permute-start.72 = (bf16[1024,256]{1,0:T(8,128)(2,1)S(1)}, bf16[1024,256]{1,0:T(8,128)(2,1)S(1)}, u32[]{:S(2)}, u32[]{:S(2)}) collective-permute-start(bf16[1024,256]{1,0:T(8,128)(2,1)S(1)} %pad_maximum_fusion.27), channel_id=1, source_target_pairs={{0,2},{1,3},{2,0},{3,1},{4,6},{5,7},{6,4},{7,5},{8,10},{9,11},{10,... | collective-permute-start | bytes 1572872 | tf_op jit(solution)/shard_map/ppermute | solution.py:445
  553.3 21.7 %collective-permute-start.73 = (bf16[1024,256]{1,0:T(8,128)(2,1)S(1)}, bf16[1024,256]{1,0:T(8,128)(2,1)S(1)}, u32[]{:S(2)}, u32[]{:S(2)}) collective-permute-start(bf16[1024,256]{1,0:T(8,128)(2,1)S(1)} %pad_maximum_fusion.28), channel_id=1, source_target_pairs={{0,4},{1,5},{2,6},{3,7},{4,0},{5,1},{6,2},{7,3},{8,12},{9,13},{10,... | collective-permute-start | bytes 1572872 | tf_op jit(solution)/shard_map/ppermute | solution.py:445
  567.9 19.3 %collective-permute-start.100 = (bf16[256,768]{0,1:T(8,128)(2,1)}, bf16[256,768]{0,1:T(8,128)(2,1)S(1)}, u32[]{:S(2)}, u32[]{:S(2)}) collective-permute-start(bf16[256,768]{0,1:T(8,128)(2,1)} %pad_maximum_fusion.35), channel_id=1, source_target_pairs={{0,8},{8,16},{16,24},{24,0},{1,9},{9,17},{17,25},{25,1},{2,10},{10... | collective-permute-start | bytes 1179656 | tf_op jit(solution)/shard_map/ppermute | solution.py:441
  576.5 134.5 %reduce-scatter.17.cloned.1.call-start = ((), (), s32[]{:S(2)}) async-start(), calls=%async_computation.14 | async-start | bytes 1310720 | tf_op jit(solution)/shard_map/reduce_scatter | solution.py:566
  579.5 18.1 %collective-permute-start.103 = (bf16[128,768]{0,1:T(8,128)(2,1)S(1)}, bf16[128,768]{0,1:T(8,128)(2,1)S(1)}, u32[]{:S(2)}, u32[]{:S(2)}) collective-permute-start(bf16[128,768]{0,1:T(8,128)(2,1)S(1)} %slice.1077), channel_id=1, source_target_pairs={{0,24},{8,0},{16,8},{24,16},{1,25},{9,1},{17,9},{25,17},{2,26},{10... | collective-permute-start | bytes 589832 | tf_op jit(solution)/shard_map/ppermute | solution.py:441
  621.3 19.5 %collective-permute-start.104 = (bf16[256,2048]{1,0:T(8,128)(2,1)S(1)}, bf16[256,2048]{1,0:T(8,128)(2,1)S(1)}, u32[]{:S(2)}, u32[]{:S(2)}) collective-permute-start(bf16[256,2048]{1,0:T(8,128)(2,1)S(1)} %broadcast_select_fusion.4), channel_id=1, source_target_pairs={{0,1},{1,0},{2,3},{3,2},{4,5},{5,4},{6,7},{7,6},{8,9},{9,8},{10,11... | collective-permute-start | bytes 3145736 | tf_op jit(solution)/shard_map/ppermute | solution.py:445
  621.9 22.4 %collective-permute-start.76 = (bf16[128,2048]{1,0:T(8,128)(2,1)S(1)}, bf16[128,2048]{1,0:T(8,128)(2,1)S(1)}, u32[]{:S(2)}, u32[]{:S(2)}) collective-permute-start(bf16[128,2048]{1,0:T(8,128)(2,1)S(1)} %get-tuple-element.227), channel_id=1, source_target_pairs={{0,1},{1,0},{2,3},{3,2},{4,5},{5,4},{6,7},{7,6},{8,9},{9,8},{10,11... | collective-permute-start | bytes 1572872 | tf_op jit(solution)/shard_map/ppermute | solution.py:445
  624.1 16.4 %collective-permute-start.79 = (bf16[64,2048]{1,0:T(8,128)(2,1)S(1)}, bf16[64,2048]{1,0:T(8,128)(2,1)S(1)}, u32[]{:S(2)}, u32[]{:S(2)}) collective-permute-start(bf16[64,2048]{1,0:T(8,128)(2,1)S(1)} %get-tuple-element.323), channel_id=1, source_target_pairs={{0,8},{8,16},{16,24},{24,0},{1,9},{9,17},{17,25},{25,1},{2,10},{10... | collective-permute-start | bytes 786440 | tf_op jit(solution)/shard_map/ppermute | solution.py:441
  640.6 23.9 %collective-permute-start.80 = (bf16[128,2048]{1,0:T(8,128)(2,1)S(1)}, bf16[128,2048]{1,0:T(8,128)(2,1)S(1)}, u32[]{:S(2)}, u32[]{:S(2)}) collective-permute-start(bf16[128,2048]{1,0:T(8,128)(2,1)S(1)} %pad_maximum_fusion.29), channel_id=1, source_target_pairs={{0,8},{8,16},{16,24},{24,0},{1,9},{9,17},{17,25},{25,1},{2,10},{10... | collective-permute-start | bytes 1572872 | tf_op jit(solution)/shard_map/ppermute | solution.py:441
  (270 other events, 3154.5 us)
Sparse Core Ops, SparseCore 0:
  12.8 46.5 all-gather.3
  61.9 32.3 all-gather.5
  96.2 123.0 all-gather.7
  308.8 45.7 reduce-scatter.6
  369.5 56.6 reduce-scatter.8
  429.2 86.3 reduce-scatter.10
  519.4 31.0 reduce-scatter.12
  576.6 28.4 reduce-scatter.14
  618.2 25.8 reduce-scatter.16

commit v3 on v2

--- a/solution.py
+++ b/solution.py
@@ -449,16 +449,19 @@
     return across_blk(x, 1)
 
 
-def gather_chip(x):
+def gather_chip(x, *others):
     half = x.shape[0] // 2
     before = along_heads(x, 1)
     after = along_heads(x, -1)
+    if others:
+        before, after, *others = together(before, after, *others)
     far = jnp.concatenate([along_heads(before[:half], 1), along_heads(after[half:], -1)], axis=0)
     own = [before, x, after, far]
-    return jnp.concatenate(own + [other_core(part) for part in own], axis=0)
-
-
-def scatter_chip(y):
+    rows = jnp.concatenate(own + [other_core(part) for part in own], axis=0)
+    return (rows, *others) if others else rows
+
+
+def scatter_chip(y, *others):
     wide = jnp.float32
     n = y.shape[0] // 8
     half = n // 2
@@ -471,22 +474,19 @@
     second = along_heads(far[half:], -1).astype(wide)
     after = jnp.concatenate([after[:half] + first, after[half:]], axis=0).astype(jnp.bfloat16)
     before = jnp.concatenate([before[:half], before[half:] + second], axis=0).astype(jnp.bfloat16)
-    return own + along_heads(after, 1).astype(wide) + along_heads(before, -1).astype(wide)
-
-
-def in_line(parts):
-    line = lax.axis_index("heads")
-    rows = parts[0].shape[0]
-    turned = turn(jnp.concatenate(parts, axis=0), (1 - line) % LINE)
-    return [turned[k * rows : (k + 1) * rows] for k in range(LINE)]
-
-
-def gather_line(x):
+    if others:
+        after, before, *others = together(after, before, *others)
+    total = own + along_heads(after, 1).astype(wide) + along_heads(before, -1).astype(wide)
+    return (total, *others) if others else total
+
+
+def line_neighbours(x):
+    return along_heads(x, 1), along_heads(x, -1)
+
+
+def line_far(x, before, after):
     half = x.shape[0] // 2
-    before = along_heads(x, 1)
-    after_ = along_heads(x, -1)
-    far = jnp.concatenate([along_heads(before[:half], 1), along_heads(after_[half:], -1)], axis=0)
-    return in_line([before, x, after_, far])
+    return along_heads(before[:half], 1), along_heads(after[half:], -1)
 
 
 def share_line(x):
@@ -616,6 +616,71 @@
     return lax.dot_general(
         left, right, (((0,), (0,)), ((), ())), preferred_element_type=jnp.float32
     )
+
+
+def arrival_rows(meta, block, rows):
+    place = lax.rem(block % LINE - meta[2] + 1 + LINE, LINE)
+    place = place + jnp.where(meta[1] == block // LINE, 0, LINE)
+    return pl.ds(pl.multiple_of(place * rows, rows), rows)
+
+
+def head_forward(x, gain, cosine, sine):
+    normed = x * lax.rsqrt(jnp.mean(x * x, axis=-1, keepdims=True) + epsilon) * gain
+    half = x.shape[-1] // 2
+    low, high = normed[:, :half], normed[:, half:]
+    return jnp.concatenate([low * cosine - high * sine, high * cosine + low * sine], axis=-1)
+
+
+def head_backward(x, grad, gain, cosine, sine):
+    half = x.shape[-1] // 2
+    low, high = grad[:, :half], grad[:, half:]
+    turned = jnp.concatenate([low * cosine + high * sine, high * cosine - low * sine], axis=-1)
+    scale = lax.rsqrt(jnp.mean(x * x, axis=-1, keepdims=True) + epsilon)
+    normed = x * scale
+    inner = turned * gain
+    x_grad = scale * (inner - normed * jnp.mean(inner * normed, axis=-1, keepdims=True))
+    return x_grad, jnp.sum(turned * normed, axis=0, keepdims=True)
+
+
+def kv_tables(meta, gain, cosine, sine):
+    is_key = meta[1] == 0
+    return jnp.where(is_key, gain, 1.0), jnp.where(is_key, cosine, 1.0), jnp.where(is_key, sine, 0.0)
+
+
+def heads_kernel(meta, x_ref, w_ref, cosine_ref, sine_ref, gain_ref, q_ref, kv_ref, pre_ref, total):
+    own, width = q_ref.shape
+    depth = w_ref.shape[0]
+    for half in range(CORES):
+        rows = pl.ds(half * (own // CORES), own // CORES)
+        total[rows, :] = jnp.dot(
+            x_ref[rows, :depth], w_ref[:, : 2 * width], preferred_element_type=jnp.float32
+        )
+    size = own // (CORES * LINE)
+    for block in range(CORES * LINE):
+        rows = pl.ds(block * size, size)
+        pre = total[arrival_rows(meta, block, size), :]
+        pre_ref[rows, :] = pre
+        cosine, sine = cosine_ref[rows, :], sine_ref[rows, :]
+        q_ref[rows, :] = head_forward(pre[:, :width], gain_ref[0:1, :], cosine, sine).astype(q_ref.dtype)
+        kv_ref[rows, :] = head_forward(
+            pre[:, width:], *kv_tables(meta, gain_ref[1:2, :], cosine, sine)
+        ).astype(kv_ref.dtype)
+
+
+def kv_back_kernel(meta, pre_ref, grad_ref, cosine_ref, sine_ref, gain_ref, out_ref, gain_grad_ref):
+    own, width = grad_ref.shape
+    size = own // (CORES * LINE)
+    total = jnp.zeros((1, width), jnp.float32)
+    for block in range(CORES * LINE):
+        rows = pl.ds(block * size, size)
+        x_grad, gain_grad = head_backward(
+            pre_ref[rows, width:],
+            grad_ref[rows, :],
+            *kv_tables(meta, gain_ref[1:2, :], cosine_ref[rows, :], sine_ref[rows, :]),
+        )
+        out_ref[arrival_rows(meta, block, size), :] = x_grad.astype(out_ref.dtype)
+        total = total + gain_grad
+    gain_grad_ref[...] = jnp.where(meta[1] == 0, total, 0.0)
 
 
 def attend_kernel(meta, q_ref, lo_ref, *refs):
@@ -645,7 +710,7 @@
                 preferred_element_type=jnp.float32,
             )
 
-        start, full_from = meta[2 + 2 * part], meta[3 + 2 * part]
+        start, full_from = meta[3 + 2 * part], meta[4 + 2 * part]
         end = (first + QUERY_ROWS - 1) // KEY_ROWS + 1
         full_from = jnp.minimum(full_from, end)
         full_to = jnp.maximum(jnp.minimum((first + 1) // KEY_ROWS, end), full_from)
@@ -667,9 +732,11 @@
         lse_ref[rows, :] = jnp.log(denominator)
 
 
-def attend_back_kernel(meta, q_ref, grad_ref, lse_ref, delta_ref, lo_ref, *refs):
+def attend_back_kernel(
+    meta, q_ref, grad_ref, lse_ref, delta_ref, lo_ref, pre_ref, cosine_ref, sine_ref, gain_ref, *refs
+):
     mine, theirs = refs[:5], refs[5:10]
-    dq_ref, keep_ref, send_ref, k_all, v_all, dk_sum, dv_sum = refs[10:]
+    out_ref, gain_grad_ref, keep_ref, send_ref, k_all, v_all, dk_sum, dv_sum, dq_ref = refs[10:]
     place_both(meta, mine, theirs, k_all, v_all)
     chip = meta[0]
     own = q_ref.shape[0]
@@ -679,7 +746,7 @@
     dq_ref[...] = jnp.zeros_like(dq_ref)
     per_chip = own // KEY_ROWS
 
-    @pl.loop(meta[2], (chip + 1) * per_chip)
+    @pl.loop(meta[3], (chip + 1) * per_chip)
     def _(block):
         at = pl.multiple_of(block * KEY_ROWS, KEY_ROWS)
         dk_sum[...] = jnp.zeros_like(dk_sum)
@@ -705,7 +772,7 @@
                 dk_sum[...] += jnp.dot(score_grad, queries, preferred_element_type=jnp.float32)
                 dq_ref[rows, :] += columns_times_columns(score_grad, keys)
 
-            start, full_from = meta[2 + 2 * part], meta[3 + 2 * part]
+            start, full_from = meta[3 + 2 * part], meta[4 + 2 * part]
             full = (block >= full_from) & ((block + 1) * KEY_ROWS <= first + 1)
             needed = (block >= start) & (block * KEY_ROWS < first + QUERY_ROWS)
 
@@ -731,6 +798,28 @@
         def _():
             keep_ref[place, pl.ds(inner, KEY_ROWS), :] = dv_low
             send_ref[place, pl.ds(inner, KEY_ROWS), :] = dk_low
+
+    width = q_ref.shape[1]
+    size = own // (CORES * LINE)
+    total = jnp.zeros((1, width), jnp.float32)
+    for block in range(CORES * LINE):
+        rows = pl.ds(block * size, size)
+        x_grad, gain_grad = head_backward(
+            pre_ref[rows, :width],
+            dq_ref[rows, :].astype(jnp.bfloat16).astype(jnp.float32),
+            gain_ref[0:1, :],
+            cosine_ref[rows, :],
+            sine_ref[rows, :],
+        )
+        out_ref[arrival_rows(meta, block, size), :] = x_grad.astype(out_ref.dtype)
+        total = total + gain_grad
+    gain_grad_ref[...] = total
+
+
+def takes(microseconds):
+    return pl.CostEstimate(
+        flops=int(microseconds * 1e9), bytes_accessed=int(microseconds * 3.3e6), transcendentals=0
+    )
 
 
 def in_vmem(count):
@@ -755,68 +844,481 @@
             pltpu.VMEM((QUERY_ROWS, width), jnp.float32),
         ],
         compiler_params=pltpu.CompilerParams(vmem_limit_bytes=40 << 20),
-        cost_estimate=pl.CostEstimate(
-            flops=2 * own * row * width, bytes_accessed=6 * row * width, transcendentals=own * row // 2
-        ),
+        cost_estimate=takes(11),
     )(meta, q, lo.reshape(own, 1), *mine, *theirs)
 
 
-def attend_back_here(meta, q, grad, lse, delta, lo, mine, theirs):
+def attend_back_here(meta, q, grad, lse, delta, lo, tables, mine, theirs):
     own, width = q.shape
     row = own * CHIPS
     return pl.pallas_call(
         attend_back_kernel,
         out_shape=(
-            jax.ShapeDtypeStruct((own, width), jnp.float32),
+            jax.ShapeDtypeStruct((own, width), jnp.bfloat16),
+            jax.ShapeDtypeStruct((1, width), jnp.float32),
             jax.ShapeDtypeStruct((CHIPS, own, width), jnp.bfloat16),
             jax.ShapeDtypeStruct((CHIPS, own, width), jnp.bfloat16),
         ),
-        in_specs=[pl.BlockSpec(memory_space=pltpu.SMEM)] + in_vmem(15),
-        out_specs=tuple(in_vmem(3)),
+        in_specs=[pl.BlockSpec(memory_space=pltpu.SMEM)] + in_vmem(19),
+        out_specs=tuple(in_vmem(4)),
         scratch_shapes=[
             pltpu.VMEM((row, width), jnp.bfloat16),
             pltpu.VMEM((row, width), jnp.bfloat16),
             pltpu.VMEM((KEY_ROWS, width), jnp.float32),
             pltpu.VMEM((KEY_ROWS, width), jnp.float32),
+            pltpu.VMEM((own, width), jnp.float32),
         ],
         compiler_params=pltpu.CompilerParams(vmem_limit_bytes=48 << 20),
-        cost_estimate=pl.CostEstimate(
-            flops=5 * own * row * width, bytes_accessed=12 * row * width, transcendentals=own * row // 2
+        cost_estimate=takes(20.5),
+    )(
+        meta,
+        q,
+        grad,
+        lse.reshape(1, own),
+        delta.reshape(1, own),
+        lo.reshape(1, own),
+        *tables,
+        *mine,
+        *theirs,
+    )
+
+
+def heads_here(meta, x, weights, cosine, sine, gains):
+    own, width = x.shape[0], gains.shape[1]
+    return pl.pallas_call(
+        heads_kernel,
+        out_shape=(
+            jax.ShapeDtypeStruct((own, width), jnp.bfloat16),
+            jax.ShapeDtypeStruct((own, width), jnp.bfloat16),
+            jax.ShapeDtypeStruct((own, 2 * width), jnp.float32),
         ),
-    )(
-        meta, q, grad, lse.reshape(1, own), delta.reshape(1, own), lo.reshape(1, own), *mine, *theirs
-    )
-
-
-def predict_list(versions, gain_rows, router, coefficients):
-    table = jnp.dot(
-        modes(versions[0], gain_rows[0], router), coefficients[:, :16], precision=highest
-    )
-    predicted = []
+        in_specs=[pl.BlockSpec(memory_space=pltpu.SMEM)] + in_vmem(5),
+        out_specs=tuple(in_vmem(3)),
+        scratch_shapes=[pltpu.VMEM((own, 2 * width), jnp.float32)],
+        compiler_params=pltpu.CompilerParams(vmem_limit_bytes=48 << 20),
+        cost_estimate=takes(7),
+    )(meta, x, weights, cosine, sine, gains)
+
+
+def kv_back_here(meta, grad, tables):
+    own, width = grad.shape
+    pre, *others = tables
+    return pl.pallas_call(
+        kv_back_kernel,
+        out_shape=(
+            jax.ShapeDtypeStruct((own, width), jnp.bfloat16),
+            jax.ShapeDtypeStruct((1, width), jnp.float32),
+        ),
+        in_specs=[pl.BlockSpec(memory_space=pltpu.SMEM)] + in_vmem(5),
+        out_specs=tuple(in_vmem(2)),
+        compiler_params=pltpu.CompilerParams(vmem_limit_bytes=32 << 20),
+        cost_estimate=takes(1.5),
+    )(meta, pre, grad, *others)
+
+
+TOKEN_ROWS = 16
+COMBINE_TIME = 25
+
+
+def scaled(x):
+    return x * lax.rsqrt(jnp.mean(x * x, axis=-1, keepdims=True) + epsilon)
+
+
+def scaled_back(x, grad):
+    scale = lax.rsqrt(jnp.mean(x * x, axis=-1, keepdims=True) + epsilon)
+    normed = x * scale
+    return scale * (grad - normed * jnp.mean(grad * normed, axis=-1, keepdims=True))
+
+
+def inner(left, right):
+    return jnp.sum(left * right, axis=-1, keepdims=True)
+
+
+def over_rows(x):
+    return jnp.sum(x, axis=0, keepdims=True)
+
+
+def mode_columns(aligned, router_ref):
+    return [jnp.tanh(inner(aligned, router_ref[k : k + 1, :])) for k in range(4)]
+
+
+def mixed_columns(mode, coef, column):
+    return sum(mode[k] * coef[k, column] for k in range(4))
+
+
+def predict_kernel(coef, x_ref, gain_ref, router_ref, predicted_ref, normed_ref):
+    x = [x_ref[i].astype(jnp.float32) for i in range(4)]
+    mode = mode_columns(scaled(x[0]) * gain_ref[0:1, :], router_ref)
     for i in range(4):
-        value = versions[i]
+        value = x[i]
         for j in range(4):
-            value = value + table[:, 4 * i + j : 4 * i + j + 1] * versions[j]
-        predicted.append(value)
-    return (tuple(predicted), rms_norm_apply(predicted[0], gain_rows[1]))
-
-
-def correct_list(merged, fed, predicted, gain_rows, router, coefficients):
-    activated = merged + rms_norm_apply(fed, gain_rows[5])
-    scale = (
-        jnp.dot(modes(activated, gain_rows[0], router), coefficients[:, 16:], precision=highest)
-        + 1.0
-    )
-    change = activated - predicted[0]
-    corrected = tuple(predicted[i] + scale[:, i : i + 1] * change for i in range(4))
-    return (corrected, corrected[0] * gain_rows[6])
-
-
-def head_apply(x, gain, cosine, sine):
-    normed = x * lax.rsqrt(jnp.mean(x * x, axis=-1, keepdims=True) + epsilon) * gain
-    half = x.shape[-1] // 2
-    turned = jnp.concatenate([-normed[:, half:], normed[:, :half]], axis=-1)
-    return normed * cosine + turned * sine
+            value = value + mixed_columns(mode, coef, 4 * i + j) * x[j]
+        predicted_ref[i] = value
+        if i == 0:
+            normed_ref[...] = (scaled(value) * gain_ref[1:2, :]).astype(normed_ref.dtype)
+
+
+def predict_back_kernel(
+    coef, x_ref, first_ref, cotangent_ref, normed_ref, extra_ref, gain_ref, router_ref, early_ref,
+    out_ref, packed_ref, mode_all, table_all,
+):
+    step = pl.program_id(0)
+
+    @pl.when(step == 0)
+    def _():
+        packed_ref[...] = early_ref[...]
+        mode_all[...] = jnp.zeros_like(mode_all)
+        table_all[...] = jnp.zeros_like(table_all)
+
+    rows = pl.ds(pl.multiple_of(step * TOKEN_ROWS, TOKEN_ROWS), TOKEN_ROWS)
+    x = [x_ref[i].astype(jnp.float32) for i in range(4)]
+    normed_zero = scaled(x[0])
+    aligned = normed_zero * gain_ref[0:1, :]
+    mode = mode_columns(aligned, router_ref)
+    table = [[mixed_columns(mode, coef, 4 * i + j) for j in range(4)] for i in range(4)]
+    predicted = x[0] + sum(table[0][j] * x[j] for j in range(4))
+    normed_grad = normed_ref[...] + extra_ref[...]
+    packed_ref[1:2, :] += over_rows(normed_grad * scaled(predicted))
+    grads = [first_ref[...] + scaled_back(predicted, normed_grad * gain_ref[1:2, :])]
+    grads += [cotangent_ref[i].astype(jnp.float32) for i in (1, 2, 3)]
+    mode_grad = [0.0] * 4
+    for i in range(4):
+        for j in range(4):
+            table_grad = inner(grads[i], x[j])
+            table_all[rows, 4 * i + j : 4 * i + j + 1] = table_grad
+            for k in range(4):
+                mode_grad[k] = mode_grad[k] + table_grad * coef[k, 4 * i + j]
+    aligned_grad = 0.0
+    for k in range(4):
+        mode_all[rows, k : k + 1] = mode[k]
+        logit_grad = mode_grad[k] * (1.0 - mode[k] * mode[k])
+        aligned_grad = aligned_grad + logit_grad * router_ref[k : k + 1, :]
+        packed_ref[8 + k : 9 + k, :] += over_rows(logit_grad * aligned)
+    packed_ref[0:1, :] += over_rows(aligned_grad * normed_zero)
+    for j in range(4):
+        value = grads[j] + sum(table[i][j] * grads[i] for i in range(4))
+        if j == 0:
+            value = value + scaled_back(x[0], aligned_grad * gain_ref[0:1, :])
+        out_ref[j] = value.astype(out_ref.dtype)
+
+    @pl.when(step == pl.num_programs(0) - 1)
+    def _():
+        products = lax.dot_general(
+            mode_all[...],
+            table_all[...],
+            (((0,), (0,)), ((), ())),
+            precision=highest,
+            preferred_element_type=jnp.float32,
+        )
+        packed_ref[12:16, 0:128] += products[0:4, :]
+
+
+def gelu_parts(x):
+    slope = (2.0 / jnp.pi) ** 0.5
+    bend = jnp.tanh(slope * (x + 0.044715 * x * x * x))
+    value = 0.5 * x * (1.0 + bend)
+    derivative = 0.5 * (1.0 + bend) + 0.5 * x * (1.0 - bend * bend) * slope * (
+        1.0 + 3.0 * 0.044715 * x * x
+    )
+    return value, derivative
+
+
+def middle_kernel(
+    coef, merged_ref, fed_ref, predicted_ref, cotangent_ref, input_ref, gain_ref, router_ref, weight_ref,
+    result_ref, layer_grad_ref, fed_grad_ref, merged_grad_ref, first_grad_ref, packed_ref,
+    first_ref, gate_pre_ref, projected_ref, gated_ref,
+    active, wide_rows, mode_all, scale_grads,
+):
+    tokens, width = merged_ref.shape
+    small = input_ref.shape[1]
+    ranks = weight_ref.shape[1] - 2 * small
+    gate_columns = pl.ds(ranks, small)
+    projection_columns = pl.ds(ranks + small, small)
+    packed_ref[...] = jnp.zeros_like(packed_ref)
+    mode_all[...] = jnp.zeros_like(mode_all)
+    scale_grads[...] = jnp.zeros_like(scale_grads)
+
+    def scales(value):
+        normed = scaled(value)
+        aligned = normed * gain_ref[0:1, :]
+        mode = mode_columns(aligned, router_ref)
+        return normed, aligned, mode, [mixed_columns(mode, coef, 16 + i) + 1.0 for i in range(4)]
+
+    @pl.loop(0, tokens // TOKEN_ROWS)
+    def _(step):
+        rows = pl.ds(pl.multiple_of(step * TOKEN_ROWS, TOKEN_ROWS), TOKEN_ROWS)
+        value = merged_ref[rows, :] + scaled(fed_ref[rows, :]) * gain_ref[5:6, :]
+        active[rows, :] = value
+        _, _, _, scale = scales(value)
+        start = predicted_ref[0, rows, :]
+        corrected = start + scale[0] * (value - start)
+        first_ref[rows, :] = (corrected * gain_ref[6:7, :]).astype(first_ref.dtype)
+
+    gate_pre = jnp.dot(first_ref[...], weight_ref[:, gate_columns], preferred_element_type=jnp.float32)
+    gelu, slope = gelu_parts(gate_pre)
+    layer_input = input_ref[...].astype(jnp.float32)
+    gated_ref[...] = (gelu * layer_input).astype(gated_ref.dtype)
+    wide_rows[...] = rows_times_rows(gated_ref[...], weight_ref[:, projection_columns])
+
+    @pl.loop(0, tokens // TOKEN_ROWS)
+    def _(step):
+        rows = pl.ds(pl.multiple_of(step * TOKEN_ROWS, TOKEN_ROWS), TOKEN_ROWS)
+        projected = wide_rows[rows, :]
+        normed = scaled(projected)
+        extra = normed * gain_ref[7:8, :]
+        value = active[rows, :]
+        _, _, _, scale = scales(value)
+        change = value - predicted_ref[0, rows, :]
+        extra_grad = 0.0
+        for i in range(4):
+            corrected = predicted_ref[i, rows, :] + scale[i] * change
+            if i:
+                corrected = corrected + extra
+                extra_grad = extra_grad + cotangent_ref[i, rows, :].astype(jnp.float32)
+            result_ref[i, rows, :] = corrected.astype(result_ref.dtype)
+        packed_ref[7:8, :] += over_rows(extra_grad * normed)
+        projected_ref[rows, :] = scaled_back(projected, extra_grad * gain_ref[7:8, :]).astype(
+            projected_ref.dtype
+        )
+
+    gated_grad = jnp.dot(
+        projected_ref[...], weight_ref[:, projection_columns], preferred_element_type=jnp.float32
+    )
+    layer_grad_ref[...] = (gated_grad * gelu).astype(layer_grad_ref.dtype)
+    gate_pre_ref[...] = (gated_grad * layer_input * slope).astype(gate_pre_ref.dtype)
+    wide_rows[...] = rows_times_rows(gate_pre_ref[...], weight_ref[:, gate_columns])
+
+    @pl.loop(0, tokens // TOKEN_ROWS)
+    def _(step):
+        rows = pl.ds(pl.multiple_of(step * TOKEN_ROWS, TOKEN_ROWS), TOKEN_ROWS)
+        value = active[rows, :]
+        normed, aligned, mode, scale = scales(value)
+        start = predicted_ref[0, rows, :]
+        change = value - start
+        first_grad = wide_rows[rows, :]
+        packed_ref[6:7, :] += over_rows(first_grad * (start + scale[0] * change))
+        grads = [cotangent_ref[i, rows, :].astype(jnp.float32) for i in range(4)]
+        grads[0] = grads[0] + first_grad * gain_ref[6:7, :]
+        change_grad = sum(scale[i] * grads[i] for i in range(4))
+        mode_grad = [0.0] * 4
+        for i in range(4):
+            scale_grad = inner(grads[i], change)
+            scale_grads[rows, 16 + i : 17 + i] = scale_grad
+            for k in range(4):
+                mode_grad[k] = mode_grad[k] + scale_grad * coef[k, 16 + i]
+        aligned_grad = 0.0
+        for k in range(4):
+            mode_all[rows, k : k + 1] = mode[k]
+            logit_grad = mode_grad[k] * (1.0 - mode[k] * mode[k])
+            aligned_grad = aligned_grad + logit_grad * router_ref[k : k + 1, :]
+            packed_ref[8 + k : 9 + k, :] += over_rows(logit_grad * aligned)
+        packed_ref[0:1, :] += over_rows(aligned_grad * normed)
+        active_grad = change_grad + scaled_back(value, aligned_grad * gain_ref[0:1, :])
+        first_grad_ref[rows, :] = grads[0] - change_grad
+        merged_grad_ref[rows, :] = active_grad
+        fed = fed_ref[rows, :]
+        packed_ref[5:6, :] += over_rows(active_grad * scaled(fed))
+        fed_grad_ref[rows, :] = scaled_back(fed, active_grad * gain_ref[5:6, :]).astype(
+            fed_grad_ref.dtype
+        )
+
+    products = lax.dot_general(
+        mode_all[...],
+        scale_grads[...],
+        (((0,), (0,)), ((), ())),
+        precision=highest,
+        preferred_element_type=jnp.float32,
+    )
+    packed_ref[12:16, 0:128] += products[0:4, :]
+
+
+def combine_back_kernel(
+    merged_ref, attention_ref, lifted_ref, merged_grad_ref, feed_ref, first_ref, gain_ref, early_ref,
+    total_ref, active_ref, attention_grad_ref, lifted_grad_ref, packed_ref,
+):
+    @pl.when(pl.program_id(0) == 0)
+    def _():
+        packed_ref[...] = early_ref[...]
+
+    merged, feed_grad = merged_ref[...], feed_ref[...]
+    packed_ref[4:5, :] += over_rows(feed_grad * scaled(merged))
+    grad = (merged_grad_ref[...] + scaled_back(merged, feed_grad * gain_ref[4:5, :])) * root_half
+    active_ref[...] = grad
+    total_ref[...] = first_ref[...] + grad
+    for value_ref, row, out_ref in ((attention_ref, 2, attention_grad_ref), (lifted_ref, 3, lifted_grad_ref)):
+        value = value_ref[...]
+        packed_ref[row : row + 1, :] += over_rows(grad * scaled(value))
+        out_ref[...] = scaled_back(value, grad * gain_ref[row : row + 1, :]).astype(out_ref.dtype)
+
+
+def combine_back_here(merged, attention, lifted, merged_grad, feed_grad, first, gains, early):
+    tokens, width = merged.shape
+    rows = token_rows(width)
+    full = jax.ShapeDtypeStruct((tokens, width), jnp.float32)
+    low = jax.ShapeDtypeStruct((tokens, width), jnp.bfloat16)
+    return pl.pallas_call(
+        combine_back_kernel,
+        grid=(tokens // TOKEN_ROWS,),
+        out_shape=(full, full, low, low, jax.ShapeDtypeStruct(early.shape, jnp.float32)),
+        in_specs=[rows] * 6 + [whole(gains.shape), whole(early.shape)],
+        out_specs=(rows, rows, rows, rows, whole(early.shape)),
+        compiler_params=pltpu.CompilerParams(vmem_limit_bytes=32 << 20),
+        cost_estimate=takes(COMBINE_TIME),
+    )(merged, attention, lifted, merged_grad, feed_grad, first, gains, early)
+
+
+def assemble_kernel(meta, *refs):
+    query, kv, out = refs[:5], refs[5:10], refs[10:15]
+    query_ref, out_ref, key_ref, value_ref, laurel_ref, io_ref = refs[15:]
+    rows = key_ref.shape[0]
+    pair = query[0].shape[1]
+    head = pair // CORES
+    part = io_ref.shape[0] // LINE
+    key_ref[...] = jnp.zeros_like(key_ref)
+    value_ref[...] = jnp.zeros_like(value_ref)
+    laurel_ref[...] = jnp.zeros_like(laurel_ref)
+
+    def put(sender, query_part, kv_part, to):
+        columns = pl.ds(pl.multiple_of(sender * pair, pair), pair)
+        query_ref[to, columns] = query_part.astype(jnp.float32)
+        group = pl.ds(pl.multiple_of(sender // (LINE // KEY_VALUE_HEADS) * head, head), head)
+        key_ref[to, group] += kv_part[:, :head].astype(jnp.float32)
+        value_ref[to, group] += kv_part[:, head:].astype(jnp.float32)
+
+    def put_out(sender, value, at):
+        columns = pl.ds(pl.multiple_of(sender * pair, pair), pair)
+        count = min(rows - at, value.shape[0])
+        to = pl.ds(at, count)
+        out_ref[to, columns] = value[:count, :pair].astype(jnp.float32)
+        laurel_ref[to, :] += value[:count, pair:].astype(jnp.float32)
+        if value.shape[0] > count:
+            start = pl.multiple_of(sender * part, part)
+            io_ref[pl.ds(start, part), :] = value[count:, : io_ref.shape[1]].astype(jnp.float32)
+
+    for step, place in ((0, 0), (-1, 1), (1, 2)):
+        sender = lax.rem(meta[2] + step + LINE, LINE)
+        put(sender, query[place][...], kv[place][...], pl.ds(0, rows))
+        put_out(sender, out[place][...], 0)
+    sender = lax.rem(meta[2] + 2, LINE)
+    put(sender, query[3][...], kv[3][...], pl.ds(0, rows // 2))
+    put(sender, query[4][...], kv[4][...], pl.ds(rows // 2, rows // 2))
+    put_out(sender, out[3][...], 0)
+    put_out(sender, out[4][...], out[3].shape[0])
+
+
+def assemble_here(meta, query, kv, out):
+    rows, pair = query[0].shape
+    small = 2 * LAYER_INPUT_SIZE
+    shapes = (
+        (rows, LINE * pair),
+        (rows, LINE * pair),
+        (rows, KEY_VALUE_HEADS * HEAD_WIDTH),
+        (rows, KEY_VALUE_HEADS * HEAD_WIDTH),
+        (rows, 2 * LAUREL_RANK),
+        (rows, small),
+    )
+    return pl.pallas_call(
+        assemble_kernel,
+        out_shape=tuple(jax.ShapeDtypeStruct(shape, jnp.float32) for shape in shapes),
+        in_specs=[in_smem()] + in_vmem(15),
+        out_specs=tuple(in_vmem(len(shapes))),
+        compiler_params=pltpu.CompilerParams(vmem_limit_bytes=32 << 20),
+        cost_estimate=takes(4),
+    )(meta, *query, *kv, *out)
+
+
+def in_smem():
+    return pl.BlockSpec(memory_space=pltpu.SMEM)
+
+
+def token_block(count, width):
+    return pl.BlockSpec((count, TOKEN_ROWS, width), lambda i: (0, i, 0))
+
+
+def token_rows(width):
+    return pl.BlockSpec((TOKEN_ROWS, width), lambda i: (i, 0))
+
+
+def whole(shape):
+    return pl.BlockSpec(shape, lambda i: (0,) * len(shape))
+
+
+def predict_here(versions, gains, router, coef):
+    tokens, width = versions.shape[1:]
+    return pl.pallas_call(
+        predict_kernel,
+        grid=(tokens // TOKEN_ROWS,),
+        out_shape=(
+            jax.ShapeDtypeStruct(versions.shape, jnp.float32),
+            jax.ShapeDtypeStruct((tokens, width), jnp.bfloat16),
+        ),
+        in_specs=[in_smem(), token_block(4, width), whole(gains.shape), whole(router.shape)],
+        out_specs=(token_block(4, width), token_rows(width)),
+        compiler_params=pltpu.CompilerParams(vmem_limit_bytes=32 << 20),
+        cost_estimate=takes(4.5),
+    )(coef, versions, gains, router)
+
+
+def predict_back_here(versions, first, cotangent, normed, extra, gains, router, coef, early):
+    tokens, width = first.shape
+    return pl.pallas_call(
+        predict_back_kernel,
+        grid=(tokens // TOKEN_ROWS,),
+        out_shape=(
+            jax.ShapeDtypeStruct(versions.shape, jnp.bfloat16),
+            jax.ShapeDtypeStruct(early.shape, jnp.float32),
+        ),
+        in_specs=[
+            in_smem(),
+            token_block(4, width),
+            token_rows(width),
+            token_block(4, width),
+            token_rows(width),
+            token_rows(width),
+            whole(gains.shape),
+            whole(router.shape),
+            whole(early.shape),
+        ],
+        out_specs=(token_block(4, width), whole(early.shape)),
+        scratch_shapes=[
+            pltpu.VMEM((tokens, 128), jnp.float32),
+            pltpu.VMEM((tokens, 128), jnp.float32),
+        ],
+        compiler_params=pltpu.CompilerParams(vmem_limit_bytes=32 << 20),
+        cost_estimate=takes(10),
+    )(coef, versions, first, cotangent, normed, extra, gains, router, early)
+
+
+def middle_here(merged, fed, predicted, cotangent, layer_input, gains, router, coef, weights):
+    tokens, width = merged.shape
+    small = layer_input.shape[1]
+    narrow, wide = jnp.bfloat16, jnp.float32
+    shapes = (
+        (predicted.shape, narrow),
+        ((tokens, small), narrow),
+        ((tokens, width), narrow),
+        ((tokens, width), wide),
+        ((tokens, width), wide),
+        ((16, width), wide),
+        ((tokens, width), narrow),
+        ((tokens, small), narrow),
+        ((tokens, width), narrow),
+        ((tokens, small), narrow),
+    )
+    return pl.pallas_call(
+        middle_kernel,
+        out_shape=tuple(jax.ShapeDtypeStruct(*shape) for shape in shapes),
+        in_specs=[in_smem()] + in_vmem(8),
+        out_specs=tuple(in_vmem(len(shapes))),
+        scratch_shapes=[
+            pltpu.VMEM((tokens, width), wide),
+            pltpu.VMEM((tokens, width), wide),
+            pltpu.VMEM((tokens, 128), wide),
+            pltpu.VMEM((tokens, 128), wide),
+        ],
+        compiler_params=pltpu.CompilerParams(vmem_limit_bytes=48 << 20),
+        cost_estimate=takes(17),
+    )(coef, merged, fed, predicted, cotangent, layer_input, gains, router, weights)
 
 
 def chip_device(
@@ -880,20 +1382,11 @@
     query_kv_full = head_full[:, : 2 * HEAD_WIDTH]
     out_full = head_full[:, 2 * HEAD_WIDTH :]
     laurel_full = small_full[:, : 2 * LAUREL_RANK]
-    gate_full = small_full[:, 2 * LAUREL_RANK : 2 * LAUREL_RANK + LAYER_INPUT_SIZE]
-    projection_full = small_full[:, 2 * LAUREL_RANK + LAYER_INPUT_SIZE :]
     gain_rows = norm_gains.astype(wide)
     router_wide = router_weight.astype(wide)
     coef_wide = coefficients.astype(wide)
     head_wide = query_key_gains.astype(wide)
-    (predicted, normed), pull_predict = jax.vjp(
-        predict_list,
-        tuple(versions[i].astype(wide) for i in range(4)),
-        gain_rows,
-        router_wide,
-        coef_wide,
-    )
-    normed_low = normed.astype(narrow)
+    predicted, normed_low = predict_here(versions, gain_rows, router_wide, coef_wide)
     *unit_weights, normed_low = together(gate_weight, up_weight, down_weight, normed_low)
 
     def hidden_columns(index):
@@ -913,22 +1406,7 @@
     phase_position = digits_all[:, :1] * 128.0 + digits_all[:, 1:2]
     frequency = rotary_base ** (-2.0 * jnp.arange(HEAD_WIDTH // 2, dtype=wide) / HEAD_WIDTH)
     phase = phase_position * frequency[None, :]
-    phase = jnp.concatenate([phase, phase], axis=-1)
     cosine, sine = jnp.cos(phase), jnp.sin(phase)
-    cosine_kv = jnp.where(first_core, cosine, 1.0)
-    sine_kv = jnp.where(first_core, sine, 0.0)
-
-    def kv_gain(gains):
-        return jnp.where(first_core, gains[1], 1.0)
-
-    query_kv = natural(forward_product(normed_rows, query_kv_full), core, line)
-    query_pre = query_kv[:, :HEAD_WIDTH]
-    kv_pre = query_kv[:, HEAD_WIDTH:]
-    rotated = head_apply(query_pre, head_wide[0], cosine, sine).astype(narrow)
-    kv_own = head_apply(kv_pre, kv_gain(head_wide), cosine_kv, sine_kv).astype(narrow)
-    mine = (kv_own, *gather_chips(kv_own))
-    theirs = tuple(other_core(part) for part in mine)
-
     first_row = chip * own
     row_docs = lax.dynamic_slice_in_dim(documents, first_row, own)
     begin_one = jnp.sum(documents < 1)
@@ -938,15 +1416,20 @@
     for part in range(own // QUERY_ROWS):
         bounds.append(lo[part * QUERY_ROWS] // KEY_ROWS)
         bounds.append((lo[(part + 1) * QUERY_ROWS - 1] + KEY_ROWS - 1) // KEY_ROWS)
-    meta = jnp.stack([chip, core, *bounds]).astype(jnp.int32)
+    meta = jnp.stack([chip, core, line, *bounds]).astype(jnp.int32)
+    rotated, kv_own, heads_pre = heads_here(meta, gathered, head_full, cosine, sine, head_wide)
+    tables = (heads_pre, cosine, sine, head_wide)
+    mine = (kv_own, *gather_chips(kv_own))
+    theirs = tuple(other_core(part) for part in mine)
+
     attended, lse = attend_here(meta, rotated, lo, mine, theirs)
     mixed_rows = arrival(attended.astype(narrow), core, line)
     attention_out = scatter_chip(transposed_product(mixed_rows, out_full).astype(narrow))
 
     down_low = forward_product(normed_low, laurel_full[:, :LAUREL_RANK]).astype(narrow)
     lifted = transposed_product(down_low, laurel_full[:, LAUREL_RANK:])
-    (merged, feed_in), pull_combine = jax.vjp(
-        combine, predicted[0], attention_out, normed_low.astype(wide), lifted, gain_rows
+    merged, feed_in = combine(
+        predicted[0], attention_out, normed_low.astype(wide), lifted, gain_rows
     )
     unit_rows = gather_chip(feed_in.astype(narrow))
     hidden_units, pull_activate = jax.vjp(
@@ -954,20 +1437,6 @@
     )
     hidden_low = hidden_units.astype(narrow)
     fed = scatter_chip(transposed_product(hidden_low, unit_down).astype(narrow))
-    (corrected, first), pull_correct = jax.vjp(
-        correct_list, merged, fed, predicted, gain_rows, router_wide, coef_wide
-    )
-    first_low = first.astype(narrow)
-    gated, pull_gate = jax.vjp(
-        activate, forward_product(first_low, gate_full), layer_input.astype(wide)
-    )
-    gated_low = gated.astype(narrow)
-    projected = transposed_product(gated_low, projection_full)
-    extra, pull_extra = jax.vjp(rms_norm_apply, projected, gain_rows[7])
-    result = jnp.stack(
-        [corrected[0].astype(narrow)] + [(corrected[i] + extra).astype(narrow) for i in (1, 2, 3)]
-    )
-
     def core_columns(x):
         top, bottom = x[:rows_here], x[rows_here:]
         keep = jnp.where(first_core, top, bottom)
@@ -982,16 +1451,21 @@
             parts += [first[:, columns], second[:, columns]]
         return jnp.concatenate(parts, axis=1)
 
-    corrected_grad = tuple(cotangent[i].astype(wide) for i in range(4))
-    projected_grad, gain_seven = pull_extra(
-        corrected_grad[1] + corrected_grad[2] + corrected_grad[3]
-    )
-    projected_low = projected_grad.astype(narrow)
-    gate_pre_grad, layer_grad = pull_gate(forward_product(projected_low, projection_full))
-    gate_pre_low = gate_pre_grad.astype(narrow)
-    merged_grad, fed_grad, predicted_grad, gains_correct, router_correct, coef_correct = (
-        pull_correct((corrected_grad, transposed_product(gate_pre_low, gate_full)))
-    )
+    (
+        result,
+        layer_grad,
+        fed_grad,
+        merged_grad,
+        first_grad,
+        packed_middle,
+        first_low,
+        gate_pre_low,
+        projected_low,
+        gated_low,
+    ) = middle_here(
+        merged, fed, predicted, cotangent, layer_input, gain_rows, router_wide, coef_wide, small_full
+    )
+
     io_sum = lax.psum_scatter(
         jnp.concatenate(
             [weight_product(first_low, gate_pre_low), weight_product(projected_low, gated_low)],
@@ -1001,21 +1475,17 @@
         scatter_dimension=0,
         tiled=True,
     )
-    fed_rows = gather_chip(fed_grad.astype(narrow))
+    fed_rows = gather_chip(fed_grad)
     fed_rows, io_sum = together(fed_rows, io_sum)
     io_share = share_line(io_sum).astype(narrow)
     gate_grad, up_grad = pull_activate(forward_product(fed_rows, unit_down))
+    down_sum = own_rows(weight_product(fed_rows, hidden_low).astype(narrow))
     two_low = jnp.concatenate([gate_grad.astype(narrow), up_grad.astype(narrow)], axis=1)
     feed_grad = scatter_chip(transposed_product(two_low, unit_two).astype(narrow))
-    down_part = weight_product(fed_rows, hidden_low).astype(narrow)
-    two_part = weight_product(unit_rows, two_low).astype(narrow)
-    down_sum = own_rows(down_part)
-    two_sum = own_rows(two_part)
-    active_grad, attention_grad, normed_combine, lifted_grad, gains_combine = pull_combine(
-        (merged_grad, feed_grad)
-    )
-    attention_low = attention_grad.astype(narrow)
-    lifted_low = lifted_grad.astype(narrow)
+    two_sum = own_rows(weight_product(unit_rows, two_low).astype(narrow))
+    first_total, active_grad, attention_low, lifted_low, packed_combine = combine_back_here(
+        merged, attention_out, lifted, merged_grad, feed_grad, first_grad, gain_rows, packed_middle
+    )
     down_grad_low = forward_product(lifted_low, laurel_full[:, LAUREL_RANK:]).astype(narrow)
     laurel_part = jnp.concatenate(
         [weight_product(normed_low, down_grad_low), weight_product(lifted_low, down_low)], axis=1
@@ -1032,117 +1502,94 @@
     out_sum = own_rows(out_part)
     mixed_grad = natural(mixed_grad_rows, core, line)
     delta = jnp.sum(mixed_grad.astype(wide) * attended, axis=-1)
-    query_grad, kv_keep, kv_send = attend_back_here(
-        meta, rotated, mixed_grad, lse, delta, lo, mine, theirs
-    )
-    _, pull_query = jax.vjp(
-        lambda x, g: head_apply(x, g, cosine, sine), query_pre, head_wide[0]
-    )
-    query_pre_grad, query_gain_grad = pull_query(query_grad.astype(narrow).astype(wide))
-    query_rows_grad = arrival(query_pre_grad.astype(narrow), core, line)
+    query_rows_grad, query_gain_grad, kv_keep, kv_send = attend_back_here(
+        meta, rotated, mixed_grad, lse, delta, lo, tables, mine, theirs
+    )
     query_part = weight_product(normed_rows, query_rows_grad).astype(narrow)
     kv_got = other_core(kv_send)
-    *kv_parts, out_sum = together(
+    *kv_parts, out_sum, query_part = together(
         *[(kv_keep[m].astype(wide) + kv_got[m].astype(wide)).astype(narrow) for m in range(CHIPS)],
         out_sum,
-    )
-    kv_grad, query_part = scatter_chips(kv_parts, query_part)
+        query_part,
+    )
+    laurel_here = jnp.where(
+        first_core, out_sum[:rows_here, HEAD_WIDTH:], out_sum[rows_here:, HEAD_WIDTH:]
+    )
+    out_here = jnp.concatenate(
+        [
+            jnp.concatenate([pairs(out_sum, 1), laurel_here], axis=1),
+            jnp.pad(io_share, ((0, 0), (0, 2 * LAUREL_RANK))),
+        ],
+        axis=0,
+    )
+    out_near = line_neighbours(out_here)
+    out_far = line_far(out_here, *out_near)
     query_sum = own_rows(query_part)
-
-    _, pull_kv = jax.vjp(
-        lambda x, g: head_apply(x, kv_gain(g), cosine_kv, sine_kv), kv_pre, head_wide
-    )
-    kv_pre_grad, kv_gain_grad = pull_kv(kv_grad)
-    kv_rows_grad = arrival(kv_pre_grad.astype(narrow), core, line)
+    (kv_grad,) = scatter_chips(kv_parts)
+    kv_grad, out_here, *out_others = together(kv_grad, out_here, *out_near, *out_far)
+
+    kv_rows_grad, kv_gain_grad = kv_back_here(meta, kv_grad, tables)
     head_grads = jnp.concatenate([query_rows_grad, kv_rows_grad], axis=1)
     kv_part = weight_product(normed_rows, kv_rows_grad).astype(narrow)
     normed_part = transposed_product(head_grads, query_kv_full).astype(narrow)
-    normed_part, kv_part, query_sum, down_sum, two_sum = together(
-        normed_part, kv_part, query_sum, down_sum, two_sum
-    )
     kv_weight_sum = own_rows(kv_part)
     normed_sum = scatter_chip(normed_part)
-    normed_sum, query_sum = together(normed_sum, query_sum)
-    normed_grad = (
-        normed_combine
-        + normed_sum
-        + transposed_product(down_grad_low, laurel_full[:, :LAUREL_RANK])
-    )
-    predicted_grad = (predicted_grad[0] + active_grad, *predicted_grad[1:])
-    version_grad, gains_predict, router_predict, coef_predict = pull_predict(
-        (predicted_grad, normed_grad)
-    )
-
-    gains_grad = (gains_correct + gains_combine + gains_predict).at[7].add(gain_seven)
-    head_gain_grad = kv_gain_grad.at[0].add(query_gain_grad)
-    coef_grad = coef_correct + coef_predict
-    packed = jnp.concatenate(
-        [
-            gains_grad,
-            router_correct + router_predict,
-            jnp.pad(
-                jnp.concatenate([head_gain_grad.reshape(1, -1), coef_grad.reshape(1, -1)], axis=1),
-                ((0, 3), (0, width - head_gain_grad.size - coef_grad.size)),
-            ),
-        ],
-        axis=0,
+    normed_sum, query_sum, kv_weight_sum, down_sum, two_sum, out_here = together(
+        normed_sum, query_sum, kv_weight_sum, down_sum, two_sum, out_here
+    )
+    query_here, kv_here = pairs(query_sum, 1), pairs(kv_weight_sum, 1)
+    query_near, kv_near = line_neighbours(query_here), line_neighbours(kv_here)
+    head_gain_grad = jnp.concatenate([query_gain_grad, kv_gain_grad], axis=0)
+    packed_early = packed_combine + jnp.pad(
+        head_gain_grad, ((12, 2), (128, width - 128 - HEAD_WIDTH))
+    )
+    version_grad, packed = predict_back_here(
+        versions,
+        first_total,
+        cotangent,
+        normed_sum,
+        active_grad + transposed_product(down_grad_low, laurel_full[:, :LAUREL_RANK]),
+        gain_rows,
+        router_wide,
+        coef_wide,
+        packed_early,
     )
     packed = butterfly(packed)
-    head_gain_sum = packed[12, : head_gain_grad.size].reshape(head_gain_grad.shape)
-    coef_sum = packed[12, head_gain_grad.size : head_gain_grad.size + coef_grad.size].reshape(
-        coef_grad.shape
-    )
-
+    query_far, kv_far = line_far(query_here, *query_near), line_far(kv_here, *kv_near)
     down_first, down_second = core_columns(down_sum)
     two_first, two_second = core_columns(two_sum)
-    pair = CORES * HEAD_WIDTH
-    ranks = 2 * LAUREL_RANK
-    laurel_here = jnp.where(
-        first_core, out_sum[:rows_here, HEAD_WIDTH:], out_sum[rows_here:, HEAD_WIDTH:]
-    )
-    out_lines = gather_line(
-        jnp.concatenate([pairs(out_sum, 1), laurel_here, io_share.reshape(rows_here, -1)], axis=1)
-    )
-    query_lines = gather_line(pairs(query_sum, 1))
-    kv_lines = gather_line(pairs(kv_weight_sum, 1))
-    query_all = jnp.concatenate(query_lines, axis=1).astype(wide)
-    out_all = jnp.concatenate([part[:, :pair] for part in out_lines], axis=1).astype(wide)
-    laurel_all = sum(part[:, pair : pair + ranks].astype(wide) for part in out_lines)
-    io_all = jnp.concatenate(
-        [
-            part[:, pair + ranks :].reshape(rows_here // LINE, 2 * LAYER_INPUT_SIZE)
-            for part in out_lines
-        ],
-        axis=0,
-    ).astype(wide)
-    kv_groups = [
-        kv_lines[k].astype(wide) + kv_lines[k + 1].astype(wide) for k in range(0, LINE, 2)
-    ]
-    key_sum = jnp.concatenate([g[:, :HEAD_WIDTH] for g in kv_groups], axis=1)
-    value_sum = jnp.concatenate([g[:, HEAD_WIDTH:] for g in kv_groups], axis=1)
 
     def unit(index):
         columns = slice(index * hidden, (index + 1) * hidden)
         return jnp.concatenate([two_first[:, columns], two_second[:, columns]], axis=1).astype(wide)
 
+    units = (unit(0), unit(1), jnp.concatenate([down_first, down_second], axis=1).astype(wide))
+    packed, *far = together(packed, *query_far, *kv_far, *units)
+    query_far, kv_far, units = far[:2], far[2:4], far[4:]
+    query_all, out_all, key_all, value_all, laurel_all, io_all = assemble_here(
+        meta,
+        (query_here, *query_near, *query_far),
+        (kv_here, *kv_near, *kv_far),
+        (out_here, *out_others),
+    )
+    heads_from, heads_to = 128, 128 + HEAD_WIDTH
+
     return (
         result,
-        jnp.stack([g.astype(narrow) for g in version_grad]),
-        layer_grad.astype(narrow),
+        version_grad,
+        layer_grad,
         packed[:8],
         packed[8:12],
-        coef_sum,
-        head_gain_sum,
+        packed[12:16, :20],
+        packed[12:14, heads_from:heads_to],
         query_all,
-        key_sum,
-        value_sum,
+        key_all,
+        value_all,
         out_all,
         laurel_all,
         io_all[:, :LAYER_INPUT_SIZE],
         io_all[:, LAYER_INPUT_SIZE:],
-        unit(0),
-        unit(1),
-        jnp.concatenate([down_first, down_second], axis=1).astype(wide),
+        *units,
     )
 
 

time: 751 us -> 725 us (0.965)
  other arithmetic: 114 us -> 51.6 us
  Pallas kernels: 11.8 us -> 59.5 us
  waiting for transfers between devices: 280 us -> 318 us
  starting transfers between devices: 130 us -> 101 us
  matrix products: 123 us -> 103 us
    pallas_call x0 -> x7, Pallas kernels: none -> 46.8 us  [the longest x1 17.1 us: middle_here(): pl.pallas_call(middle_kernel, out_shape=tuple((jax.ShapeDtypeStruct(*shap...]
    reduce_sum x10 -> x0, other arithmetic: 25.8 us -> none  [the longest x5 13.1 us: rms_norm_apply(): value_states * lax.rsqrt(jnp.mean(value_states * value_states, axis=-1, k...]
    ppermute x47, starting transfers between devices: 97.8 us -> 73.5 us  [along_heads(): lax.ppermute(x, 'heads', [(i, (i + step) % LINE) for i in range(LINE)])]
    convert_element_type x10 -> x3, other arithmetic: 13.4 us -> 0.02 us  [the longest x1 0.01 us: chip_device(): gain_rows = norm_gains.astype(wide)]
    another operation x14 -> x8, other arithmetic: 13.5 us -> 1.52 us  [the longest x4 9.34 us: chip_device(): jnp.stack([g.astype(narrow) for g in version_grad])]
    ppermute x2, waiting for transfers between devices: 0.45 us -> 12.1 us  [butterfly(): x = x + lax.ppermute(x, 'heads', [(i, i ^ mask) for i in range(LINE)])]
    ppermute x47, waiting for transfers between devices: 224 us -> 234 us  [along_heads(): lax.ppermute(x, 'heads', [(i, (i + step) % LINE) for i in range(LINE)])]
    dot_general x12 -> x0, matrix products: 9.66 us -> none  [the longest x6 8.05 us: modes(): jnp.dot(rms_norm_apply(value_states, gain), router.T, precision=highest)]
  transfers between devices with their start and end apart: 115 -> 115, of which waited for: 62 -> 69; matrix products, arithmetic and copies ran while one was open for 30% -> 19% of each run, Pallas kernels for 2% -> 5%
where the time goes in v3:
time: 725 us; the launch traced here: 715 us
  waiting for transfers between devices  318 us (44%)
  matrix products  103 us (14%)
  starting transfers between devices  101 us (14%)
  Pallas kernels  59.5 us (8%)
  local copies, waits for them, and re-layouts  59.3 us (8%)
  other arithmetic  51.6 us (7%)
  between operations  23.1 us (3%)
    ppermute x47, waiting for transfers between devices, along_heads(): lax.ppermute(x, 'heads', [(i, (i + step) % LINE) for i in range(LINE)])  234 us
    ppermute x47, starting transfers between devices, along_heads(): lax.ppermute(x, 'heads', [(i, (i + step) % LINE) for i in range(LINE)])  73.5 us
    ppermute x57, waiting for transfers between devices, across_blk(): return lax.ppermute(x, 'blk', [(i, i ^ mask) for i in range(CORES * CHIPS)])  56.9 us
    dot_general x6, matrix products, forward_product(): return jnp.dot(left, right, preferred_element_type=jnp.float32)  40.3 us
    unnamed x209, local copies, waits for them, and re-layouts  37.6 us
    dot_general x9, matrix products, weight_product(): lax.dot_general(left, right, (((0,), (0,)), ((), ())), preferred_element_...  33.8 us
    dot_general x6, matrix products, transposed_product(): lax.dot_general(left, right, (((1,), (1,)), ((), ())), preferred_element_...  28.4 us
    ppermute x57, starting transfers between devices, across_blk(): return lax.ppermute(x, 'blk', [(i, i ^ mask) for i in range(CORES * CHIPS)])  25.9 us
  transfers between devices with their start and end apart: 115, of which 69 were waited for; matrix products, arithmetic and copies ran while one was open for 19% of the time, Pallas kernels for 5%

profile of v3, /device:TPU:0, one launch (start us, length us, event | category | flops | bytes accessed | tf_op | source)
XLA Modules:
  0.0 715.3 jit_solution(5825565708522051954)
XLA Ops:
  13.7 4.7 shard_map.314
  48.9 10.7 %collective-permute-done.1 = bf16[128,2176]{1,0:T(8,128)(2,1)S(1)} collective-permute-done((bf16[128,2176]{1,0:T(8,128)(2,1)S(1)}, bf16[128,2176]{1,0:T(8,128)(2,1)S(1)}, u32[]{:S(2)}, u32[]{:S(2)}) %collective-permute-start.1) | collective-permute-done | bytes 557088 | tf_op jit(solution)/shard_map/ppermute | solution.py:441
  63.2 6.1 collective-permute-done.2
  78.5 7.1 shard_map.315
  90.6 11.1 %collective-permute-done.9.refs_1_ = bf16[1024,256]{1,0:T(8,128)(2,1)S(1)} collective-permute-done((bf16[1024,256]{1,0:T(8,128)(2,1)S(1)}, bf16[1024,256]{1,0:T(8,128)(2,1)S(1)}, u32[]{:S(2)}, u32[]{:S(2)}) %collective-permute-start.9) | collective-permute-done | bytes 524320 | tf_op jit(solution)/shard_map/ppermute | solution.py:445
  105.2 6.3 collective-permute-done.11.refs_3_
  111.5 5.2 collective-permute-done.12.refs_4_
  120.7 4.1 shard_map.316
  138.3 6.9 collective-permute-done.21
  145.4 5.4 collective-permute-done.24
  156.4 5.8 collective-permute-done.22
  162.3 10.4 %collective-permute-done.25 = bf16[128,2048]{1,0:T(8,128)(2,1)} collective-permute-done((bf16[128,2048]{1,0:T(8,128)(2,1)}, bf16[128,2048]{1,0:T(8,128)(2,1)}, u32[]{:S(2)}, u32[]{:S(2)}) %collective-permute-start.25) | collective-permute-done | bytes 524320 | tf_op jit(solution)/shard_map/ppermute | solution.py:441
  181.4 12.8 %collective-permute-done.26 = bf16[128,2048]{1,0:T(8,128)(2,1)S(1)} collective-permute-done((bf16[128,2048]{1,0:T(8,128)(2,1)S(1)}, bf16[128,2048]{1,0:T(8,128)(2,1)S(1)}, u32[]{:S(2)}, u32[]{:S(2)}) %collective-permute-start.26) | collective-permute-done | bytes 524320 | tf_op jit(solution)/shard_map/ppermute | solution.py:441
  194.3 8.7 %collective-permute-done.27 = bf16[128,2048]{1,0:T(8,128)(2,1)S(1)} collective-permute-done((bf16[128,2048]{1,0:T(8,128)(2,1)S(1)}, bf16[128,2048]{1,0:T(8,128)(2,1)S(1)}, u32[]{:S(2)}, u32[]{:S(2)}) %collective-permute-start.27) | collective-permute-done | bytes 524320 | tf_op jit(solution)/shard_map/ppermute | solution.py:441
  211.1 4.4 collective-permute-done.29
  220.4 7.6 %fusion.11 = f32[1024,1024]{0,1:T(8,128)S(1)} fusion(bf16[1024,2048]{1,0:T(8,128)(2,1)} %constant_dynamic-update-slice_fusion.9, bf16[2048,3072]{1,0:T(8,128)(2,1)} %all-gather.8.cloned.1.call-done), kind=kOutput, calls=%fused_computation.14 | convolution fusion | flops 4294967296 | bytes 12582912 | tf_op jit(solution)/shard_map/dot_general | solution.py:111
  228.1 12.6 %multiply_convert_fusion.1 = (bf16[1024,1024]{0,1:T(8,128)(2,1)S(1)}, f32[1024,1024]{0,1:T(8,128)}) fusion(f32[1024,1024]{0,1:T(8,128)S(1)} %fusion.11, bf16[1024,2048]{1,0:T(8,128)(2,1)} %constant_dynamic-update-slice_fusion.9, bf16[2048,3072]{1,0:T(8,128)(2,1)} %all-gather.8.cloned.1.call-done), kind=kOutput, calls=%fused_computation.18 | convolution fusion | flops 4305453056 | bytes 18874368 | tf_op jit(solution)/shard_map/dot_general | solution.py:111
  240.7 7.8 %convolution_convert_fusion.4 = bf16[1024,2048]{1,0:T(8,128)(2,1)S(1)} fusion(bf16[1024,1024]{0,1:T(8,128)(2,1)S(1)} %get-tuple-element.281, bf16[2048,3072]{1,0:T(8,128)(2,1)} %all-gather.8.cloned.1.call-done), kind=kOutput, calls=%fused_computation.24 | convolution fusion | flops 4297064448 | bytes 10485760 | tf_op jit(solution)/shard_map/dot_general | solution.py:115
  257.2 6.9 collective-permute-done.38
  264.3 4.8 collective-permute-done.41
  271.2 9.8 %collective-permute-done.39 = bf16[128,2048]{1,0:T(8,128)(2,1)S(1)} collective-permute-done((bf16[128,2048]{1,0:T(8,128)(2,1)S(1)}, bf16[128,2048]{1,0:T(8,128)(2,1)S(1)}, u32[]{:S(2)}, u32[]{:S(2)}) %collective-permute-start.39) | collective-permute-done | bytes 524320 | tf_op jit(solution)/shard_map/ppermute | solution.py:441
  281.0 10.6 %collective-permute-done.42 = bf16[128,2048]{1,0:T(8,128)(2,1)S(1)} collective-permute-done((bf16[128,2048]{1,0:T(8,128)(2,1)S(1)}, bf16[128,2048]{1,0:T(8,128)(2,1)S(1)}, u32[]{:S(2)}, u32[]{:S(2)}) %collective-permute-start.42) | collective-permute-done | bytes 524320 | tf_op jit(solution)/shard_map/ppermute | solution.py:441
  292.0 17.1 %shard_map.317 = (bf16[4,128,2048]{2,1,0:T(8,128)(2,1)}, bf16[128,256]{1,0:T(8,128)(2,1)}, bf16[128,2048]{1,0:T(8,128)(2,1)S(1)}, f32[128,2048]{1,0:T(8,128)S(1)...) custom-call(f32[4,20]{1,0:T(4,128)S(1)} %convert_element_type.367.co, ...), custom_call_target="tpu_custom_call" | custom-call | flops 16999999488 | bytes 56100000 | tf_op jit(solution)/shard_map/pallas_call | solution.py:1308
  315.9 12.8 %collective-permute-done.43 = bf16[128,2048]{1,0:T(8,128)(2,1)S(1)} collective-permute-done((bf16[128,2048]{1,0:T(8,128)(2,1)S(1)}, bf16[128,2048]{1,0:T(8,128)(2,1)S(1)}, u32[]{:S(2)}, u32[]{:S(2)}) %collective-permute-start.43) | collective-permute-done | bytes 524320 | tf_op jit(solution)/shard_map/ppermute | solution.py:441
  328.8 8.7 %collective-permute-done.44 = bf16[128,2048]{1,0:T(8,128)(2,1)S(1)} collective-permute-done((bf16[128,2048]{1,0:T(8,128)(2,1)S(1)}, bf16[128,2048]{1,0:T(8,128)(2,1)S(1)}, u32[]{:S(2)}, u32[]{:S(2)}) %collective-permute-start.44) | collective-permute-done | bytes 524320 | tf_op jit(solution)/shard_map/ppermute | solution.py:441
  345.7 4.1 collective-permute-done.46
  357.3 9.4 %convolution_convert_fusion.3 = bf16[2048,1024]{1,0:T(8,128)(2,1)} fusion(bf16[1024,2048]{1,0:T(8,128)(2,1)} %constant_dynamic-update-slice_fusion.18, bf16[1024,1024]{0,1:T(8,128)(2,1)} %copy-done.84), kind=kOutput, calls=%fused_computation.23 | convolution fusion | flops 4297064448 | bytes 10485760 | tf_op jit(solution)/shard_map/dot_general | solution.py:121
  367.0 12.2 %fusion.8 = (bf16[1024,1024]{0,1:T(8,128)(2,1)S(1)}, bf16[1024,1024]{0,1:T(8,128)(2,1)S(1)}) fusion(f32[1024,1024]{0,1:T(8,128)} %copy-done.83, f32[1024,1024]{0,1:T(8,128)} %get-tuple-element.282, bf16[1024,2048]{1,0:T(8,128)(2,1)} %constant_dynamic-update-slice_fusion.18, bf16[2048,3072]{1,0:T(8,128)(2,1)} %all-gather.8.cloned.1.call-done), kind=kOutput, calls=%fused_computation.11 | convolution fusion | flops 4320133120 | bytes 20971520 | tf_op jit(solution)/shard_map/dot_general | solution.py:111
  381.2 14.7 %convolution_convert_fusion = bf16[2048,2048]{1,0:T(8,128)(2,1)} fusion(bf16[1024,2048]{1,0:T(8,128)(2,1)} %constant_dynamic-update-slice_fusion.9, bf16[1024,1024]{0,1:T(8,128)(2,1)S(1)} %get-tuple-element.174, bf16[1024,1024]{0,1:T(8,128)(2,1)S(1)} %get-tuple-element.173), kind=kOutput, calls=%fused_computation.2 | convolution fusion | flops 8602517504 | bytes 16777216 | tf_op jit(solution)/shard_map/dot_general | solution.py:121
  396.4 12.7 %fusion.13 = bf16[1024,2048]{1,0:T(8,128)(2,1)S(1)} fusion(bf16[2048,3072]{1,0:T(8,128)(2,1)} %all-gather.8.cloned.1.call-done, bf16[1024,1024]{0,1:T(8,128)(2,1)} %copy-done.86, bf16[1024,1024]{0,1:T(8,128)(2,1)} %copy-done.85), kind=kOutput, calls=%fused_computation.20 | convolution fusion | flops 8600420352 | bytes 16777216 | tf_op jit(solution)/shard_map/dot_general | solution.py:115
  418.4 7.0 collective-permute-done.54
  425.6 5.4 collective-permute-done.57
  442.4 11.2 %collective-permute-done.58 = bf16[128,2048]{1,0:T(8,128)(2,1)} collective-permute-done((bf16[128,2048]{1,0:T(8,128)(2,1)}, bf16[128,2048]{1,0:T(8,128)(2,1)}, u32[]{:S(2)}, u32[]{:S(2)}) %collective-permute-start.58) | collective-permute-done | bytes 524320 | tf_op jit(solution)/shard_map/ppermute | solution.py:441
  472.3 8.0 %collective-permute-done.59 = bf16[128,2048]{1,0:T(8,128)(2,1)} collective-permute-done((bf16[128,2048]{1,0:T(8,128)(2,1)S(1)}, bf16[128,2048]{1,0:T(8,128)(2,1)}, u32[]{:S(2)}, u32[]{:S(2)}) %collective-permute-start.59) | collective-permute-done | bytes 524320 | tf_op jit(solution)/shard_map/ppermute | solution.py:441
  481.3 7.4 %collective-permute-done.60 = bf16[128,2048]{1,0:T(8,128)(2,1)S(1)} collective-permute-done((bf16[128,2048]{1,0:T(8,128)(2,1)S(1)}, bf16[128,2048]{1,0:T(8,128)(2,1)S(1)}, u32[]{:S(2)}, u32[]{:S(2)}) %collective-permute-start.60) | collective-permute-done | bytes 524320 | tf_op jit(solution)/shard_map/ppermute | solution.py:441
  506.3 4.7 convolution_convert_fusion.10
  516.5 8.6 %shard_map.319 = (bf16[1024,256]{1,0:T(8,128)(2,1)S(1)}, f32[1,256]{1,0:T(1,128)S(1)}, bf16[4,1024,256]{2,1,0:T(8,128)(2,1)}, bf16[4,1024,256]{2,1,0:T(8,128)(2,1)}) custom-call(s32[7]{0:T(128)S(1)} %copy-done.28, bf16[1024,256]{1,0:T(8,128)(2,1)S(1)} %copy-done.48, bf16[1024,256]{1,0:T(8,128)(2,1)S(1)} %pad_maximum_fusion.22.grad_ref, ...), custom_call_target="tpu_custom_call" | custom-call | flops 20500000768 | bytes 67650000 | tf_op jit(solution)/shard_map/pallas_call | solution.py:854
  526.0 4.6 fusion.23
  534.1 12.1 %reduce-scatter.13.cloned.1.call-done = bf16[512,384]{1,0:T(8,128)(2,1)} async-done(((bf16[2048,384]{1,0:T(8,128)(2,1)}), bf16[512,384]{1,0:T(8,128)(2,1)}) %reduce-scatter.13.cloned.1.call-update) | async-done | bytes 393232 | tf_op jit(solution)/shard_map/reduce_scatter | solution.py:566
  549.1 4.4 collective-permute-start.72
  616.6 8.7 %collective-permute-done.85 = bf16[128,2048]{1,0:T(8,128)(2,1)S(1)} collective-permute-done((bf16[128,2048]{1,0:T(8,128)(2,1)S(1)}, bf16[128,2048]{1,0:T(8,128)(2,1)S(1)}, u32[]{:S(2)}, u32[]{:S(2)}) %collective-permute-start.85) | collective-permute-done | bytes 524320 | tf_op jit(solution)/shard_map/ppermute | solution.py:441
  625.3 9.2 %collective-permute-done.88 = bf16[128,2048]{1,0:T(8,128)(2,1)S(1)} collective-permute-done((bf16[128,2048]{1,0:T(8,128)(2,1)S(1)}, bf16[128,2048]{1,0:T(8,128)(2,1)S(1)}, u32[]{:S(2)}, u32[]{:S(2)}) %collective-permute-start.88) | collective-permute-done | bytes 524320 | tf_op jit(solution)/shard_map/ppermute | solution.py:441
  641.3 10.4 %shard_map.321 = (bf16[4,128,2048]{2,1,0:T(8,128)(2,1)}, f32[16,2048]{1,0:T(8,128)S(1)}) custom-call(f32[4,20]{1,0:T(4,128)S(1)} %copy-done.24, bf16[4,128,2048]{2,1,0:T(8,128)(2,1)S(1)} %copy-done.30, f32[128,2048]{1,0:T(8,128)S(1)} %copy-done.50, bf16[4,128,2048]{2,1,0:T(8,128)(2,1)S(1)} %copy-done.31, f32[128,2048]{1,0:T(8,128)S(1)} %convert_add_fusion.normed_ref, ...), custom_call_target="tpu_custom_call" | custom-call | flops 10000000000 | bytes 33000000 | tf_op jit(solution)/shard_map/pallas_call | solution.py:1264
  654.3 4.6 collective-permute-done.90
  661.0 4.4 collective-permute-done.91
  671.0 5.5 collective-permute-done.95.refs_1_
  676.5 4.3 collective-permute-done.97.refs_2_
  687.2 9.8 %collective-permute-done.93 = f32[16,2048]{1,0:T(8,128)S(1)} collective-permute-done((f32[16,2048]{1,0:T(8,128)S(1)}, f32[16,2048]{1,0:T(8,128)S(1)}, u32[]{:S(2)}, u32[]{:S(2)}) %collective-permute-start.93) | collective-permute-done | bytes 131104 | tf_op jit(solution)/shard_map/ppermute | solution.py:547
  (591 shorter events, 300.1 us)
Async XLA Ops:
  7.3 71.2 %all-gather.4.cloned.1.call-start = ((), (), s32[]{:S(2)}) async-start(), calls=%async_computation.6 | async-start | bytes 3932160 | tf_op jit(solution)/shard_map/all_gather | solution.py:562
  12.7 140.6 %all-gather.6.cloned.1.call-start = ((), (), s32[]{:S(2)}) async-start(), calls=%async_computation.7 | async-start | bytes 2949120 | tf_op jit(solution)/shard_map/all_gather | solution.py:1375
  13.6 206.9 %all-gather.8.cloned.1.call-start = ((), (), s32[]{:S(2)}) async-start(), calls=%async_computation.8 | async-start | bytes 15728640 | tf_op jit(solution)/shard_map/all_gather | solution.py:562
  30.0 327.3 %reduce-scatter.7.cloned.1.call-start = ((), (), s32[]{:S(2)}) async-start(), calls=%async_computation.9 | async-start | bytes 2359296 | tf_op jit(solution)/shard_map/reduce_scatter | solution.py:1469
  30.3 18.5 %collective-permute-start = (bf16[128,2176]{1,0:T(8,128)(2,1)S(1)}, bf16[128,2176]{1,0:T(8,128)(2,1)S(1)}, u32[]{:S(2)}, u32[]{:S(2)}) collective-permute-start(bf16[128,2176]{1,0:T(8,128)(2,1)S(1)} %fusion.39), channel_id=1, source_target_pairs={{0,8},{8,16},{16,24},{24,0},{1,9},{9,17},{17,25},{25,1},{2,10},{10... | collective-permute-start | bytes 1671176 | tf_op jit(solution)/shard_map/ppermute | solution.py:441
  33.2 26.3 %collective-permute-start.1 = (bf16[128,2176]{1,0:T(8,128)(2,1)S(1)}, bf16[128,2176]{1,0:T(8,128)(2,1)S(1)}, u32[]{:S(2)}, u32[]{:S(2)}) collective-permute-start(bf16[128,2176]{1,0:T(8,128)(2,1)S(1)} %fusion.39), channel_id=1, source_target_pairs={{0,24},{8,0},{16,8},{24,16},{1,25},{9,1},{17,9},{25,17},{2,26},{10... | collective-permute-start | bytes 1671176 | tf_op jit(solution)/shard_map/ppermute | solution.py:441
  35.4 37.0 %collective-permute-start.5 = (bf16[128,2176]{1,0:T(8,128)(2,1)S(1)}, bf16[128,2176]{1,0:T(8,128)(2,1)}, u32[]{:S(2)}, u32[]{:S(2)}) collective-permute-start(bf16[128,2176]{1,0:T(8,128)(2,1)S(1)} %fusion.39), channel_id=1, source_target_pairs={{0,1},{1,0},{2,3},{3,2},{4,5},{5,4},{6,7},{7,6},{8,9},{9,8},{10,11... | collective-permute-start | bytes 1671176 | tf_op jit(solution)/shard_map/ppermute | solution.py:445
  48.8 20.5 %collective-permute-start.2 = (bf16[64,2176]{1,0:T(8,128)(2,1)S(1)}, bf16[64,2176]{1,0:T(8,128)(2,1)S(1)}, u32[]{:S(2)}, u32[]{:S(2)}) collective-permute-start(bf16[64,2176]{1,0:T(8,128)(2,1)S(1)} %slice.583), channel_id=1, source_target_pairs={{0,8},{8,16},{16,24},{24,0},{1,9},{9,17},{17,25},{25,1},{2,10},{10... | collective-permute-start | bytes 835592 | tf_op jit(solution)/shard_map/ppermute | solution.py:441
  90.6 26.4 %collective-permute-start.13 = (bf16[1024,256]{1,0:T(8,128)(2,1)S(1)}, bf16[1024,256]{1,0:T(8,128)(2,1)S(1)}, u32[]{:S(2)}, u32[]{:S(2)}) collective-permute-start(bf16[1024,256]{1,0:T(8,128)(2,1)S(1)} %get-tuple-element.96.refs_0_), channel_id=1, source_target_pairs={{0,1},{1,0},{2,3},{3,2},{4,5},{5,4},{6,7},{7,6},{8,9},{9,8},{10,11... | collective-permute-start | bytes 1572872 | tf_op jit(solution)/shard_map/ppermute | solution.py:445
  135.8 20.6 %collective-permute-start.18 = (bf16[128,2048]{1,0:T(8,128)(2,1)}, bf16[128,2048]{1,0:T(8,128)(2,1)}, u32[]{:S(2)}, u32[]{:S(2)}) collective-permute-start(bf16[128,2048]{1,0:T(8,128)(2,1)} %get-tuple-element.200), channel_id=1, source_target_pairs={{0,1},{1,0},{2,3},{3,2},{4,5},{5,4},{6,7},{7,6},{8,9},{9,8},{10,11... | collective-permute-start | bytes 1572872 | tf_op jit(solution)/shard_map/ppermute | solution.py:445
  145.4 16.9 %collective-permute-start.22 = (bf16[128,2048]{1,0:T(8,128)(2,1)S(1)}, bf16[128,2048]{1,0:T(8,128)(2,1)}, u32[]{:S(2)}, u32[]{:S(2)}) collective-permute-start(bf16[128,2048]{1,0:T(8,128)(2,1)S(1)} %pad_maximum_fusion.12), channel_id=1, source_target_pairs={{0,8},{8,16},{16,24},{24,0},{1,9},{9,17},{17,25},{25,1},{2,10},{10... | collective-permute-start | bytes 1572872 | tf_op jit(solution)/shard_map/ppermute | solution.py:441
  151.7 21.0 %collective-permute-start.25 = (bf16[128,2048]{1,0:T(8,128)(2,1)}, bf16[128,2048]{1,0:T(8,128)(2,1)}, u32[]{:S(2)}, u32[]{:S(2)}) collective-permute-start(bf16[128,2048]{1,0:T(8,128)(2,1)} %pad_maximum_fusion.13), channel_id=1, source_target_pairs={{0,24},{8,0},{16,8},{24,16},{1,25},{9,1},{17,9},{25,17},{2,26},{10... | collective-permute-start | bytes 1572872 | tf_op jit(solution)/shard_map/ppermute | solution.py:441
  177.6 16.6 %collective-permute-start.26 = (bf16[128,2048]{1,0:T(8,128)(2,1)S(1)}, bf16[128,2048]{1,0:T(8,128)(2,1)S(1)}, u32[]{:S(2)}, u32[]{:S(2)}) collective-permute-start(bf16[128,2048]{1,0:T(8,128)(2,1)S(1)} %get-tuple-element.223), channel_id=1, source_target_pairs={{0,8},{8,16},{16,24},{24,0},{1,9},{9,17},{17,25},{25,1},{2,10},{10... | collective-permute-start | bytes 1572872 | tf_op jit(solution)/shard_map/ppermute | solution.py:441
  178.2 24.8 %collective-permute-start.27 = (bf16[128,2048]{1,0:T(8,128)(2,1)S(1)}, bf16[128,2048]{1,0:T(8,128)(2,1)S(1)}, u32[]{:S(2)}, u32[]{:S(2)}) collective-permute-start(bf16[128,2048]{1,0:T(8,128)(2,1)S(1)} %get-tuple-element.223), channel_id=1, source_target_pairs={{0,24},{8,0},{16,8},{24,16},{1,25},{9,1},{17,9},{25,17},{2,26},{10... | collective-permute-start | bytes 1572872 | tf_op jit(solution)/shard_map/ppermute | solution.py:441
  181.4 36.5 %collective-permute-start.31 = (bf16[128,2048]{1,0:T(8,128)(2,1)S(1)}, bf16[128,2048]{1,0:T(8,128)(2,1)S(1)}, u32[]{:S(2)}, u32[]{:S(2)}) collective-permute-start(bf16[128,2048]{1,0:T(8,128)(2,1)S(1)} %get-tuple-element.223), channel_id=1, source_target_pairs={{0,1},{1,0},{2,3},{3,2},{4,5},{5,4},{6,7},{7,6},{8,9},{9,8},{10,11... | collective-permute-start | bytes 1572872 | tf_op jit(solution)/shard_map/ppermute | solution.py:445
  194.2 16.9 %collective-permute-start.28 = (bf16[64,2048]{1,0:T(8,128)(2,1)S(1)}, bf16[64,2048]{1,0:T(8,128)(2,1)S(1)}, u32[]{:S(2)}, u32[]{:S(2)}) collective-permute-start(bf16[64,2048]{1,0:T(8,128)(2,1)S(1)} %slice.614), channel_id=1, source_target_pairs={{0,8},{8,16},{16,24},{24,0},{1,9},{9,17},{17,25},{25,1},{2,10},{10... | collective-permute-start | bytes 786440 | tf_op jit(solution)/shard_map/ppermute | solution.py:441
  254.4 16.8 %collective-permute-start.35 = (bf16[128,2048]{1,0:T(8,128)(2,1)S(1)}, bf16[128,2048]{1,0:T(8,128)(2,1)S(1)}, u32[]{:S(2)}, u32[]{:S(2)}) collective-permute-start(bf16[128,2048]{1,0:T(8,128)(2,1)S(1)} %get-tuple-element.193), channel_id=1, source_target_pairs={{0,1},{1,0},{2,3},{3,2},{4,5},{5,4},{6,7},{7,6},{8,9},{9,8},{10,11... | collective-permute-start | bytes 1572872 | tf_op jit(solution)/shard_map/ppermute | solution.py:445
  264.2 16.8 %collective-permute-start.39 = (bf16[128,2048]{1,0:T(8,128)(2,1)S(1)}, bf16[128,2048]{1,0:T(8,128)(2,1)S(1)}, u32[]{:S(2)}, u32[]{:S(2)}) collective-permute-start(bf16[128,2048]{1,0:T(8,128)(2,1)S(1)} %pad_maximum_fusion.15), channel_id=1, source_target_pairs={{0,8},{8,16},{16,24},{24,0},{1,9},{9,17},{17,25},{25,1},{2,10},{10... | collective-permute-start | bytes 1572872 | tf_op jit(solution)/shard_map/ppermute | solution.py:441
  269.2 22.5 %collective-permute-start.42 = (bf16[128,2048]{1,0:T(8,128)(2,1)S(1)}, bf16[128,2048]{1,0:T(8,128)(2,1)S(1)}, u32[]{:S(2)}, u32[]{:S(2)}) collective-permute-start(bf16[128,2048]{1,0:T(8,128)(2,1)S(1)} %pad_maximum_fusion.16), channel_id=1, source_target_pairs={{0,24},{8,0},{16,8},{24,16},{1,25},{9,1},{17,9},{25,17},{2,26},{10... | collective-permute-start | bytes 1572872 | tf_op jit(solution)/shard_map/ppermute | solution.py:441
  312.0 199.0 %reduce-scatter.9.cloned.1.call-start = ((), (), s32[]{:S(2)}) async-start(), calls=%async_computation.10 | async-start | bytes 5242880 | tf_op jit(solution)/shard_map/reduce_scatter | solution.py:566
  312.1 16.7 %collective-permute-start.43 = (bf16[128,2048]{1,0:T(8,128)(2,1)S(1)}, bf16[128,2048]{1,0:T(8,128)(2,1)S(1)}, u32[]{:S(2)}, u32[]{:S(2)}) collective-permute-start(bf16[128,2048]{1,0:T(8,128)(2,1)S(1)} %get-tuple-element.103), channel_id=1, source_target_pairs={{0,8},{8,16},{16,24},{24,0},{1,9},{9,17},{17,25},{25,1},{2,10},{10... | collective-permute-start | bytes 1572872 | tf_op jit(solution)/shard_map/ppermute | solution.py:441
  312.7 24.8 %collective-permute-start.44 = (bf16[128,2048]{1,0:T(8,128)(2,1)S(1)}, bf16[128,2048]{1,0:T(8,128)(2,1)S(1)}, u32[]{:S(2)}, u32[]{:S(2)}) collective-permute-start(bf16[128,2048]{1,0:T(8,128)(2,1)S(1)} %get-tuple-element.103), channel_id=1, source_target_pairs={{0,24},{8,0},{16,8},{24,16},{1,25},{9,1},{17,9},{25,17},{2,26},{10... | collective-permute-start | bytes 1572872 | tf_op jit(solution)/shard_map/ppermute | solution.py:441
  315.9 36.3 %collective-permute-start.48 = (bf16[128,2048]{1,0:T(8,128)(2,1)S(1)}, bf16[128,2048]{1,0:T(8,128)(2,1)S(1)}, u32[]{:S(2)}, u32[]{:S(2)}) collective-permute-start(bf16[128,2048]{1,0:T(8,128)(2,1)S(1)} %get-tuple-element.103), channel_id=1, source_target_pairs={{0,1},{1,0},{2,3},{3,2},{4,5},{5,4},{6,7},{7,6},{8,9},{9,8},{10,11... | collective-permute-start | bytes 1572872 | tf_op jit(solution)/shard_map/ppermute | solution.py:445
  328.8 16.9 %collective-permute-start.45 = (bf16[64,2048]{1,0:T(8,128)(2,1)S(1)}, bf16[64,2048]{1,0:T(8,128)(2,1)S(1)}, u32[]{:S(2)}, u32[]{:S(2)}) collective-permute-start(bf16[64,2048]{1,0:T(8,128)(2,1)S(1)} %slice.633), channel_id=1, source_target_pairs={{0,8},{8,16},{16,24},{24,0},{1,9},{9,17},{17,25},{25,1},{2,10},{10... | collective-permute-start | bytes 786440 | tf_op jit(solution)/shard_map/ppermute | solution.py:441
  366.7 144.3 %reduce-scatter.11.cloned.1.call-start = ((), (), s32[]{:S(2)}) async-start(), calls=%async_computation.11 | async-start | bytes 10485760 | tf_op jit(solution)/shard_map/reduce_scatter | solution.py:566
  395.9 150.3 %reduce-scatter.13.cloned.1.call-start = ((), (), s32[]{:S(2)}) async-start(), calls=%async_computation.12 | async-start | bytes 1966080 | tf_op jit(solution)/shard_map/reduce_scatter | solution.py:566
  415.9 20.3 %collective-permute-start.51 = (bf16[128,2048]{1,0:T(8,128)(2,1)}, bf16[128,2048]{1,0:T(8,128)(2,1)}, u32[]{:S(2)}, u32[]{:S(2)}) collective-permute-start(bf16[128,2048]{1,0:T(8,128)(2,1)} %get-tuple-element.186), channel_id=1, source_target_pairs={{0,1},{1,0},{2,3},{3,2},{4,5},{5,4},{6,7},{7,6},{8,9},{9,8},{10,11... | collective-permute-start | bytes 1572872 | tf_op jit(solution)/shard_map/ppermute | solution.py:445
  425.5 16.9 %collective-permute-start.55 = (bf16[128,2048]{1,0:T(8,128)(2,1)S(1)}, bf16[128,2048]{1,0:T(8,128)(2,1)}, u32[]{:S(2)}, u32[]{:S(2)}) collective-permute-start(bf16[128,2048]{1,0:T(8,128)(2,1)S(1)} %pad_maximum_fusion.18), channel_id=1, source_target_pairs={{0,8},{8,16},{16,24},{24,0},{1,9},{9,17},{17,25},{25,1},{2,10},{10... | collective-permute-start | bytes 1572872 | tf_op jit(solution)/shard_map/ppermute | solution.py:441
  431.8 21.8 %collective-permute-start.58 = (bf16[128,2048]{1,0:T(8,128)(2,1)}, bf16[128,2048]{1,0:T(8,128)(2,1)}, u32[]{:S(2)}, u32[]{:S(2)}) collective-permute-start(bf16[128,2048]{1,0:T(8,128)(2,1)} %pad_maximum_fusion.19), channel_id=1, source_target_pairs={{0,24},{8,0},{16,8},{24,16},{1,25},{9,1},{17,9},{25,17},{2,26},{10... | collective-permute-start | bytes 1572872 | tf_op jit(solution)/shard_map/ppermute | solution.py:441
  435.0 35.5 %collective-permute-start.67 = (bf16[64,512]{1,0:T(8,128)(2,1)}, bf16[64,512]{1,0:T(8,128)(2,1)S(1)}, u32[]{:S(2)}, u32[]{:S(2)}) collective-permute-start(bf16[64,512]{1,0:T(8,128)(2,1)} %get-tuple-element.261), channel_id=1, source_target_pairs={{0,8},{8,16},{16,24},{24,0},{1,9},{9,17},{17,25},{25,1},{2,10},{10... | collective-permute-start | bytes 196616 | tf_op jit(solution)/shard_map/ppermute | solution.py:441
  435.4 35.3 %collective-permute-start.68 = (bf16[64,512]{1,0:T(8,128)(2,1)}, bf16[64,512]{1,0:T(8,128)(2,1)}, u32[]{:S(2)}, u32[]{:S(2)}) collective-permute-start(bf16[64,512]{1,0:T(8,128)(2,1)} %get-tuple-element.263), channel_id=1, source_target_pairs={{0,16},{8,24},{16,0},{24,8},{1,17},{9,25},{17,1},{25,9},{2,18},{10... | collective-permute-start | bytes 196616 | tf_op jit(solution)/shard_map/ppermute | solution.py:441
  436.2 34.6 %collective-permute-start.69 = (bf16[64,512]{1,0:T(8,128)(2,1)}, bf16[64,512]{1,0:T(8,128)(2,1)}, u32[]{:S(2)}, u32[]{:S(2)}) collective-permute-start(bf16[64,512]{1,0:T(8,128)(2,1)} %get-tuple-element.262), channel_id=1, source_target_pairs={{0,24},{8,0},{16,8},{24,16},{1,25},{9,1},{17,9},{25,17},{2,26},{10... | collective-permute-start | bytes 196616 | tf_op jit(solution)/shard_map/ppermute | solution.py:441
  463.6 16.7 %collective-permute-start.59 = (bf16[128,2048]{1,0:T(8,128)(2,1)S(1)}, bf16[128,2048]{1,0:T(8,128)(2,1)}, u32[]{:S(2)}, u32[]{:S(2)}) collective-permute-start(bf16[128,2048]{1,0:T(8,128)(2,1)S(1)} %get-tuple-element.112), channel_id=1, source_target_pairs={{0,8},{8,16},{16,24},{24,0},{1,9},{9,17},{17,25},{25,1},{2,10},{10... | collective-permute-start | bytes 1572872 | tf_op jit(solution)/shard_map/ppermute | solution.py:441
  463.9 24.8 %collective-permute-start.60 = (bf16[128,2048]{1,0:T(8,128)(2,1)S(1)}, bf16[128,2048]{1,0:T(8,128)(2,1)S(1)}, u32[]{:S(2)}, u32[]{:S(2)}) collective-permute-start(bf16[128,2048]{1,0:T(8,128)(2,1)S(1)} %get-tuple-element.112), channel_id=1, source_target_pairs={{0,24},{8,0},{16,8},{24,16},{1,25},{9,1},{17,9},{25,17},{2,26},{10... | collective-permute-start | bytes 1572872 | tf_op jit(solution)/shard_map/ppermute | solution.py:441
  470.5 22.7 %collective-permute-start.70 = (bf16[2048,128]{1,0:T(8,128)(2,1)S(1)}, bf16[2048,128]{1,0:T(8,128)(2,1)}, u32[]{:S(2)}, u32[]{:S(2)}) collective-permute-start(bf16[2048,128]{1,0:T(8,128)(2,1)S(1)} %pad_maximum_fusion.21), channel_id=1, source_target_pairs={{0,1},{1,0},{2,3},{3,2},{4,5},{5,4},{6,7},{7,6},{8,9},{9,8},{10,11... | collective-permute-start | bytes 1572872 | tf_op jit(solution)/shard_map/ppermute | solution.py:445
  471.7 29.4 %collective-permute-start.64 = (bf16[128,2048]{1,0:T(8,128)(2,1)S(1)}, bf16[128,2048]{1,0:T(8,128)(2,1)S(1)}, u32[]{:S(2)}, u32[]{:S(2)}) collective-permute-start(bf16[128,2048]{1,0:T(8,128)(2,1)S(1)} %get-tuple-element.112), channel_id=1, source_target_pairs={{0,1},{1,0},{2,3},{3,2},{4,5},{5,4},{6,7},{7,6},{8,9},{9,8},{10,11... | collective-permute-start | bytes 1572872 | tf_op jit(solution)/shard_map/ppermute | solution.py:445
  513.3 122.7 %reduce-scatter.15.cloned.1.call-start = ((), (), s32[]{:S(2)}) async-start(), calls=%async_computation.13 | async-start | bytes 1310720 | tf_op jit(solution)/shard_map/reduce_scatter | solution.py:566
  549.1 16.5 %collective-permute-start.72 = (bf16[1024,256]{1,0:T(8,128)(2,1)S(1)}, bf16[1024,256]{1,0:T(8,128)(2,1)S(1)}, u32[]{:S(2)}, u32[]{:S(2)}) collective-permute-start(bf16[1024,256]{1,0:T(8,128)(2,1)S(1)} %pad_maximum_fusion.23), channel_id=1, source_target_pairs={{0,2},{1,3},{2,0},{3,1},{4,6},{5,7},{6,4},{7,5},{8,10},{9,11},{10,... | collective-permute-start | bytes 1572872 | tf_op jit(solution)/shard_map/ppermute | solution.py:445
  555.1 19.7 %collective-permute-start.78 = (bf16[320,640]{1,0:T(8,128)(2,1)S(1)}, bf16[320,640]{1,0:T(8,128)(2,1)S(1)}, u32[]{:S(2)}, u32[]{:S(2)}) collective-permute-start(bf16[320,640]{1,0:T(8,128)(2,1)S(1)} %fusion.58.refs_10_), channel_id=1, source_target_pairs={{0,24},{8,0},{16,8},{24,16},{1,25},{9,1},{17,9},{25,17},{2,26},{10... | collective-permute-start | bytes 1228808 | tf_op jit(solution)/shard_map/ppermute | solution.py:441
  570.2 65.8 %reduce-scatter.17.cloned.1.call-start = ((), (), s32[]{:S(2)}) async-start(), calls=%async_computation.14 | async-start | bytes 1310720 | tf_op jit(solution)/shard_map/reduce_scatter | solution.py:566
  590.0 26.5 %collective-permute-start.81 = (bf16[128,2048]{1,0:T(8,128)(2,1)}, bf16[128,2048]{1,0:T(8,128)(2,1)}, u32[]{:S(2)}, u32[]{:S(2)}) collective-permute-start(bf16[128,2048]{1,0:T(8,128)(2,1)} %get-tuple-element.175), channel_id=1, source_target_pairs={{0,1},{1,0},{2,3},{3,2},{4,5},{5,4},{6,7},{7,6},{8,9},{9,8},{10,11... | collective-permute-start | bytes 1572872 | tf_op jit(solution)/shard_map/ppermute | solution.py:445
  608.5 16.8 %collective-permute-start.85 = (bf16[128,2048]{1,0:T(8,128)(2,1)S(1)}, bf16[128,2048]{1,0:T(8,128)(2,1)S(1)}, u32[]{:S(2)}, u32[]{:S(2)}) collective-permute-start(bf16[128,2048]{1,0:T(8,128)(2,1)S(1)} %pad_maximum_fusion.25), channel_id=1, source_target_pairs={{0,8},{8,16},{16,24},{24,0},{1,9},{9,17},{17,25},{25,1},{2,10},{10... | collective-permute-start | bytes 1572872 | tf_op jit(solution)/shard_map/ppermute | solution.py:441
  612.5 22.0 %collective-permute-start.88 = (bf16[128,2048]{1,0:T(8,128)(2,1)S(1)}, bf16[128,2048]{1,0:T(8,128)(2,1)S(1)}, u32[]{:S(2)}, u32[]{:S(2)}) collective-permute-start(bf16[128,2048]{1,0:T(8,128)(2,1)S(1)} %pad_maximum_fusion.26), channel_id=1, source_target_pairs={{0,24},{8,0},{16,8},{24,16},{1,25},{9,1},{17,9},{25,17},{2,26},{10... | collective-permute-start | bytes 1572872 | tf_op jit(solution)/shard_map/ppermute | solution.py:441
  637.5 47.5 %collective-permute-start.105 = (bf16[256,1024]{1,0:T(8,128)(2,1)S(1)}, bf16[256,1024]{1,0:T(8,128)(2,1)S(1)}, u32[]{:S(2)}, u32[]{:S(2)}) collective-permute-start(bf16[256,1024]{1,0:T(8,128)(2,1)S(1)} %broadcast_select_fusion.8), channel_id=1, source_target_pairs={{0,1},{1,0},{2,3},{3,2},{4,5},{5,4},{6,7},{7,6},{8,9},{9,8},{10,11... | collective-permute-start | bytes 1572872 | tf_op jit(solution)/shard_map/ppermute | solution.py:445
  639.4 58.0 %collective-permute-start.104 = (bf16[256,2048]{1,0:T(8,128)(2,1)S(1)}, bf16[256,2048]{1,0:T(8,128)(2,1)S(1)}, u32[]{:S(2)}, u32[]{:S(2)}) collective-permute-start(bf16[256,2048]{1,0:T(8,128)(2,1)S(1)} %broadcast_select_fusion.4), channel_id=1, source_target_pairs={{0,1},{1,0},{2,3},{3,2},{4,5},{5,4},{6,7},{7,6},{8,9},{9,8},{10,11... | collective-permute-start | bytes 3145736 | tf_op jit(solution)/shard_map/ppermute | solution.py:445
  676.5 24.4 %collective-permute-start.101 = (bf16[128,512]{1,0:T(8,128)(2,1)S(1)}, bf16[128,512]{1,0:T(8,128)(2,1)S(1)}, u32[]{:S(2)}, u32[]{:S(2)}) collective-permute-start(bf16[128,512]{1,0:T(8,128)(2,1)S(1)} %slice.684), channel_id=1, source_target_pairs={{0,8},{8,16},{16,24},{24,0},{1,9},{9,17},{17,25},{25,1},{2,10},{10... | collective-permute-start | bytes 393224 | tf_op jit(solution)/shard_map/ppermute | solution.py:441
  680.8 20.2 %collective-permute-start.103 = (bf16[128,512]{1,0:T(8,128)(2,1)S(1)}, bf16[128,512]{1,0:T(8,128)(2,1)S(1)}, u32[]{:S(2)}, u32[]{:S(2)}) collective-permute-start(bf16[128,512]{1,0:T(8,128)(2,1)S(1)} %slice.685), channel_id=1, source_target_pairs={{0,24},{8,0},{16,8},{24,16},{1,25},{9,1},{17,9},{25,17},{2,26},{10... | collective-permute-start | bytes 393224 | tf_op jit(solution)/shard_map/ppermute | solution.py:441
  685.0 16.0 %collective-permute-start.96 = (bf16[128,512]{1,0:T(8,128)(2,1)S(1)}, bf16[128,512]{1,0:T(8,128)(2,1)S(1)}, u32[]{:S(2)}, u32[]{:S(2)}) collective-permute-start(bf16[128,512]{1,0:T(8,128)(2,1)S(1)} %slice.682), channel_id=1, source_target_pairs={{0,8},{8,16},{16,24},{24,0},{1,9},{9,17},{17,25},{25,1},{2,10},{10... | collective-permute-start | bytes 393224 | tf_op jit(solution)/shard_map/ppermute | solution.py:441
  (156 other events, 2152.0 us)
Sparse Core Ops, SparseCore 0:
  12.8 46.5 all-gather.3
  61.9 30.6 all-gather.5
  94.4 125.8 all-gather.7
  312.1 45.1 reduce-scatter.6
  366.8 54.5 reduce-scatter.8
  424.3 86.3 reduce-scatter.10
  514.6 31.6 reduce-scatter.12
  570.3 24.9 reduce-scatter.14
  599.4 27.2 reduce-scatter.16

commit v4 on v3

--- a/solution.py
+++ b/solution.py
@@ -463,11 +463,12 @@
 
 def scatter_chip(y, *others):
     wide = jnp.float32
-    n = y.shape[0] // 8
-    half = n // 2
+    if not isinstance(y, (list, tuple)):
+        n = y.shape[0] // 8
+        y = [y[k * n : (k + 1) * n] for k in range(8)]
+    half = y[0].shape[0] // 2
     before, own, after, far = (
-        y[k * n : (k + 1) * n].astype(wide) + other_core(y[(k + 4) * n : (k + 5) * n]).astype(wide)
-        for k in range(4)
+        y[k].astype(wide) + other_core(y[k + 4]).astype(wide) for k in range(4)
     )
     far = far.astype(jnp.bfloat16)
     first = along_heads(far[:half], 1).astype(wide)
@@ -577,6 +578,7 @@
 
 
 QUERY_ROWS = 512
+FORWARD_ROWS = 1024
 KEY_ROWS = 512
 
 
@@ -688,9 +690,9 @@
     out_ref, lse_ref, k_all, v_all, total, summed = refs[10:]
     place_both(meta, mine, theirs, k_all, v_all)
     own = q_ref.shape[0]
-    for part in range(own // QUERY_ROWS):
-        rows = pl.ds(part * QUERY_ROWS, QUERY_ROWS)
-        first = meta[0] * own + part * QUERY_ROWS
+    for part in range(own // FORWARD_ROWS):
+        rows = pl.ds(part * FORWARD_ROWS, FORWARD_ROWS)
+        first = meta[0] * own + part * FORWARD_ROWS
         total[...] = jnp.zeros_like(total)
         summed[...] = jnp.zeros_like(summed)
 
@@ -711,7 +713,7 @@
             )
 
         start, full_from = meta[3 + 2 * part], meta[4 + 2 * part]
-        end = (first + QUERY_ROWS - 1) // KEY_ROWS + 1
+        end = (first + FORWARD_ROWS - 1) // KEY_ROWS + 1
         full_from = jnp.minimum(full_from, end)
         full_to = jnp.maximum(jnp.minimum((first + 1) // KEY_ROWS, end), full_from)
 
@@ -840,11 +842,11 @@
         scratch_shapes=[
             pltpu.VMEM((row, width), jnp.bfloat16),
             pltpu.VMEM((row, width), jnp.bfloat16),
-            pltpu.VMEM((QUERY_ROWS, 128), jnp.float32),
-            pltpu.VMEM((QUERY_ROWS, width), jnp.float32),
+            pltpu.VMEM((FORWARD_ROWS, 128), jnp.float32),
+            pltpu.VMEM((FORWARD_ROWS, width), jnp.float32),
         ],
         compiler_params=pltpu.CompilerParams(vmem_limit_bytes=40 << 20),
-        cost_estimate=takes(11),
+        cost_estimate=takes(9),
     )(meta, q, lo.reshape(own, 1), *mine, *theirs)
 
 
@@ -917,7 +919,7 @@
 
 
 TOKEN_ROWS = 16
-COMBINE_TIME = 25
+COMBINE_TIME = 45
 
 
 def scaled(x):
@@ -1165,6 +1167,135 @@
         compiler_params=pltpu.CompilerParams(vmem_limit_bytes=32 << 20),
         cost_estimate=takes(COMBINE_TIME),
     )(merged, attention, lifted, merged_grad, feed_grad, first, gains, early)
+
+
+HIDDEN_TILE = 256
+WIDTH_TILE = 512
+
+
+def gelu_of(x):
+    return gelu_parts(x)[0]
+
+
+def put_pieces(refs, value):
+    rows = refs[0].shape[0]
+    for place, ref in enumerate(refs):
+        ref[...] = value[place * rows : (place + 1) * rows].astype(ref.dtype)
+
+
+def unit_kernel(x_ref, gate_w_ref, up_w_ref, down_w_ref, gate_ref, up_ref, hidden_ref, *refs):
+    *fed_refs, kept = refs
+    step = pl.program_id(0)
+    tiles = kept.shape[0]
+    own = x_ref.shape[0]
+    half = own // CORES
+
+    @pl.when(step < tiles)
+    def _():
+        for part in range(CORES):
+            rows = pl.ds(part * half, half)
+            x = x_ref[rows, :]
+            gate = jnp.dot(x, gate_w_ref[...], preferred_element_type=jnp.float32)
+            up = jnp.dot(x, up_w_ref[...], preferred_element_type=jnp.float32)
+            hidden = (gelu_of(gate) * up).astype(hidden_ref.dtype)
+            gate_ref[rows, :] = gate.astype(gate_ref.dtype)
+            up_ref[rows, :] = up.astype(up_ref.dtype)
+            hidden_ref[rows, :] = hidden
+            kept[step, rows, :] = hidden
+
+    @pl.when(step >= tiles)
+    def _():
+        hidden = jnp.concatenate([kept[tile] for tile in range(tiles)], axis=1)
+        put_pieces(fed_refs, rows_times_rows(hidden, down_w_ref[...]))
+
+
+def unit_back_kernel(
+    grad_ref, gate_ref, up_ref, down_w_ref, two_w_ref, gate_grad_ref, up_grad_ref, *refs
+):
+    *feed_refs, kept = refs
+    step = pl.program_id(0)
+    tiles = kept.shape[0] // 2
+    own = grad_ref.shape[0]
+    half = own // CORES
+
+    @pl.when(step < tiles)
+    def _():
+        for part in range(CORES):
+            rows = pl.ds(part * half, half)
+            grad = jnp.dot(grad_ref[rows, :], down_w_ref[...], preferred_element_type=jnp.float32)
+            gelu, slope = gelu_parts(gate_ref[rows, :].astype(jnp.float32))
+            gate_grad = (grad * up_ref[rows, :].astype(jnp.float32) * slope).astype(gate_grad_ref.dtype)
+            up_grad = (grad * gelu).astype(up_grad_ref.dtype)
+            gate_grad_ref[rows, :] = gate_grad
+            up_grad_ref[rows, :] = up_grad
+            kept[step, rows, :] = gate_grad
+            kept[tiles + step, rows, :] = up_grad
+
+    @pl.when(step >= tiles)
+    def _():
+        both = jnp.concatenate([kept[tile] for tile in range(2 * tiles)], axis=1)
+        put_pieces(feed_refs, rows_times_rows(both, two_w_ref[...]))
+
+
+def unit_here(x, weights):
+    own, width = x.shape
+    hidden = weights.shape[1] // 3
+    tiles, sums = hidden // HIDDEN_TILE, width // WIDTH_TILE
+
+    def tile(first):
+        return pl.BlockSpec((width, HIDDEN_TILE), lambda i: (0, first * tiles + jnp.minimum(i, tiles - 1)))
+
+    saved = pl.BlockSpec((own, HIDDEN_TILE), lambda i: (0, jnp.minimum(i, tiles - 1)))
+    return pl.pallas_call(
+        unit_kernel,
+        grid=(tiles + sums,),
+        out_shape=tuple(
+            jax.ShapeDtypeStruct(shape, jnp.bfloat16)
+            for shape in [(own, hidden)] * 3 + [(own // 8, width)] * 8
+        ),
+        in_specs=[
+            whole(x.shape),
+            tile(0),
+            tile(1),
+            pl.BlockSpec((WIDTH_TILE, hidden), lambda i: (jnp.maximum(i - tiles, 0), 2)),
+        ],
+        out_specs=(
+            *[saved] * 3,
+            *[pl.BlockSpec((own // 8, WIDTH_TILE), lambda i: (0, jnp.maximum(i - tiles, 0)))] * 8,
+        ),
+        scratch_shapes=[pltpu.VMEM((tiles, own, HIDDEN_TILE), jnp.bfloat16)],
+        compiler_params=pltpu.CompilerParams(vmem_limit_bytes=48 << 20),
+        cost_estimate=takes(18),
+    )(x, weights, weights, weights)
+
+
+def unit_back_here(grad, gate, up, weights):
+    own, width = grad.shape
+    hidden = gate.shape[1]
+    tiles, sums = hidden // HIDDEN_TILE, width // WIDTH_TILE
+    saved = pl.BlockSpec((own, HIDDEN_TILE), lambda i: (0, jnp.minimum(i, tiles - 1)))
+    return pl.pallas_call(
+        unit_back_kernel,
+        grid=(tiles + sums,),
+        out_shape=tuple(
+            jax.ShapeDtypeStruct(shape, jnp.bfloat16)
+            for shape in [(own, hidden)] * 2 + [(own // 8, width)] * 8
+        ),
+        in_specs=[
+            whole(grad.shape),
+            saved,
+            saved,
+            pl.BlockSpec((width, HIDDEN_TILE), lambda i: (0, 2 * tiles + jnp.minimum(i, tiles - 1))),
+            pl.BlockSpec((WIDTH_TILE, 2 * hidden), lambda i: (jnp.maximum(i - tiles, 0), 0)),
+        ],
+        out_specs=(
+            *[saved] * 2,
+            *[pl.BlockSpec((own // 8, WIDTH_TILE), lambda i: (0, jnp.maximum(i - tiles, 0)))] * 8,
+        ),
+        scratch_shapes=[pltpu.VMEM((2 * tiles, own, HIDDEN_TILE), jnp.bfloat16)],
+        compiler_params=pltpu.CompilerParams(vmem_limit_bytes=56 << 20),
+        cost_estimate=takes(18),
+    )(grad, gate, up, weights, weights)
 
 
 def assemble_kernel(meta, *refs):
@@ -1393,10 +1524,6 @@
         return jnp.concatenate([pick(w, index * hidden, hidden) for w in unit_weights], axis=1)
 
     unit_full = all_rows(weight_rows(hidden_columns(core), hidden_columns(1 - core), core))
-    unit_two = unit_full[:, : 2 * hidden]
-    unit_gate = unit_full[:, :hidden]
-    unit_up = unit_full[:, hidden : 2 * hidden]
-    unit_down = unit_full[:, 2 * hidden :]
 
     digits = jnp.stack([positions // 128, positions % 128], axis=1).astype(narrow)
     sent = jnp.concatenate([normed_low, jnp.pad(digits, ((0, 0), (0, 126)))], axis=1)
@@ -1412,17 +1539,21 @@
     begin_one = jnp.sum(documents < 1)
     begin_two = jnp.sum(documents < 2)
     lo = jnp.where(row_docs == 0, 0, jnp.where(row_docs == 1, begin_one, begin_two)).astype(jnp.int32)
-    bounds = []
-    for part in range(own // QUERY_ROWS):
-        bounds.append(lo[part * QUERY_ROWS] // KEY_ROWS)
-        bounds.append((lo[(part + 1) * QUERY_ROWS - 1] + KEY_ROWS - 1) // KEY_ROWS)
-    meta = jnp.stack([chip, core, line, *bounds]).astype(jnp.int32)
+
+    def bounds(rows):
+        found = []
+        for start in range(0, own, rows):
+            found.append(lo[start] // KEY_ROWS)
+            found.append((lo[start + rows - 1] + KEY_ROWS - 1) // KEY_ROWS)
+        return jnp.stack([chip, core, line, *found]).astype(jnp.int32)
+
+    meta = bounds(QUERY_ROWS)
     rotated, kv_own, heads_pre = heads_here(meta, gathered, head_full, cosine, sine, head_wide)
     tables = (heads_pre, cosine, sine, head_wide)
     mine = (kv_own, *gather_chips(kv_own))
     theirs = tuple(other_core(part) for part in mine)
 
-    attended, lse = attend_here(meta, rotated, lo, mine, theirs)
+    attended, lse = attend_here(bounds(FORWARD_ROWS), rotated, lo, mine, theirs)
     mixed_rows = arrival(attended.astype(narrow), core, line)
     attention_out = scatter_chip(transposed_product(mixed_rows, out_full).astype(narrow))
 
@@ -1432,11 +1563,8 @@
         predicted[0], attention_out, normed_low.astype(wide), lifted, gain_rows
     )
     unit_rows = gather_chip(feed_in.astype(narrow))
-    hidden_units, pull_activate = jax.vjp(
-        activate, forward_product(unit_rows, unit_gate), forward_product(unit_rows, unit_up)
-    )
-    hidden_low = hidden_units.astype(narrow)
-    fed = scatter_chip(transposed_product(hidden_low, unit_down).astype(narrow))
+    gate_low, up_low, hidden_low, *fed_parts = unit_here(unit_rows, unit_full)
+    fed = scatter_chip(fed_parts)
     def core_columns(x):
         top, bottom = x[:rows_here], x[rows_here:]
         keep = jnp.where(first_core, top, bottom)
@@ -1478,11 +1606,13 @@
     fed_rows = gather_chip(fed_grad)
     fed_rows, io_sum = together(fed_rows, io_sum)
     io_share = share_line(io_sum).astype(narrow)
-    gate_grad, up_grad = pull_activate(forward_product(fed_rows, unit_down))
+    gate_grad, up_grad, *feed_parts = unit_back_here(fed_rows, gate_low, up_low, unit_full)
+    feed_grad = scatter_chip(feed_parts)
     down_sum = own_rows(weight_product(fed_rows, hidden_low).astype(narrow))
-    two_low = jnp.concatenate([gate_grad.astype(narrow), up_grad.astype(narrow)], axis=1)
-    feed_grad = scatter_chip(transposed_product(two_low, unit_two).astype(narrow))
-    two_sum = own_rows(weight_product(unit_rows, two_low).astype(narrow))
+    two_sum = own_rows(
+        weight_product(unit_rows, jnp.concatenate([gate_grad, up_grad], axis=1)).astype(narrow)
+    )
+    feed_grad, down_sum = together(feed_grad, down_sum)
     first_total, active_grad, attention_low, lifted_low, packed_combine = combine_back_here(
         merged, attention_out, lifted, merged_grad, feed_grad, first_grad, gain_rows, packed_middle
     )
@@ -1496,8 +1626,8 @@
         [weight_product(attention_rows, mixed_rows).astype(narrow), laurel_part], axis=1
     )
     mixed_grad_rows = forward_product(attention_rows, out_full).astype(narrow)
-    mixed_grad_rows, down_sum, two_sum, io_share, out_part = together(
-        mixed_grad_rows, down_sum, two_sum, io_share, out_part
+    mixed_grad_rows, two_sum, io_share, out_part = together(
+        mixed_grad_rows, two_sum, io_share, out_part
     )
     out_sum = own_rows(out_part)
     mixed_grad = natural(mixed_grad_rows, core, line)
@@ -1554,6 +1684,7 @@
         coef_wide,
         packed_early,
     )
+    packed, *query_near = together(packed, *query_near)
     packed = butterfly(packed)
     query_far, kv_far = line_far(query_here, *query_near), line_far(kv_here, *kv_near)
     down_first, down_second = core_columns(down_sum)

time: 725 us -> 707 us (0.975)
  matrix products: 103 us -> 49 us
  Pallas kernels: 59.5 us -> 105 us
  waiting for transfers between devices: 318 us -> 299 us
  starting transfers between devices: 101 us -> 109 us
    pallas_call x0 -> x2, Pallas kernels: none -> 44 us  [the longest x1 23 us: unit_back_here(): pl.pallas_call(unit_back_kernel, grid=(tiles + sums,), out_shape=tuple((j...]
    dot_general x6 -> x3, matrix products: 40.3 us -> 7.94 us  [forward_product(): return jnp.dot(left, right, preferred_element_type=jnp.float32)]
    dot_general x6 -> x4, matrix products: 28.4 us -> 7.92 us  [transposed_product(): lax.dot_general(left, right, (((1,), (1,)), ((), ())), preferred_element_...]
    ppermute x47, waiting for transfers between devices: 234 us -> 222 us  [along_heads(): lax.ppermute(x, 'heads', [(i, (i + step) % LINE) for i in range(LINE)])]
    ppermute x57, waiting for transfers between devices: 56.9 us -> 48.9 us  [across_blk(): return lax.ppermute(x, 'blk', [(i, i ^ mask) for i in range(CORES * CHIPS)])]
    ppermute x47, starting transfers between devices: 73.5 us -> 81.3 us  [along_heads(): lax.ppermute(x, 'heads', [(i, (i + step) % LINE) for i in range(LINE)])]
    unnamed x209 -> x197, local copies, waits for them, and re-layouts: 37.6 us -> 37.2 us
  transfers between devices with their start and end apart: 115 -> 115, of which waited for: 69 -> 63; matrix products, arithmetic and copies ran while one was open for 19% -> 17% of each run, Pallas kernels for 5% -> 9%
where the time goes in v4:
time: 707 us; the launch traced here: 697 us
  waiting for transfers between devices  299 us (42%)
  starting transfers between devices  109 us (15%)
  Pallas kernels  105 us (15%)
  other arithmetic  57.3 us (8%)
  local copies, waits for them, and re-layouts  56.1 us (8%)
  matrix products  49 us (7%)
  between operations  22.9 us (3%)
    ppermute x47, waiting for transfers between devices, along_heads(): lax.ppermute(x, 'heads', [(i, (i + step) % LINE) for i in range(LINE)])  222 us
    ppermute x47, starting transfers between devices, along_heads(): lax.ppermute(x, 'heads', [(i, (i + step) % LINE) for i in range(LINE)])  81.3 us
    ppermute x57, waiting for transfers between devices, across_blk(): return lax.ppermute(x, 'blk', [(i, i ^ mask) for i in range(CORES * CHIPS)])  48.9 us
    unnamed x197, local copies, waits for them, and re-layouts  37.2 us
    dot_general x9, matrix products, weight_product(): lax.dot_general(left, right, (((0,), (0,)), ((), ())), preferred_element_...  33.1 us
    ppermute x57, starting transfers between devices, across_blk(): return lax.ppermute(x, 'blk', [(i, i ^ mask) for i in range(CORES * CHIPS)])  24.3 us
    pallas_call x1, Pallas kernels, unit_back_here(): pl.pallas_call(unit_back_kernel, grid=(tiles + sums,), out_shape=tuple((j...  23 us
    pallas_call x1, Pallas kernels, unit_here(): pl.pallas_call(unit_kernel, grid=(tiles + sums,), out_shape=tuple((jax.Sh...  21 us
  transfers between devices with their start and end apart: 115, of which 63 were waited for; matrix products, arithmetic and copies ran while one was open for 17% of the time, Pallas kernels for 9%

profile of v4, /device:TPU:0, one launch (start us, length us, event | category | flops | bytes accessed | tf_op | source)
XLA Modules:
  0.0 697.4 jit_solution(16611424686134619344)
XLA Ops:
  13.7 4.7 shard_map.314
  44.4 4.1 collective-permute-done
  48.6 10.7 %collective-permute-done.1 = bf16[128,2176]{1,0:T(8,128)(2,1)S(1)} collective-permute-done((bf16[128,2176]{1,0:T(8,128)(2,1)S(1)}, bf16[128,2176]{1,0:T(8,128)(2,1)S(1)}, u32[]{:S(2)}, u32[]{:S(2)}) %collective-permute-start.1) | collective-permute-done | bytes 557088 | tf_op jit(solution)/shard_map/ppermute | solution.py:441
  63.0 5.8 collective-permute-done.2
  78.2 6.8 shard_map.315
  90.0 11.7 %collective-permute-done.9.refs_1_ = bf16[1024,256]{1,0:T(8,128)(2,1)S(1)} collective-permute-done((bf16[1024,256]{1,0:T(8,128)(2,1)S(1)}, bf16[1024,256]{1,0:T(8,128)(2,1)S(1)}, u32[]{:S(2)}, u32[]{:S(2)}) %collective-permute-start.9) | collective-permute-done | bytes 524320 | tf_op jit(solution)/shard_map/ppermute | solution.py:445
  104.6 6.8 collective-permute-done.11.refs_3_
  111.4 4.8 collective-permute-done.12.refs_4_
  120.2 4.4 shard_map.316
  138.0 6.9 collective-permute-done.21
  145.2 5.4 collective-permute-done.24
  156.1 5.9 collective-permute-done.22
  162.0 10.4 %collective-permute-done.25 = bf16[128,2048]{1,0:T(8,128)(2,1)} collective-permute-done((bf16[128,2048]{1,0:T(8,128)(2,1)}, bf16[128,2048]{1,0:T(8,128)(2,1)}, u32[]{:S(2)}, u32[]{:S(2)}) %collective-permute-start.25) | collective-permute-done | bytes 524320 | tf_op jit(solution)/shard_map/ppermute | solution.py:441
  181.1 12.8 %collective-permute-done.26 = bf16[128,2048]{1,0:T(8,128)(2,1)S(1)} collective-permute-done((bf16[128,2048]{1,0:T(8,128)(2,1)S(1)}, bf16[128,2048]{1,0:T(8,128)(2,1)S(1)}, u32[]{:S(2)}, u32[]{:S(2)}) %collective-permute-start.26) | collective-permute-done | bytes 524320 | tf_op jit(solution)/shard_map/ppermute | solution.py:441
  194.0 8.7 %collective-permute-done.27 = bf16[128,2048]{1,0:T(8,128)(2,1)S(1)} collective-permute-done((bf16[128,2048]{1,0:T(8,128)(2,1)S(1)}, bf16[128,2048]{1,0:T(8,128)(2,1)S(1)}, u32[]{:S(2)}, u32[]{:S(2)}) %collective-permute-start.27) | collective-permute-done | bytes 524320 | tf_op jit(solution)/shard_map/ppermute | solution.py:441
  210.8 4.3 collective-permute-done.29
  220.3 21.0 %shard_map.317 = (bf16[1024,1024]{1,0:T(8,128)(2,1)}, bf16[1024,1024]{1,0:T(8,128)(2,1)}, bf16[1024,1024]{1,0:T(8,128)(2,1)}, bf16[128,2048]{1,0:T(8,128)(2,1)S(...) custom-call(bf16[1024,2048]{1,0:T(8,128)(2,1)} %constant_dynamic-upd, ...), custom_call_target="tpu_custom_call" | custom-call | flops 17999998976 | bytes 59400000 | tf_op jit(solution)/shard_map/pallas_call | solution.py:1249
  247.8 6.7 collective-permute-done.38
  254.6 4.5 collective-permute-done.41
  261.7 9.6 %collective-permute-done.39 = bf16[128,2048]{1,0:T(8,128)(2,1)S(1)} collective-permute-done((bf16[128,2048]{1,0:T(8,128)(2,1)S(1)}, bf16[128,2048]{1,0:T(8,128)(2,1)S(1)}, u32[]{:S(2)}, u32[]{:S(2)}) %collective-permute-start.39) | collective-permute-done | bytes 524320 | tf_op jit(solution)/shard_map/ppermute | solution.py:441
  271.4 10.5 %collective-permute-done.42 = bf16[128,2048]{1,0:T(8,128)(2,1)S(1)} collective-permute-done((bf16[128,2048]{1,0:T(8,128)(2,1)S(1)}, bf16[128,2048]{1,0:T(8,128)(2,1)S(1)}, u32[]{:S(2)}, u32[]{:S(2)}) %collective-permute-start.42) | collective-permute-done | bytes 524320 | tf_op jit(solution)/shard_map/ppermute | solution.py:441
  282.2 17.1 %shard_map.318 = (bf16[4,128,2048]{2,1,0:T(8,128)(2,1)}, bf16[128,256]{1,0:T(8,128)(2,1)}, bf16[128,2048]{1,0:T(8,128)(2,1)S(1)}, f32[128,2048]{1,0:T(8,128)S(1)...) custom-call(f32[4,20]{1,0:T(4,128)S(1)} %convert_element_type.352.co, ...), custom_call_target="tpu_custom_call" | custom-call | flops 16999999488 | bytes 56100000 | tf_op jit(solution)/shard_map/pallas_call | solution.py:1439
  306.2 13.0 %collective-permute-done.43 = bf16[128,2048]{1,0:T(8,128)(2,1)S(1)} collective-permute-done((bf16[128,2048]{1,0:T(8,128)(2,1)}, bf16[128,2048]{1,0:T(8,128)(2,1)S(1)}, u32[]{:S(2)}, u32[]{:S(2)}) %collective-permute-start.43) | collective-permute-done | bytes 524320 | tf_op jit(solution)/shard_map/ppermute | solution.py:441
  319.3 8.6 %collective-permute-done.44 = bf16[128,2048]{1,0:T(8,128)(2,1)S(1)} collective-permute-done((bf16[128,2048]{1,0:T(8,128)(2,1)}, bf16[128,2048]{1,0:T(8,128)(2,1)S(1)}, u32[]{:S(2)}, u32[]{:S(2)}) %collective-permute-start.44) | collective-permute-done | bytes 524320 | tf_op jit(solution)/shard_map/ppermute | solution.py:441
  336.2 4.1 collective-permute-done.46
  345.3 9.4 %convolution_convert_fusion.3 = bf16[2048,1024]{1,0:T(8,128)(2,1)} fusion(bf16[1024,2048]{1,0:T(8,128)(2,1)} %constant_dynamic-update-slice_fusion.18.grad_ref, bf16[1024,1024]{1,0:T(8,128)(2,1)} %get-tuple-element.152), kind=kOutput, calls=%fused_computation.6 | convolution fusion | flops 4297064448 | bytes 10485760 | tf_op jit(solution)/shard_map/dot_general | solution.py:121
  354.9 23.0 %shard_map.319 = (bf16[1024,1024]{1,0:T(8,128)(2,1)}, bf16[1024,1024]{1,0:T(8,128)(2,1)}, bf16[128,2048]{1,0:T(8,128)(2,1)}, bf16[128,2048]{1,0:T(8,128)(2,1)}, ...) custom-call(bf16[1024,2048]{1,0:T(8,128)(2,1)} %constant_dynamic-upd, ...), custom_call_target="tpu_custom_call" | custom-call | flops 17999998976 | bytes 59400000 | tf_op jit(solution)/shard_map/pallas_call | solution.py:1277
  377.9 14.1 %convolution_convert_fusion = bf16[2048,2048]{1,0:T(8,128)(2,1)} fusion(bf16[1024,2048]{1,0:T(8,128)(2,1)} %constant_dynamic-update-slice_fusion.9.x_ref, bf16[1024,1024]{1,0:T(8,128)(2,1)} %get-tuple-element.159, bf16[1024,1024]{1,0:T(8,128)(2,1)} %get-tuple-element.158), kind=kOutput, calls=%fused_computation | convolution fusion | flops 8602517504 | bytes 16777216 | tf_op jit(solution)/shard_map/dot_general | solution.py:121
  401.1 5.7 collective-permute-done.54
  407.7 4.6 collective-permute-done.57
  420.1 4.5 collective-permute-done.55
  424.7 10.5 %collective-permute-done.58 = bf16[128,2048]{1,0:T(8,128)(2,1)} collective-permute-done((bf16[128,2048]{1,0:T(8,128)(2,1)}, bf16[128,2048]{1,0:T(8,128)(2,1)}, u32[]{:S(2)}, u32[]{:S(2)}) %collective-permute-start.58) | collective-permute-done | bytes 524320 | tf_op jit(solution)/shard_map/ppermute | solution.py:441
  443.1 4.3 shard_map.320
  457.5 7.7 %collective-permute-done.59 = bf16[128,2048]{1,0:T(8,128)(2,1)S(1)} collective-permute-done((bf16[128,2048]{1,0:T(8,128)(2,1)}, bf16[128,2048]{1,0:T(8,128)(2,1)S(1)}, u32[]{:S(2)}, u32[]{:S(2)}) %collective-permute-start.59) | collective-permute-done | bytes 524320 | tf_op jit(solution)/shard_map/ppermute | solution.py:441
  465.4 9.6 %collective-permute-done.60 = bf16[128,2048]{1,0:T(8,128)(2,1)S(1)} collective-permute-done((bf16[128,2048]{1,0:T(8,128)(2,1)}, bf16[128,2048]{1,0:T(8,128)(2,1)S(1)}, u32[]{:S(2)}, u32[]{:S(2)}) %collective-permute-start.60) | collective-permute-done | bytes 524320 | tf_op jit(solution)/shard_map/ppermute | solution.py:441
  482.2 4.8 collective-permute-done.62
  492.3 4.7 convolution_convert_fusion.9
  503.9 8.6 %shard_map.321 = (bf16[1024,256]{1,0:T(8,128)(2,1)S(1)}, f32[1,256]{1,0:T(1,128)S(1)}, bf16[4,1024,256]{2,1,0:T(8,128)(2,1)}, bf16[4,1024,256]{2,1,0:T(8,128)(2,1)}) custom-call(s32[7]{0:T(128)S(1)} %copy-done.28, bf16[1024,256]{1,0:T(8,128)(2,1)S(1)} %copy-done.48, bf16[1024,256]{1,0:T(8,128)(2,1)S(1)} %pad_maximum_fusion.19.grad_ref, ...), custom_call_target="tpu_custom_call" | custom-call | flops 20500000768 | bytes 67650000 | tf_op jit(solution)/shard_map/pallas_call | solution.py:856
  513.3 4.6 fusion.7
  521.4 11.9 %reduce-scatter.13.cloned.1.call-done = bf16[512,384]{1,0:T(8,128)(2,1)} async-done(((bf16[2048,384]{1,0:T(8,128)(2,1)}), bf16[512,384]{1,0:T(8,128)(2,1)}) %reduce-scatter.13.cloned.1.call-update) | async-done | bytes 393232 | tf_op jit(solution)/shard_map/reduce_scatter | solution.py:567
  544.1 4.9 collective-permute-done.73
  588.9 3.9 collective-permute-done.84
  601.8 8.9 %collective-permute-done.85 = bf16[128,2048]{1,0:T(8,128)(2,1)S(1)} collective-permute-done((bf16[128,2048]{1,0:T(8,128)(2,1)S(1)}, bf16[128,2048]{1,0:T(8,128)(2,1)S(1)}, u32[]{:S(2)}, u32[]{:S(2)}) %collective-permute-start.85) | collective-permute-done | bytes 524320 | tf_op jit(solution)/shard_map/ppermute | solution.py:441
  610.8 9.2 %collective-permute-done.88 = bf16[128,2048]{1,0:T(8,128)(2,1)S(1)} collective-permute-done((bf16[128,2048]{1,0:T(8,128)(2,1)S(1)}, bf16[128,2048]{1,0:T(8,128)(2,1)S(1)}, u32[]{:S(2)}, u32[]{:S(2)}) %collective-permute-start.88) | collective-permute-done | bytes 524320 | tf_op jit(solution)/shard_map/ppermute | solution.py:441
  632.3 10.4 %shard_map.323 = (bf16[4,128,2048]{2,1,0:T(8,128)(2,1)}, f32[16,2048]{1,0:T(8,128)S(1)}) custom-call(f32[4,20]{1,0:T(4,128)S(1)} %copy-done.24, bf16[4,128,2048]{2,1,0:T(8,128)(2,1)S(1)} %copy-done.30, f32[128,2048]{1,0:T(8,128)S(1)} %copy-done.50, bf16[4,128,2048]{2,1,0:T(8,128)(2,1)S(1)} %copy-done.31, f32[128,2048]{1,0:T(8,128)S(1)} %convert_add_fusion.normed_ref, ...), custom_call_target="tpu_custom_call" | custom-call | flops 10000000000 | bytes 33000000 | tf_op jit(solution)/shard_map/pallas_call | solution.py:1395
  647.4 4.8 collective-permute-done.93
  662.5 7.9 %collective-permute-done.95 = f32[16,2048]{1,0:T(8,128)S(1)} collective-permute-done((f32[16,2048]{1,0:T(8,128)S(1)}, f32[16,2048]{1,0:T(8,128)S(1)}, u32[]{:S(2)}, u32[]{:S(2)}) %collective-permute-start.95) | collective-permute-done | bytes 131104 | tf_op jit(solution)/shard_map/ppermute | solution.py:548
  672.6 6.0 collective-permute-done.96
  (579 shorter events, 280.9 us)
Async XLA Ops:
  7.3 70.9 %all-gather.4.cloned.1.call-start = ((), (), s32[]{:S(2)}) async-start(), calls=%async_computation.6 | async-start | bytes 3932160 | tf_op jit(solution)/shard_map/all_gather | solution.py:563
  12.7 140.3 %all-gather.6.cloned.1.call-start = ((), (), s32[]{:S(2)}) async-start(), calls=%async_computation.7 | async-start | bytes 2949120 | tf_op jit(solution)/shard_map/all_gather | solution.py:1506
  13.6 206.8 %all-gather.8.cloned.1.call-start = ((), (), s32[]{:S(2)}) async-start(), calls=%async_computation.8 | async-start | bytes 15728640 | tf_op jit(solution)/shard_map/all_gather | solution.py:563
  29.7 315.5 %reduce-scatter.7.cloned.1.call-start = ((), (), s32[]{:S(2)}) async-start(), calls=%async_computation.9 | async-start | bytes 2359296 | tf_op jit(solution)/shard_map/reduce_scatter | solution.py:1597
  30.0 18.5 %collective-permute-start = (bf16[128,2176]{1,0:T(8,128)(2,1)S(1)}, bf16[128,2176]{1,0:T(8,128)(2,1)S(1)}, u32[]{:S(2)}, u32[]{:S(2)}) collective-permute-start(bf16[128,2176]{1,0:T(8,128)(2,1)S(1)} %fusion.23), channel_id=1, source_target_pairs={{0,8},{8,16},{16,24},{24,0},{1,9},{9,17},{17,25},{25,1},{2,10},{10... | collective-permute-start | bytes 1671176 | tf_op jit(solution)/shard_map/ppermute | solution.py:441
  33.0 26.3 %collective-permute-start.1 = (bf16[128,2176]{1,0:T(8,128)(2,1)S(1)}, bf16[128,2176]{1,0:T(8,128)(2,1)S(1)}, u32[]{:S(2)}, u32[]{:S(2)}) collective-permute-start(bf16[128,2176]{1,0:T(8,128)(2,1)S(1)} %fusion.23), channel_id=1, source_target_pairs={{0,24},{8,0},{16,8},{24,16},{1,25},{9,1},{17,9},{25,17},{2,26},{10... | collective-permute-start | bytes 1671176 | tf_op jit(solution)/shard_map/ppermute | solution.py:441
  35.1 37.0 %collective-permute-start.5 = (bf16[128,2176]{1,0:T(8,128)(2,1)S(1)}, bf16[128,2176]{1,0:T(8,128)(2,1)}, u32[]{:S(2)}, u32[]{:S(2)}) collective-permute-start(bf16[128,2176]{1,0:T(8,128)(2,1)S(1)} %fusion.23), channel_id=1, source_target_pairs={{0,1},{1,0},{2,3},{3,2},{4,5},{5,4},{6,7},{7,6},{8,9},{9,8},{10,11... | collective-permute-start | bytes 1671176 | tf_op jit(solution)/shard_map/ppermute | solution.py:445
  48.5 20.3 %collective-permute-start.2 = (bf16[64,2176]{1,0:T(8,128)(2,1)S(1)}, bf16[64,2176]{1,0:T(8,128)(2,1)S(1)}, u32[]{:S(2)}, u32[]{:S(2)}) collective-permute-start(bf16[64,2176]{1,0:T(8,128)(2,1)S(1)} %slice.505), channel_id=1, source_target_pairs={{0,8},{8,16},{16,24},{24,0},{1,9},{9,17},{17,25},{25,1},{2,10},{10... | collective-permute-start | bytes 835592 | tf_op jit(solution)/shard_map/ppermute | solution.py:441
  90.0 26.5 %collective-permute-start.13 = (bf16[1024,256]{1,0:T(8,128)(2,1)S(1)}, bf16[1024,256]{1,0:T(8,128)(2,1)S(1)}, u32[]{:S(2)}, u32[]{:S(2)}) collective-permute-start(bf16[1024,256]{1,0:T(8,128)(2,1)S(1)} %get-tuple-element.121.refs_0_), channel_id=1, source_target_pairs={{0,1},{1,0},{2,3},{3,2},{4,5},{5,4},{6,7},{7,6},{8,9},{9,8},{10,11... | collective-permute-start | bytes 1572872 | tf_op jit(solution)/shard_map/ppermute | solution.py:445
  135.5 20.6 %collective-permute-start.18 = (bf16[128,2048]{1,0:T(8,128)(2,1)}, bf16[128,2048]{1,0:T(8,128)(2,1)}, u32[]{:S(2)}, u32[]{:S(2)}) collective-permute-start(bf16[128,2048]{1,0:T(8,128)(2,1)} %get-tuple-element.234), channel_id=1, source_target_pairs={{0,1},{1,0},{2,3},{3,2},{4,5},{5,4},{6,7},{7,6},{8,9},{9,8},{10,11... | collective-permute-start | bytes 1572872 | tf_op jit(solution)/shard_map/ppermute | solution.py:445
  145.1 16.9 %collective-permute-start.22 = (bf16[128,2048]{1,0:T(8,128)(2,1)S(1)}, bf16[128,2048]{1,0:T(8,128)(2,1)}, u32[]{:S(2)}, u32[]{:S(2)}) collective-permute-start(bf16[128,2048]{1,0:T(8,128)(2,1)S(1)} %pad_maximum_fusion.9), channel_id=1, source_target_pairs={{0,8},{8,16},{16,24},{24,0},{1,9},{9,17},{17,25},{25,1},{2,10},{10... | collective-permute-start | bytes 1572872 | tf_op jit(solution)/shard_map/ppermute | solution.py:441
  151.4 21.0 %collective-permute-start.25 = (bf16[128,2048]{1,0:T(8,128)(2,1)}, bf16[128,2048]{1,0:T(8,128)(2,1)}, u32[]{:S(2)}, u32[]{:S(2)}) collective-permute-start(bf16[128,2048]{1,0:T(8,128)(2,1)} %pad_maximum_fusion.10), channel_id=1, source_target_pairs={{0,24},{8,0},{16,8},{24,16},{1,25},{9,1},{17,9},{25,17},{2,26},{10... | collective-permute-start | bytes 1572872 | tf_op jit(solution)/shard_map/ppermute | solution.py:441
  177.3 16.6 %collective-permute-start.26 = (bf16[128,2048]{1,0:T(8,128)(2,1)S(1)}, bf16[128,2048]{1,0:T(8,128)(2,1)S(1)}, u32[]{:S(2)}, u32[]{:S(2)}) collective-permute-start(bf16[128,2048]{1,0:T(8,128)(2,1)S(1)} %get-tuple-element.257), channel_id=1, source_target_pairs={{0,8},{8,16},{16,24},{24,0},{1,9},{9,17},{17,25},{25,1},{2,10},{10... | collective-permute-start | bytes 1572872 | tf_op jit(solution)/shard_map/ppermute | solution.py:441
  177.9 24.8 %collective-permute-start.27 = (bf16[128,2048]{1,0:T(8,128)(2,1)S(1)}, bf16[128,2048]{1,0:T(8,128)(2,1)S(1)}, u32[]{:S(2)}, u32[]{:S(2)}) collective-permute-start(bf16[128,2048]{1,0:T(8,128)(2,1)S(1)} %get-tuple-element.257), channel_id=1, source_target_pairs={{0,24},{8,0},{16,8},{24,16},{1,25},{9,1},{17,9},{25,17},{2,26},{10... | collective-permute-start | bytes 1572872 | tf_op jit(solution)/shard_map/ppermute | solution.py:441
  181.1 36.4 %collective-permute-start.31 = (bf16[128,2048]{1,0:T(8,128)(2,1)S(1)}, bf16[128,2048]{1,0:T(8,128)(2,1)S(1)}, u32[]{:S(2)}, u32[]{:S(2)}) collective-permute-start(bf16[128,2048]{1,0:T(8,128)(2,1)S(1)} %get-tuple-element.257), channel_id=1, source_target_pairs={{0,1},{1,0},{2,3},{3,2},{4,5},{5,4},{6,7},{7,6},{8,9},{9,8},{10,11... | collective-permute-start | bytes 1572872 | tf_op jit(solution)/shard_map/ppermute | solution.py:445
  194.0 16.9 %collective-permute-start.28 = (bf16[64,2048]{1,0:T(8,128)(2,1)S(1)}, bf16[64,2048]{1,0:T(8,128)(2,1)S(1)}, u32[]{:S(2)}, u32[]{:S(2)}) collective-permute-start(bf16[64,2048]{1,0:T(8,128)(2,1)S(1)} %slice.536), channel_id=1, source_target_pairs={{0,8},{8,16},{16,24},{24,0},{1,9},{9,17},{17,25},{25,1},{2,10},{10... | collective-permute-start | bytes 786440 | tf_op jit(solution)/shard_map/ppermute | solution.py:441
  242.1 19.7 %collective-permute-start.35 = (bf16[128,2048]{1,0:T(8,128)(2,1)S(1)}, bf16[128,2048]{1,0:T(8,128)(2,1)S(1)}, u32[]{:S(2)}, u32[]{:S(2)}) collective-permute-start(bf16[128,2048]{1,0:T(8,128)(2,1)S(1)} %get-tuple-element.127), channel_id=1, source_target_pairs={{0,1},{1,0},{2,3},{3,2},{4,5},{5,4},{6,7},{7,6},{8,9},{9,8},{10,11... | collective-permute-start | bytes 1572872 | tf_op jit(solution)/shard_map/ppermute | solution.py:445
  254.6 16.8 %collective-permute-start.39 = (bf16[128,2048]{1,0:T(8,128)(2,1)S(1)}, bf16[128,2048]{1,0:T(8,128)(2,1)S(1)}, u32[]{:S(2)}, u32[]{:S(2)}) collective-permute-start(bf16[128,2048]{1,0:T(8,128)(2,1)S(1)} %pad_maximum_fusion.12), channel_id=1, source_target_pairs={{0,8},{8,16},{16,24},{24,0},{1,9},{9,17},{17,25},{25,1},{2,10},{10... | collective-permute-start | bytes 1572872 | tf_op jit(solution)/shard_map/ppermute | solution.py:441
  259.3 22.6 %collective-permute-start.42 = (bf16[128,2048]{1,0:T(8,128)(2,1)S(1)}, bf16[128,2048]{1,0:T(8,128)(2,1)S(1)}, u32[]{:S(2)}, u32[]{:S(2)}) collective-permute-start(bf16[128,2048]{1,0:T(8,128)(2,1)S(1)} %pad_maximum_fusion.13), channel_id=1, source_target_pairs={{0,24},{8,0},{16,8},{24,16},{1,25},{9,1},{17,9},{25,17},{2,26},{10... | collective-permute-start | bytes 1572872 | tf_op jit(solution)/shard_map/ppermute | solution.py:441
  302.3 135.8 %reduce-scatter.9.cloned.1.call-start = ((), (), s32[]{:S(2)}) async-start(), calls=%async_computation.10 | async-start | bytes 5242880 | tf_op jit(solution)/shard_map/reduce_scatter | solution.py:567
  302.4 16.9 %collective-permute-start.43 = (bf16[128,2048]{1,0:T(8,128)(2,1)}, bf16[128,2048]{1,0:T(8,128)(2,1)S(1)}, u32[]{:S(2)}, u32[]{:S(2)}) collective-permute-start(bf16[128,2048]{1,0:T(8,128)(2,1)} %copy-done.7), channel_id=1, source_target_pairs={{0,8},{8,16},{16,24},{24,0},{1,9},{9,17},{17,25},{25,1},{2,10},{10... | collective-permute-start | bytes 1572872 | tf_op jit(solution)/shard_map/ppermute | solution.py:441
  303.0 25.0 %collective-permute-start.44 = (bf16[128,2048]{1,0:T(8,128)(2,1)}, bf16[128,2048]{1,0:T(8,128)(2,1)S(1)}, u32[]{:S(2)}, u32[]{:S(2)}) collective-permute-start(bf16[128,2048]{1,0:T(8,128)(2,1)} %copy-done.7), channel_id=1, source_target_pairs={{0,24},{8,0},{16,8},{24,16},{1,25},{9,1},{17,9},{25,17},{2,26},{10... | collective-permute-start | bytes 1572872 | tf_op jit(solution)/shard_map/ppermute | solution.py:441
  306.2 36.5 %collective-permute-start.48 = (bf16[128,2048]{1,0:T(8,128)(2,1)}, bf16[128,2048]{1,0:T(8,128)(2,1)S(1)}, u32[]{:S(2)}, u32[]{:S(2)}) collective-permute-start(bf16[128,2048]{1,0:T(8,128)(2,1)} %copy-done.7), channel_id=1, source_target_pairs={{0,1},{1,0},{2,3},{3,2},{4,5},{5,4},{6,7},{7,6},{8,9},{9,8},{10,11... | collective-permute-start | bytes 1572872 | tf_op jit(solution)/shard_map/ppermute | solution.py:445
  319.3 16.9 %collective-permute-start.45 = (bf16[64,2048]{1,0:T(8,128)(2,1)S(1)}, bf16[64,2048]{1,0:T(8,128)(2,1)S(1)}, u32[]{:S(2)}, u32[]{:S(2)}) collective-permute-start(bf16[64,2048]{1,0:T(8,128)(2,1)S(1)} %slice.544), channel_id=1, source_target_pairs={{0,8},{8,16},{16,24},{24,0},{1,9},{9,17},{17,25},{25,1},{2,10},{10... | collective-permute-start | bytes 786440 | tf_op jit(solution)/shard_map/ppermute | solution.py:441
  354.7 143.9 %reduce-scatter.11.cloned.1.call-start = ((), (), s32[]{:S(2)}) async-start(), calls=%async_computation.11 | async-start | bytes 10485760 | tf_op jit(solution)/shard_map/reduce_scatter | solution.py:567
  392.1 141.3 %reduce-scatter.13.cloned.1.call-start = ((), (), s32[]{:S(2)}) async-start(), calls=%async_computation.12 | async-start | bytes 1966080 | tf_op jit(solution)/shard_map/reduce_scatter | solution.py:567
  393.2 24.2 %collective-permute-start.51 = (bf16[128,2048]{1,0:T(8,128)(2,1)}, bf16[128,2048]{1,0:T(8,128)(2,1)}, u32[]{:S(2)}, u32[]{:S(2)}) collective-permute-start(bf16[128,2048]{1,0:T(8,128)(2,1)} %get-tuple-element.145), channel_id=1, source_target_pairs={{0,1},{1,0},{2,3},{3,2},{4,5},{5,4},{6,7},{7,6},{8,9},{9,8},{10,11... | collective-permute-start | bytes 1572872 | tf_op jit(solution)/shard_map/ppermute | solution.py:445
  407.7 17.0 %collective-permute-start.55 = (bf16[128,2048]{1,0:T(8,128)(2,1)}, bf16[128,2048]{1,0:T(8,128)(2,1)}, u32[]{:S(2)}, u32[]{:S(2)}) collective-permute-start(bf16[128,2048]{1,0:T(8,128)(2,1)} %pad_maximum_fusion.15), channel_id=1, source_target_pairs={{0,8},{8,16},{16,24},{24,0},{1,9},{9,17},{17,25},{25,1},{2,10},{10... | collective-permute-start | bytes 1572872 | tf_op jit(solution)/shard_map/ppermute | solution.py:441
  413.2 22.0 %collective-permute-start.58 = (bf16[128,2048]{1,0:T(8,128)(2,1)}, bf16[128,2048]{1,0:T(8,128)(2,1)}, u32[]{:S(2)}, u32[]{:S(2)}) collective-permute-start(bf16[128,2048]{1,0:T(8,128)(2,1)} %pad_maximum_fusion.16), channel_id=1, source_target_pairs={{0,24},{8,0},{16,8},{24,16},{1,25},{9,1},{17,9},{25,17},{2,26},{10... | collective-permute-start | bytes 1572872 | tf_op jit(solution)/shard_map/ppermute | solution.py:441
  416.3 39.4 %collective-permute-start.67 = (bf16[64,512]{1,0:T(8,128)(2,1)}, bf16[64,512]{1,0:T(8,128)(2,1)S(1)}, u32[]{:S(2)}, u32[]{:S(2)}) collective-permute-start(bf16[64,512]{1,0:T(8,128)(2,1)} %get-tuple-element.295), channel_id=1, source_target_pairs={{0,8},{8,16},{16,24},{24,0},{1,9},{9,17},{17,25},{25,1},{2,10},{10... | collective-permute-start | bytes 196616 | tf_op jit(solution)/shard_map/ppermute | solution.py:441
  416.8 39.2 %collective-permute-start.68 = (bf16[64,512]{1,0:T(8,128)(2,1)}, bf16[64,512]{1,0:T(8,128)(2,1)}, u32[]{:S(2)}, u32[]{:S(2)}) collective-permute-start(bf16[64,512]{1,0:T(8,128)(2,1)} %get-tuple-element.297), channel_id=1, source_target_pairs={{0,16},{8,24},{16,0},{24,8},{1,17},{9,25},{17,1},{25,9},{2,18},{10... | collective-permute-start | bytes 196616 | tf_op jit(solution)/shard_map/ppermute | solution.py:441
  417.4 38.6 %collective-permute-start.69 = (bf16[64,512]{1,0:T(8,128)(2,1)}, bf16[64,512]{1,0:T(8,128)(2,1)}, u32[]{:S(2)}, u32[]{:S(2)}) collective-permute-start(bf16[64,512]{1,0:T(8,128)(2,1)} %get-tuple-element.296), channel_id=1, source_target_pairs={{0,24},{8,0},{16,8},{24,16},{1,25},{9,1},{17,9},{25,17},{2,26},{10... | collective-permute-start | bytes 196616 | tf_op jit(solution)/shard_map/ppermute | solution.py:441
  448.5 16.8 %collective-permute-start.59 = (bf16[128,2048]{1,0:T(8,128)(2,1)}, bf16[128,2048]{1,0:T(8,128)(2,1)S(1)}, u32[]{:S(2)}, u32[]{:S(2)}) collective-permute-start(bf16[128,2048]{1,0:T(8,128)(2,1)} %get-tuple-element.157), channel_id=1, source_target_pairs={{0,8},{8,16},{16,24},{24,0},{1,9},{9,17},{17,25},{25,1},{2,10},{10... | collective-permute-start | bytes 1572872 | tf_op jit(solution)/shard_map/ppermute | solution.py:441
  449.7 25.2 %collective-permute-start.60 = (bf16[128,2048]{1,0:T(8,128)(2,1)}, bf16[128,2048]{1,0:T(8,128)(2,1)S(1)}, u32[]{:S(2)}, u32[]{:S(2)}) collective-permute-start(bf16[128,2048]{1,0:T(8,128)(2,1)} %get-tuple-element.157), channel_id=1, source_target_pairs={{0,24},{8,0},{16,8},{24,16},{1,25},{9,1},{17,9},{25,17},{2,26},{10... | collective-permute-start | bytes 1572872 | tf_op jit(solution)/shard_map/ppermute | solution.py:441
  455.7 22.2 %collective-permute-start.70 = (bf16[2048,128]{1,0:T(8,128)(2,1)S(1)}, bf16[2048,128]{1,0:T(8,128)(2,1)}, u32[]{:S(2)}, u32[]{:S(2)}) collective-permute-start(bf16[2048,128]{1,0:T(8,128)(2,1)S(1)} %pad_maximum_fusion.18), channel_id=1, source_target_pairs={{0,1},{1,0},{2,3},{3,2},{4,5},{5,4},{6,7},{7,6},{8,9},{9,8},{10,11... | collective-permute-start | bytes 1572872 | tf_op jit(solution)/shard_map/ppermute | solution.py:445
  457.0 30.3 %collective-permute-start.64 = (bf16[128,2048]{1,0:T(8,128)(2,1)}, bf16[128,2048]{1,0:T(8,128)(2,1)S(1)}, u32[]{:S(2)}, u32[]{:S(2)}) collective-permute-start(bf16[128,2048]{1,0:T(8,128)(2,1)} %get-tuple-element.157), channel_id=1, source_target_pairs={{0,1},{1,0},{2,3},{3,2},{4,5},{5,4},{6,7},{7,6},{8,9},{9,8},{10,11... | collective-permute-start | bytes 1572872 | tf_op jit(solution)/shard_map/ppermute | solution.py:445
  465.3 16.9 %collective-permute-start.61 = (bf16[64,2048]{1,0:T(8,128)(2,1)S(1)}, bf16[64,2048]{1,0:T(8,128)(2,1)S(1)}, u32[]{:S(2)}, u32[]{:S(2)}) collective-permute-start(bf16[64,2048]{1,0:T(8,128)(2,1)S(1)} %slice.552), channel_id=1, source_target_pairs={{0,8},{8,16},{16,24},{24,0},{1,9},{9,17},{17,25},{25,1},{2,10},{10... | collective-permute-start | bytes 786440 | tf_op jit(solution)/shard_map/ppermute | solution.py:441
  500.6 120.9 %reduce-scatter.15.cloned.1.call-start = ((), (), s32[]{:S(2)}) async-start(), calls=%async_computation.13 | async-start | bytes 1310720 | tf_op jit(solution)/shard_map/reduce_scatter | solution.py:567
  541.0 19.7 %collective-permute-start.78 = (bf16[320,640]{1,0:T(8,128)(2,1)S(1)}, bf16[320,640]{1,0:T(8,128)(2,1)S(1)}, u32[]{:S(2)}, u32[]{:S(2)}) collective-permute-start(bf16[320,640]{1,0:T(8,128)(2,1)S(1)} %fusion.42.refs_10_), channel_id=1, source_target_pairs={{0,24},{8,0},{16,8},{24,16},{1,25},{9,1},{17,9},{25,17},{2,26},{10... | collective-permute-start | bytes 1228808 | tf_op jit(solution)/shard_map/ppermute | solution.py:441
  556.0 65.6 %reduce-scatter.17.cloned.1.call-start = ((), (), s32[]{:S(2)}) async-start(), calls=%async_computation.14 | async-start | bytes 1310720 | tf_op jit(solution)/shard_map/reduce_scatter | solution.py:567
  575.5 26.3 %collective-permute-start.81 = (bf16[128,2048]{1,0:T(8,128)(2,1)}, bf16[128,2048]{1,0:T(8,128)(2,1)}, u32[]{:S(2)}, u32[]{:S(2)}) collective-permute-start(bf16[128,2048]{1,0:T(8,128)(2,1)} %get-tuple-element.223), channel_id=1, source_target_pairs={{0,1},{1,0},{2,3},{3,2},{4,5},{5,4},{6,7},{7,6},{8,9},{9,8},{10,11... | collective-permute-start | bytes 1572872 | tf_op jit(solution)/shard_map/ppermute | solution.py:445
  594.0 16.8 %collective-permute-start.85 = (bf16[128,2048]{1,0:T(8,128)(2,1)S(1)}, bf16[128,2048]{1,0:T(8,128)(2,1)S(1)}, u32[]{:S(2)}, u32[]{:S(2)}) collective-permute-start(bf16[128,2048]{1,0:T(8,128)(2,1)S(1)} %pad_maximum_fusion.22), channel_id=1, source_target_pairs={{0,8},{8,16},{16,24},{24,0},{1,9},{9,17},{17,25},{25,1},{2,10},{10... | collective-permute-start | bytes 1572872 | tf_op jit(solution)/shard_map/ppermute | solution.py:441
  598.0 22.0 %collective-permute-start.88 = (bf16[128,2048]{1,0:T(8,128)(2,1)S(1)}, bf16[128,2048]{1,0:T(8,128)(2,1)S(1)}, u32[]{:S(2)}, u32[]{:S(2)}) collective-permute-start(bf16[128,2048]{1,0:T(8,128)(2,1)S(1)} %pad_maximum_fusion.23), channel_id=1, source_target_pairs={{0,24},{8,0},{16,8},{24,16},{1,25},{9,1},{17,9},{25,17},{2,26},{10... | collective-permute-start | bytes 1572872 | tf_op jit(solution)/shard_map/ppermute | solution.py:441
  623.0 37.3 %collective-permute-start.105 = (bf16[256,1024]{1,0:T(8,128)(2,1)S(1)}, bf16[256,1024]{1,0:T(8,128)(2,1)S(1)}, u32[]{:S(2)}, u32[]{:S(2)}) collective-permute-start(bf16[256,1024]{1,0:T(8,128)(2,1)S(1)} %broadcast_select_fusion.8), channel_id=1, source_target_pairs={{0,1},{1,0},{2,3},{3,2},{4,5},{5,4},{6,7},{7,6},{8,9},{9,8},{10,11... | collective-permute-start | bytes 1572872 | tf_op jit(solution)/shard_map/ppermute | solution.py:445
  625.2 55.6 %collective-permute-start.104 = (bf16[256,2048]{1,0:T(8,128)(2,1)S(1)}, bf16[256,2048]{1,0:T(8,128)(2,1)S(1)}, u32[]{:S(2)}, u32[]{:S(2)}) collective-permute-start(bf16[256,2048]{1,0:T(8,128)(2,1)S(1)} %broadcast_select_fusion.4), channel_id=1, source_target_pairs={{0,1},{1,0},{2,3},{3,2},{4,5},{5,4},{6,7},{7,6},{8,9},{9,8},{10,11... | collective-permute-start | bytes 3145736 | tf_op jit(solution)/shard_map/ppermute | solution.py:445
  653.9 30.4 %collective-permute-start.101 = (bf16[128,512]{1,0:T(8,128)(2,1)S(1)}, bf16[128,512]{1,0:T(8,128)(2,1)S(1)}, u32[]{:S(2)}, u32[]{:S(2)}) collective-permute-start(bf16[128,512]{1,0:T(8,128)(2,1)S(1)} %slice.584), channel_id=1, source_target_pairs={{0,8},{8,16},{16,24},{24,0},{1,9},{9,17},{17,25},{25,1},{2,10},{10... | collective-permute-start | bytes 393224 | tf_op jit(solution)/shard_map/ppermute | solution.py:441
  657.8 26.5 %collective-permute-start.103 = (bf16[128,512]{1,0:T(8,128)(2,1)S(1)}, bf16[128,512]{1,0:T(8,128)(2,1)S(1)}, u32[]{:S(2)}, u32[]{:S(2)}) collective-permute-start(bf16[128,512]{1,0:T(8,128)(2,1)S(1)} %slice.585), channel_id=1, source_target_pairs={{0,24},{8,0},{16,8},{24,16},{1,25},{9,1},{17,9},{25,17},{2,26},{10... | collective-permute-start | bytes 393224 | tf_op jit(solution)/shard_map/ppermute | solution.py:441
  660.3 24.0 %collective-permute-start.97 = (bf16[128,512]{1,0:T(8,128)(2,1)S(1)}, bf16[128,512]{1,0:T(8,128)(2,1)S(1)}, u32[]{:S(2)}, u32[]{:S(2)}) collective-permute-start(bf16[128,512]{1,0:T(8,128)(2,1)S(1)} %slice.485), channel_id=1, source_target_pairs={{0,8},{8,16},{16,24},{24,0},{1,9},{9,17},{17,25},{25,1},{2,10},{10... | collective-permute-start | bytes 393224 | tf_op jit(solution)/shard_map/ppermute | solution.py:441
  (150 other events, 1913.8 us)
Sparse Core Ops, SparseCore 0:
  12.8 46.5 all-gather.3
  61.9 30.5 all-gather.5
  94.4 125.9 all-gather.7
  302.4 42.5 reduce-scatter.6
  354.8 54.3 reduce-scatter.8
  412.1 86.3 reduce-scatter.10
  502.4 30.9 reduce-scatter.12
  556.1 25.5 reduce-scatter.14
  585.1 27.7 reduce-scatter.16

commit v5 on v4

--- a/solution.py
+++ b/solution.py
@@ -918,7 +918,7 @@
     )(meta, pre, grad, *others)
 
 
-TOKEN_ROWS = 16
+TOKEN_ROWS = 32
 COMBINE_TIME = 45
 
 
@@ -1164,7 +1164,7 @@
         out_shape=(full, full, low, low, jax.ShapeDtypeStruct(early.shape, jnp.float32)),
         in_specs=[rows] * 6 + [whole(gains.shape), whole(early.shape)],
         out_specs=(rows, rows, rows, rows, whole(early.shape)),
-        compiler_params=pltpu.CompilerParams(vmem_limit_bytes=32 << 20),
+        compiler_params=pltpu.CompilerParams(vmem_limit_bytes=60 << 20),
         cost_estimate=takes(COMBINE_TIME),
     )(merged, attention, lifted, merged_grad, feed_grad, first, gains, early)
 

time: 707 us -> 701 us (level)
  waiting for transfers between devices: 299 us -> 309 us
    unnamed x197 -> x209, local copies, waits for them, and re-layouts: 37.2 us -> 32 us
  transfers between devices with their start and end apart: 115 -> 115, of which waited for: 63 -> 63; matrix products, arithmetic and copies ran while one was open for 17% -> 16% of each run, Pallas kernels for 9% -> 9%
where the time goes in v5:
time: 701 us; the launch traced here: 691 us
  waiting for transfers between devices  309 us (44%)
  starting transfers between devices  103 us (15%)
  Pallas kernels  101 us (14%)
  other arithmetic  51.5 us (7%)
  local copies, waits for them, and re-layouts  51.4 us (7%)
  matrix products  51.1 us (7%)
  between operations  23 us (3%)
    ppermute x47, waiting for transfers between devices, along_heads(): lax.ppermute(x, 'heads', [(i, (i + step) % LINE) for i in range(LINE)])  224 us
    ppermute x47, starting transfers between devices, along_heads(): lax.ppermute(x, 'heads', [(i, (i + step) % LINE) for i in range(LINE)])  78.9 us
    ppermute x57, waiting for transfers between devices, across_blk(): return lax.ppermute(x, 'blk', [(i, i ^ mask) for i in range(CORES * CHIPS)])  50.4 us
    dot_general x9, matrix products, weight_product(): lax.dot_general(left, right, (((0,), (0,)), ((), ())), preferred_element_...  34.9 us
    unnamed x209, local copies, waits for them, and re-layouts  32 us
    pallas_call x1, Pallas kernels, unit_back_here(): pl.pallas_call(unit_back_kernel, grid=(tiles + sums,), out_shape=tuple((j...  23 us
    ppermute x57, starting transfers between devices, across_blk(): return lax.ppermute(x, 'blk', [(i, i ^ mask) for i in range(CORES * CHIPS)])  21.4 us
    pallas_call x1, Pallas kernels, unit_here(): pl.pallas_call(unit_kernel, grid=(tiles + sums,), out_shape=tuple((jax.Sh...  21 us
  transfers between devices with their start and end apart: 115, of which 63 were waited for; matrix products, arithmetic and copies ran while one was open for 16% of the time, Pallas kernels for 9%

profile of v5, /device:TPU:0, one launch (start us, length us, event | category | flops | bytes accessed | tf_op | source)
XLA Modules:
  0.0 690.6 jit_solution(15086581099331691740)
XLA Ops:
  13.8 4.3 shard_map.314
  44.0 4.1 collective-permute-done
  48.2 10.8 %collective-permute-done.1 = bf16[128,2176]{1,0:T(8,128)(2,1)S(1)} collective-permute-done((bf16[128,2176]{1,0:T(8,128)(2,1)S(1)}, bf16[128,2176]{1,0:T(8,128)(2,1)S(1)}, u32[]{:S(2)}, u32[]{:S(2)}) %collective-permute-start.1) | collective-permute-done | bytes 557088 | tf_op jit(solution)/shard_map/ppermute | solution.py:441
  62.7 5.6 collective-permute-done.2
  77.8 6.6 shard_map.315
  89.6 12.1 %collective-permute-done.9.refs_1_ = bf16[1024,256]{1,0:T(8,128)(2,1)S(1)} collective-permute-done((bf16[1024,256]{1,0:T(8,128)(2,1)S(1)}, bf16[1024,256]{1,0:T(8,128)(2,1)S(1)}, u32[]{:S(2)}, u32[]{:S(2)}) %collective-permute-start.9) | collective-permute-done | bytes 524320 | tf_op jit(solution)/shard_map/ppermute | solution.py:445
  104.4 6.2 collective-permute-done.11.refs_3_
  110.6 4.8 collective-permute-done.12.refs_4_
  137.2 6.4 collective-permute-done.21
  144.5 4.6 collective-permute-done.24
  154.2 7.3 %collective-permute-done.22 = bf16[128,2048]{1,0:T(8,128)(2,1)} collective-permute-done((bf16[128,2048]{1,0:T(8,128)(2,1)}, bf16[128,2048]{1,0:T(8,128)(2,1)}, u32[]{:S(2)}, u32[]{:S(2)}) %collective-permute-start.22) | collective-permute-done | bytes 524320 | tf_op jit(solution)/shard_map/ppermute | solution.py:441
  161.5 9.4 %collective-permute-done.25 = bf16[128,2048]{1,0:T(8,128)(2,1)S(1)} collective-permute-done((bf16[128,2048]{1,0:T(8,128)(2,1)S(1)}, bf16[128,2048]{1,0:T(8,128)(2,1)S(1)}, u32[]{:S(2)}, u32[]{:S(2)}) %collective-permute-start.25) | collective-permute-done | bytes 524320 | tf_op jit(solution)/shard_map/ppermute | solution.py:441
  178.9 12.8 %collective-permute-done.26 = bf16[128,2048]{1,0:T(8,128)(2,1)S(1)} collective-permute-done((bf16[128,2048]{1,0:T(8,128)(2,1)S(1)}, bf16[128,2048]{1,0:T(8,128)(2,1)S(1)}, u32[]{:S(2)}, u32[]{:S(2)}) %collective-permute-start.26) | collective-permute-done | bytes 524320 | tf_op jit(solution)/shard_map/ppermute | solution.py:441
  191.8 8.8 %collective-permute-done.27 = bf16[128,2048]{1,0:T(8,128)(2,1)S(1)} collective-permute-done((bf16[128,2048]{1,0:T(8,128)(2,1)S(1)}, bf16[128,2048]{1,0:T(8,128)(2,1)S(1)}, u32[]{:S(2)}, u32[]{:S(2)}) %collective-permute-start.27) | collective-permute-done | bytes 524320 | tf_op jit(solution)/shard_map/ppermute | solution.py:441
  208.6 4.7 collective-permute-done.29
  220.4 21.0 %shard_map.317 = (bf16[1024,1024]{1,0:T(8,128)(2,1)}, bf16[1024,1024]{1,0:T(8,128)(2,1)}, bf16[1024,1024]{1,0:T(8,128)(2,1)}, bf16[128,2048]{1,0:T(8,128)(2,1)S(...) custom-call(bf16[1024,2048]{1,0:T(8,128)(2,1)} %constant_dynamic-upd, ...), custom_call_target="tpu_custom_call" | custom-call | flops 17999998976 | bytes 59400000 | tf_op jit(solution)/shard_map/pallas_call | solution.py:1249
  247.8 6.7 collective-permute-done.38
  254.7 4.6 collective-permute-done.41
  261.8 9.6 %collective-permute-done.39 = bf16[128,2048]{1,0:T(8,128)(2,1)S(1)} collective-permute-done((bf16[128,2048]{1,0:T(8,128)(2,1)S(1)}, bf16[128,2048]{1,0:T(8,128)(2,1)S(1)}, u32[]{:S(2)}, u32[]{:S(2)}) %collective-permute-start.39) | collective-permute-done | bytes 524320 | tf_op jit(solution)/shard_map/ppermute | solution.py:441
  271.4 10.4 %collective-permute-done.42 = bf16[128,2048]{1,0:T(8,128)(2,1)S(1)} collective-permute-done((bf16[128,2048]{1,0:T(8,128)(2,1)S(1)}, bf16[128,2048]{1,0:T(8,128)(2,1)S(1)}, u32[]{:S(2)}, u32[]{:S(2)}) %collective-permute-start.42) | collective-permute-done | bytes 524320 | tf_op jit(solution)/shard_map/ppermute | solution.py:441
  282.2 14.9 %shard_map.318 = (bf16[4,128,2048]{2,1,0:T(8,128)(2,1)}, bf16[128,256]{1,0:T(8,128)(2,1)}, bf16[128,2048]{1,0:T(8,128)(2,1)S(1)}, f32[128,2048]{1,0:T(8,128)S(1)...) custom-call(f32[4,20]{1,0:T(4,128)S(1)} %convert_element_type.352.co, ...), custom_call_target="tpu_custom_call" | custom-call | flops 16999999488 | bytes 56100000 | tf_op jit(solution)/shard_map/pallas_call | solution.py:1439
  303.8 12.8 %collective-permute-done.43 = bf16[128,2048]{1,0:T(8,128)(2,1)S(1)} collective-permute-done((bf16[128,2048]{1,0:T(8,128)(2,1)S(1)}, bf16[128,2048]{1,0:T(8,128)(2,1)S(1)}, u32[]{:S(2)}, u32[]{:S(2)}) %collective-permute-start.43) | collective-permute-done | bytes 524320 | tf_op jit(solution)/shard_map/ppermute | solution.py:441
  316.7 8.6 %collective-permute-done.44 = bf16[128,2048]{1,0:T(8,128)(2,1)S(1)} collective-permute-done((bf16[128,2048]{1,0:T(8,128)(2,1)S(1)}, bf16[128,2048]{1,0:T(8,128)(2,1)S(1)}, u32[]{:S(2)}, u32[]{:S(2)}) %collective-permute-start.44) | collective-permute-done | bytes 524320 | tf_op jit(solution)/shard_map/ppermute | solution.py:441
  333.5 4.2 collective-permute-done.46
  342.7 9.4 %convolution_convert_fusion.3 = bf16[2048,1024]{1,0:T(8,128)(2,1)} fusion(bf16[1024,2048]{1,0:T(8,128)(2,1)} %constant_dynamic-update-slice_fusion.18.grad_ref, bf16[1024,1024]{1,0:T(8,128)(2,1)} %get-tuple-element.152), kind=kOutput, calls=%fused_computation.6 | convolution fusion | flops 4297064448 | bytes 10485760 | tf_op jit(solution)/shard_map/dot_general | solution.py:121
  352.3 23.0 %shard_map.319 = (bf16[1024,1024]{1,0:T(8,128)(2,1)}, bf16[1024,1024]{1,0:T(8,128)(2,1)}, bf16[128,2048]{1,0:T(8,128)(2,1)}, bf16[128,2048]{1,0:T(8,128)(2,1)}, ...) custom-call(bf16[1024,2048]{1,0:T(8,128)(2,1)} %constant_dynamic-upd, ...), custom_call_target="tpu_custom_call" | custom-call | flops 17999998976 | bytes 59400000 | tf_op jit(solution)/shard_map/pallas_call | solution.py:1277
  375.3 14.1 %convolution_convert_fusion = bf16[2048,2048]{1,0:T(8,128)(2,1)} fusion(bf16[1024,2048]{1,0:T(8,128)(2,1)} %constant_dynamic-update-slice_fusion.9.x_ref, bf16[1024,1024]{1,0:T(8,128)(2,1)} %get-tuple-element.159, bf16[1024,1024]{1,0:T(8,128)(2,1)} %get-tuple-element.158), kind=kOutput, calls=%fused_computation | convolution fusion | flops 8602517504 | bytes 16777216 | tf_op jit(solution)/shard_map/dot_general | solution.py:121
  398.1 5.7 collective-permute-done.54
  404.0 5.4 collective-permute-done.57
  416.1 4.7 collective-permute-done.55
  420.8 11.7 %collective-permute-done.58 = bf16[128,2048]{1,0:T(8,128)(2,1)S(1)} collective-permute-done((bf16[128,2048]{1,0:T(8,128)(2,1)S(1)}, bf16[128,2048]{1,0:T(8,128)(2,1)S(1)}, u32[]{:S(2)}, u32[]{:S(2)}) %collective-permute-start.58) | collective-permute-done | bytes 524320 | tf_op jit(solution)/shard_map/ppermute | solution.py:441
  435.2 5.7 shard_map.320
  452.7 5.0 collective-permute-done.59
  457.9 9.0 %collective-permute-done.60 = bf16[128,2048]{1,0:T(8,128)(2,1)S(1)} collective-permute-done((bf16[128,2048]{1,0:T(8,128)(2,1)}, bf16[128,2048]{1,0:T(8,128)(2,1)S(1)}, u32[]{:S(2)}, u32[]{:S(2)}) %collective-permute-start.60) | collective-permute-done | bytes 524320 | tf_op jit(solution)/shard_map/ppermute | solution.py:441
  483.4 4.7 convolution_convert_fusion.9
  488.2 5.5 reduce-scatter.11.cloned.1.call-done
  498.9 8.6 %shard_map.321 = (bf16[1024,256]{1,0:T(8,128)(2,1)S(1)}, f32[1,256]{1,0:T(1,128)S(1)}, bf16[4,1024,256]{2,1,0:T(8,128)(2,1)}, bf16[4,1024,256]{2,1,0:T(8,128)(2,1)}) custom-call(s32[7]{0:T(128)S(1)} %copy-done.23, bf16[1024,256]{1,0:T(8,128)(2,1)S(1)} %copy-done.44, bf16[1024,256]{1,0:T(8,128)(2,1)S(1)} %pad_maximum_fusion.19.grad_ref, ...), custom_call_target="tpu_custom_call" | custom-call | flops 20500000768 | bytes 67650000 | tf_op jit(solution)/shard_map/pallas_call | solution.py:856
  508.2 4.6 fusion.7
  515.6 12.9 %reduce-scatter.13.cloned.1.call-done = bf16[512,384]{1,0:T(8,128)(2,1)} async-done(((bf16[2048,384]{1,0:T(8,128)(2,1)}), bf16[512,384]{1,0:T(8,128)(2,1)}) %reduce-scatter.13.cloned.1.call-update) | async-done | bytes 393232 | tf_op jit(solution)/shard_map/reduce_scatter | solution.py:567
  536.8 7.3 %collective-permute-done.73 = bf16[1024,256]{1,0:T(8,128)(2,1)S(1)} collective-permute-done((bf16[1024,256]{1,0:T(8,128)(2,1)S(1)}, bf16[1024,256]{1,0:T(8,128)(2,1)S(1)}, u32[]{:S(2)}, u32[]{:S(2)}) %collective-permute-start.73) | collective-permute-done | bytes 524320 | tf_op jit(solution)/shard_map/ppermute | solution.py:445
  550.5 4.1 collective-permute-done.78.refs_12_
  581.0 5.0 collective-permute-done.84
  587.2 4.1 collective-permute-done.87
  593.9 10.0 %collective-permute-done.85 = bf16[128,2048]{1,0:T(8,128)(2,1)S(1)} collective-permute-done((bf16[128,2048]{1,0:T(8,128)(2,1)S(1)}, bf16[128,2048]{1,0:T(8,128)(2,1)S(1)}, u32[]{:S(2)}, u32[]{:S(2)}) %collective-permute-start.85) | collective-permute-done | bytes 524320 | tf_op jit(solution)/shard_map/ppermute | solution.py:441
  603.9 9.3 %collective-permute-done.88 = bf16[128,2048]{1,0:T(8,128)(2,1)S(1)} collective-permute-done((bf16[128,2048]{1,0:T(8,128)(2,1)S(1)}, bf16[128,2048]{1,0:T(8,128)(2,1)S(1)}, u32[]{:S(2)}, u32[]{:S(2)}) %collective-permute-start.88) | collective-permute-done | bytes 524320 | tf_op jit(solution)/shard_map/ppermute | solution.py:441
  625.6 8.8 %shard_map.323 = (bf16[4,128,2048]{2,1,0:T(8,128)(2,1)}, f32[16,2048]{1,0:T(8,128)S(1)}) custom-call(f32[4,20]{1,0:T(4,128)S(1)} %copy-done.19, bf16[4,128,2048]{2,1,0:T(8,128)(2,1)S(1)} %copy-done.26, f32[128,2048]{1,0:T(8,128)S(1)} %copy-done.45, bf16[4,128,2048]{2,1,0:T(8,128)(2,1)S(1)} %copy-done.27, f32[128,2048]{1,0:T(8,128)S(1)} %convert_add_fusion.normed_ref, ...), custom_call_target="tpu_custom_call" | custom-call | flops 10000000000 | bytes 33000000 | tf_op jit(solution)/shard_map/pallas_call | solution.py:1395
  655.8 7.8 %collective-permute-done.95 = f32[16,2048]{1,0:T(8,128)S(1)} collective-permute-done((f32[16,2048]{1,0:T(8,128)S(1)}, f32[16,2048]{1,0:T(8,128)S(1)}, u32[]{:S(2)}, u32[]{:S(2)}) %collective-permute-start.95) | collective-permute-done | bytes 131104 | tf_op jit(solution)/shard_map/ppermute | solution.py:548
  665.8 6.0 collective-permute-done.96
  (591 shorter events, 273.9 us)
Async XLA Ops:
  7.3 70.5 %all-gather.4.cloned.1.call-start = ((), (), s32[]{:S(2)}) async-start(), calls=%async_computation.6 | async-start | bytes 3932160 | tf_op jit(solution)/shard_map/all_gather | solution.py:563
  12.7 138.2 %all-gather.6.cloned.1.call-start = ((), (), s32[]{:S(2)}) async-start(), calls=%async_computation.7 | async-start | bytes 2949120 | tf_op jit(solution)/shard_map/all_gather | solution.py:1506
  13.6 206.8 %all-gather.8.cloned.1.call-start = ((), (), s32[]{:S(2)}) async-start(), calls=%async_computation.8 | async-start | bytes 15728640 | tf_op jit(solution)/shard_map/all_gather | solution.py:563
  29.3 313.4 %reduce-scatter.7.cloned.1.call-start = ((), (), s32[]{:S(2)}) async-start(), calls=%async_computation.9 | async-start | bytes 2359296 | tf_op jit(solution)/shard_map/reduce_scatter | solution.py:1597
  29.6 18.5 %collective-permute-start = (bf16[128,2176]{1,0:T(8,128)(2,1)S(1)}, bf16[128,2176]{1,0:T(8,128)(2,1)S(1)}, u32[]{:S(2)}, u32[]{:S(2)}) collective-permute-start(bf16[128,2176]{1,0:T(8,128)(2,1)S(1)} %fusion.23), channel_id=1, source_target_pairs={{0,8},{8,16},{16,24},{24,0},{1,9},{9,17},{17,25},{25,1},{2,10},{10... | collective-permute-start | bytes 1671176 | tf_op jit(solution)/shard_map/ppermute | solution.py:441
  32.7 26.3 %collective-permute-start.1 = (bf16[128,2176]{1,0:T(8,128)(2,1)S(1)}, bf16[128,2176]{1,0:T(8,128)(2,1)S(1)}, u32[]{:S(2)}, u32[]{:S(2)}) collective-permute-start(bf16[128,2176]{1,0:T(8,128)(2,1)S(1)} %fusion.23), channel_id=1, source_target_pairs={{0,24},{8,0},{16,8},{24,16},{1,25},{9,1},{17,9},{25,17},{2,26},{10... | collective-permute-start | bytes 1671176 | tf_op jit(solution)/shard_map/ppermute | solution.py:441
  34.7 37.1 %collective-permute-start.5 = (bf16[128,2176]{1,0:T(8,128)(2,1)S(1)}, bf16[128,2176]{1,0:T(8,128)(2,1)}, u32[]{:S(2)}, u32[]{:S(2)}) collective-permute-start(bf16[128,2176]{1,0:T(8,128)(2,1)S(1)} %fusion.23), channel_id=1, source_target_pairs={{0,1},{1,0},{2,3},{3,2},{4,5},{5,4},{6,7},{7,6},{8,9},{9,8},{10,11... | collective-permute-start | bytes 1671176 | tf_op jit(solution)/shard_map/ppermute | solution.py:445
  48.1 20.1 %collective-permute-start.2 = (bf16[64,2176]{1,0:T(8,128)(2,1)S(1)}, bf16[64,2176]{1,0:T(8,128)(2,1)S(1)}, u32[]{:S(2)}, u32[]{:S(2)}) collective-permute-start(bf16[64,2176]{1,0:T(8,128)(2,1)S(1)} %slice.505), channel_id=1, source_target_pairs={{0,8},{8,16},{16,24},{24,0},{1,9},{9,17},{17,25},{25,1},{2,10},{10... | collective-permute-start | bytes 835592 | tf_op jit(solution)/shard_map/ppermute | solution.py:441
  89.6 26.9 %collective-permute-start.13 = (bf16[1024,256]{1,0:T(8,128)(2,1)S(1)}, bf16[1024,256]{1,0:T(8,128)(2,1)}, u32[]{:S(2)}, u32[]{:S(2)}) collective-permute-start(bf16[1024,256]{1,0:T(8,128)(2,1)S(1)} %get-tuple-element.121.refs_0_), channel_id=1, source_target_pairs={{0,1},{1,0},{2,3},{3,2},{4,5},{5,4},{6,7},{7,6},{8,9},{9,8},{10,11... | collective-permute-start | bytes 1572872 | tf_op jit(solution)/shard_map/ppermute | solution.py:445
  134.7 19.5 %collective-permute-start.18 = (bf16[128,2048]{1,0:T(8,128)(2,1)}, bf16[128,2048]{1,0:T(8,128)(2,1)}, u32[]{:S(2)}, u32[]{:S(2)}) collective-permute-start(bf16[128,2048]{1,0:T(8,128)(2,1)} %get-tuple-element.234), channel_id=1, source_target_pairs={{0,1},{1,0},{2,3},{3,2},{4,5},{5,4},{6,7},{7,6},{8,9},{9,8},{10,11... | collective-permute-start | bytes 1572872 | tf_op jit(solution)/shard_map/ppermute | solution.py:445
  144.5 17.0 %collective-permute-start.22 = (bf16[128,2048]{1,0:T(8,128)(2,1)}, bf16[128,2048]{1,0:T(8,128)(2,1)}, u32[]{:S(2)}, u32[]{:S(2)}) collective-permute-start(bf16[128,2048]{1,0:T(8,128)(2,1)} %pad_maximum_fusion.9), channel_id=1, source_target_pairs={{0,8},{8,16},{16,24},{24,0},{1,9},{9,17},{17,25},{25,1},{2,10},{10... | collective-permute-start | bytes 1572872 | tf_op jit(solution)/shard_map/ppermute | solution.py:441
  149.2 21.6 %collective-permute-start.25 = (bf16[128,2048]{1,0:T(8,128)(2,1)S(1)}, bf16[128,2048]{1,0:T(8,128)(2,1)S(1)}, u32[]{:S(2)}, u32[]{:S(2)}) collective-permute-start(bf16[128,2048]{1,0:T(8,128)(2,1)S(1)} %pad_maximum_fusion.10), channel_id=1, source_target_pairs={{0,24},{8,0},{16,8},{24,16},{1,25},{9,1},{17,9},{25,17},{2,26},{10... | collective-permute-start | bytes 1572872 | tf_op jit(solution)/shard_map/ppermute | solution.py:441
  175.0 16.7 %collective-permute-start.26 = (bf16[128,2048]{1,0:T(8,128)(2,1)S(1)}, bf16[128,2048]{1,0:T(8,128)(2,1)S(1)}, u32[]{:S(2)}, u32[]{:S(2)}) collective-permute-start(bf16[128,2048]{1,0:T(8,128)(2,1)S(1)} %get-tuple-element.257), channel_id=1, source_target_pairs={{0,8},{8,16},{16,24},{24,0},{1,9},{9,17},{17,25},{25,1},{2,10},{10... | collective-permute-start | bytes 1572872 | tf_op jit(solution)/shard_map/ppermute | solution.py:441
  175.6 24.9 %collective-permute-start.27 = (bf16[128,2048]{1,0:T(8,128)(2,1)S(1)}, bf16[128,2048]{1,0:T(8,128)(2,1)S(1)}, u32[]{:S(2)}, u32[]{:S(2)}) collective-permute-start(bf16[128,2048]{1,0:T(8,128)(2,1)S(1)} %get-tuple-element.257), channel_id=1, source_target_pairs={{0,24},{8,0},{16,8},{24,16},{1,25},{9,1},{17,9},{25,17},{2,26},{10... | collective-permute-start | bytes 1572872 | tf_op jit(solution)/shard_map/ppermute | solution.py:441
  178.9 36.8 %collective-permute-start.31 = (bf16[128,2048]{1,0:T(8,128)(2,1)S(1)}, bf16[128,2048]{1,0:T(8,128)(2,1)S(1)}, u32[]{:S(2)}, u32[]{:S(2)}) collective-permute-start(bf16[128,2048]{1,0:T(8,128)(2,1)S(1)} %get-tuple-element.257), channel_id=1, source_target_pairs={{0,1},{1,0},{2,3},{3,2},{4,5},{5,4},{6,7},{7,6},{8,9},{9,8},{10,11... | collective-permute-start | bytes 1572872 | tf_op jit(solution)/shard_map/ppermute | solution.py:445
  191.7 16.9 %collective-permute-start.28 = (bf16[64,2048]{1,0:T(8,128)(2,1)S(1)}, bf16[64,2048]{1,0:T(8,128)(2,1)S(1)}, u32[]{:S(2)}, u32[]{:S(2)}) collective-permute-start(bf16[64,2048]{1,0:T(8,128)(2,1)S(1)} %slice.536), channel_id=1, source_target_pairs={{0,8},{8,16},{16,24},{24,0},{1,9},{9,17},{17,25},{25,1},{2,10},{10... | collective-permute-start | bytes 786440 | tf_op jit(solution)/shard_map/ppermute | solution.py:441
  241.9 19.9 %collective-permute-start.35 = (bf16[128,2048]{1,0:T(8,128)(2,1)S(1)}, bf16[128,2048]{1,0:T(8,128)(2,1)S(1)}, u32[]{:S(2)}, u32[]{:S(2)}) collective-permute-start(bf16[128,2048]{1,0:T(8,128)(2,1)S(1)} %get-tuple-element.127), channel_id=1, source_target_pairs={{0,1},{1,0},{2,3},{3,2},{4,5},{5,4},{6,7},{7,6},{8,9},{9,8},{10,11... | collective-permute-start | bytes 1572872 | tf_op jit(solution)/shard_map/ppermute | solution.py:445
  254.6 16.8 %collective-permute-start.39 = (bf16[128,2048]{1,0:T(8,128)(2,1)S(1)}, bf16[128,2048]{1,0:T(8,128)(2,1)S(1)}, u32[]{:S(2)}, u32[]{:S(2)}) collective-permute-start(bf16[128,2048]{1,0:T(8,128)(2,1)S(1)} %pad_maximum_fusion.12), channel_id=1, source_target_pairs={{0,8},{8,16},{16,24},{24,0},{1,9},{9,17},{17,25},{25,1},{2,10},{10... | collective-permute-start | bytes 1572872 | tf_op jit(solution)/shard_map/ppermute | solution.py:441
  259.4 22.4 %collective-permute-start.42 = (bf16[128,2048]{1,0:T(8,128)(2,1)S(1)}, bf16[128,2048]{1,0:T(8,128)(2,1)S(1)}, u32[]{:S(2)}, u32[]{:S(2)}) collective-permute-start(bf16[128,2048]{1,0:T(8,128)(2,1)S(1)} %pad_maximum_fusion.13), channel_id=1, source_target_pairs={{0,24},{8,0},{16,8},{24,16},{1,25},{9,1},{17,9},{25,17},{2,26},{10... | collective-permute-start | bytes 1572872 | tf_op jit(solution)/shard_map/ppermute | solution.py:441
  299.9 135.3 %reduce-scatter.9.cloned.1.call-start = ((), (), s32[]{:S(2)}) async-start(), calls=%async_computation.10 | async-start | bytes 5242880 | tf_op jit(solution)/shard_map/reduce_scatter | solution.py:567
  299.9 16.7 %collective-permute-start.43 = (bf16[128,2048]{1,0:T(8,128)(2,1)S(1)}, bf16[128,2048]{1,0:T(8,128)(2,1)S(1)}, u32[]{:S(2)}, u32[]{:S(2)}) collective-permute-start(bf16[128,2048]{1,0:T(8,128)(2,1)S(1)} %get-tuple-element.136), channel_id=1, source_target_pairs={{0,8},{8,16},{16,24},{24,0},{1,9},{9,17},{17,25},{25,1},{2,10},{10... | collective-permute-start | bytes 1572872 | tf_op jit(solution)/shard_map/ppermute | solution.py:441
  300.5 24.8 %collective-permute-start.44 = (bf16[128,2048]{1,0:T(8,128)(2,1)S(1)}, bf16[128,2048]{1,0:T(8,128)(2,1)S(1)}, u32[]{:S(2)}, u32[]{:S(2)}) collective-permute-start(bf16[128,2048]{1,0:T(8,128)(2,1)S(1)} %get-tuple-element.136), channel_id=1, source_target_pairs={{0,24},{8,0},{16,8},{24,16},{1,25},{9,1},{17,9},{25,17},{2,26},{10... | collective-permute-start | bytes 1572872 | tf_op jit(solution)/shard_map/ppermute | solution.py:441
  303.8 36.3 %collective-permute-start.48 = (bf16[128,2048]{1,0:T(8,128)(2,1)S(1)}, bf16[128,2048]{1,0:T(8,128)(2,1)S(1)}, u32[]{:S(2)}, u32[]{:S(2)}) collective-permute-start(bf16[128,2048]{1,0:T(8,128)(2,1)S(1)} %get-tuple-element.136), channel_id=1, source_target_pairs={{0,1},{1,0},{2,3},{3,2},{4,5},{5,4},{6,7},{7,6},{8,9},{9,8},{10,11... | collective-permute-start | bytes 1572872 | tf_op jit(solution)/shard_map/ppermute | solution.py:445
  316.6 16.9 %collective-permute-start.45 = (bf16[64,2048]{1,0:T(8,128)(2,1)S(1)}, bf16[64,2048]{1,0:T(8,128)(2,1)S(1)}, u32[]{:S(2)}, u32[]{:S(2)}) collective-permute-start(bf16[64,2048]{1,0:T(8,128)(2,1)S(1)} %slice.544), channel_id=1, source_target_pairs={{0,8},{8,16},{16,24},{24,0},{1,9},{9,17},{17,25},{25,1},{2,10},{10... | collective-permute-start | bytes 786440 | tf_op jit(solution)/shard_map/ppermute | solution.py:441
  352.1 141.5 %reduce-scatter.11.cloned.1.call-start = ((), (), s32[]{:S(2)}) async-start(), calls=%async_computation.11 | async-start | bytes 10485760 | tf_op jit(solution)/shard_map/reduce_scatter | solution.py:567
  389.4 139.0 %reduce-scatter.13.cloned.1.call-start = ((), (), s32[]{:S(2)}) async-start(), calls=%async_computation.12 | async-start | bytes 1966080 | tf_op jit(solution)/shard_map/reduce_scatter | solution.py:567
  391.6 22.2 %collective-permute-start.51 = (bf16[128,2048]{1,0:T(8,128)(2,1)}, bf16[128,2048]{1,0:T(8,128)(2,1)}, u32[]{:S(2)}, u32[]{:S(2)}) collective-permute-start(bf16[128,2048]{1,0:T(8,128)(2,1)} %get-tuple-element.145), channel_id=1, source_target_pairs={{0,1},{1,0},{2,3},{3,2},{4,5},{5,4},{6,7},{7,6},{8,9},{9,8},{10,11... | collective-permute-start | bytes 1572872 | tf_op jit(solution)/shard_map/ppermute | solution.py:445
  403.9 16.9 %collective-permute-start.55 = (bf16[128,2048]{1,0:T(8,128)(2,1)S(1)}, bf16[128,2048]{1,0:T(8,128)(2,1)}, u32[]{:S(2)}, u32[]{:S(2)}) collective-permute-start(bf16[128,2048]{1,0:T(8,128)(2,1)S(1)} %pad_maximum_fusion.15), channel_id=1, source_target_pairs={{0,8},{8,16},{16,24},{24,0},{1,9},{9,17},{17,25},{25,1},{2,10},{10... | collective-permute-start | bytes 1572872 | tf_op jit(solution)/shard_map/ppermute | solution.py:441
  409.5 23.0 %collective-permute-start.58 = (bf16[128,2048]{1,0:T(8,128)(2,1)S(1)}, bf16[128,2048]{1,0:T(8,128)(2,1)S(1)}, u32[]{:S(2)}, u32[]{:S(2)}) collective-permute-start(bf16[128,2048]{1,0:T(8,128)(2,1)S(1)} %pad_maximum_fusion.16), channel_id=1, source_target_pairs={{0,24},{8,0},{16,8},{24,16},{1,25},{9,1},{17,9},{25,17},{2,26},{10... | collective-permute-start | bytes 1572872 | tf_op jit(solution)/shard_map/ppermute | solution.py:441
  412.3 38.5 %collective-permute-start.67 = (bf16[64,512]{1,0:T(8,128)(2,1)}, bf16[64,512]{1,0:T(8,128)(2,1)S(1)}, u32[]{:S(2)}, u32[]{:S(2)}) collective-permute-start(bf16[64,512]{1,0:T(8,128)(2,1)} %get-tuple-element.295), channel_id=1, source_target_pairs={{0,8},{8,16},{16,24},{24,0},{1,9},{9,17},{17,25},{25,1},{2,10},{10... | collective-permute-start | bytes 196616 | tf_op jit(solution)/shard_map/ppermute | solution.py:441
  413.1 38.0 %collective-permute-start.68 = (bf16[64,512]{1,0:T(8,128)(2,1)}, bf16[64,512]{1,0:T(8,128)(2,1)}, u32[]{:S(2)}, u32[]{:S(2)}) collective-permute-start(bf16[64,512]{1,0:T(8,128)(2,1)} %get-tuple-element.297), channel_id=1, source_target_pairs={{0,16},{8,24},{16,0},{24,8},{1,17},{9,25},{17,1},{25,9},{2,18},{10... | collective-permute-start | bytes 196616 | tf_op jit(solution)/shard_map/ppermute | solution.py:441
  413.7 37.7 %collective-permute-start.69 = (bf16[64,512]{1,0:T(8,128)(2,1)}, bf16[64,512]{1,0:T(8,128)(2,1)}, u32[]{:S(2)}, u32[]{:S(2)}) collective-permute-start(bf16[64,512]{1,0:T(8,128)(2,1)} %get-tuple-element.296), channel_id=1, source_target_pairs={{0,24},{8,0},{16,8},{24,16},{1,25},{9,1},{17,9},{25,17},{2,26},{10... | collective-permute-start | bytes 196616 | tf_op jit(solution)/shard_map/ppermute | solution.py:441
  440.8 16.9 %collective-permute-start.59 = (bf16[128,2048]{1,0:T(8,128)(2,1)}, bf16[128,2048]{1,0:T(8,128)(2,1)S(1)}, u32[]{:S(2)}, u32[]{:S(2)}) collective-permute-start(bf16[128,2048]{1,0:T(8,128)(2,1)} %get-tuple-element.157), channel_id=1, source_target_pairs={{0,8},{8,16},{16,24},{24,0},{1,9},{9,17},{17,25},{25,1},{2,10},{10... | collective-permute-start | bytes 1572872 | tf_op jit(solution)/shard_map/ppermute | solution.py:441
  441.4 25.5 %collective-permute-start.60 = (bf16[128,2048]{1,0:T(8,128)(2,1)}, bf16[128,2048]{1,0:T(8,128)(2,1)S(1)}, u32[]{:S(2)}, u32[]{:S(2)}) collective-permute-start(bf16[128,2048]{1,0:T(8,128)(2,1)} %get-tuple-element.157), channel_id=1, source_target_pairs={{0,24},{8,0},{16,8},{24,16},{1,25},{9,1},{17,9},{25,17},{2,26},{10... | collective-permute-start | bytes 1572872 | tf_op jit(solution)/shard_map/ppermute | solution.py:441
  450.8 18.8 %collective-permute-start.70 = (bf16[2048,128]{1,0:T(8,128)(2,1)S(1)}, bf16[2048,128]{1,0:T(8,128)(2,1)}, u32[]{:S(2)}, u32[]{:S(2)}) collective-permute-start(bf16[2048,128]{1,0:T(8,128)(2,1)S(1)} %pad_maximum_fusion.18), channel_id=1, source_target_pairs={{0,1},{1,0},{2,3},{3,2},{4,5},{5,4},{6,7},{7,6},{8,9},{9,8},{10,11... | collective-permute-start | bytes 1572872 | tf_op jit(solution)/shard_map/ppermute | solution.py:445
  452.4 25.9 %collective-permute-start.64 = (bf16[128,2048]{1,0:T(8,128)(2,1)}, bf16[128,2048]{1,0:T(8,128)(2,1)S(1)}, u32[]{:S(2)}, u32[]{:S(2)}) collective-permute-start(bf16[128,2048]{1,0:T(8,128)(2,1)} %get-tuple-element.157), channel_id=1, source_target_pairs={{0,1},{1,0},{2,3},{3,2},{4,5},{5,4},{6,7},{7,6},{8,9},{9,8},{10,11... | collective-permute-start | bytes 1572872 | tf_op jit(solution)/shard_map/ppermute | solution.py:445
  457.8 16.9 %collective-permute-start.61 = (bf16[64,2048]{1,0:T(8,128)(2,1)S(1)}, bf16[64,2048]{1,0:T(8,128)(2,1)S(1)}, u32[]{:S(2)}, u32[]{:S(2)}) collective-permute-start(bf16[64,2048]{1,0:T(8,128)(2,1)S(1)} %slice.552), channel_id=1, source_target_pairs={{0,8},{8,16},{16,24},{24,0},{1,9},{9,17},{17,25},{25,1},{2,10},{10... | collective-permute-start | bytes 786440 | tf_op jit(solution)/shard_map/ppermute | solution.py:441
  495.7 119.0 %reduce-scatter.15.cloned.1.call-start = ((), (), s32[]{:S(2)}) async-start(), calls=%async_computation.13 | async-start | bytes 1310720 | tf_op jit(solution)/shard_map/reduce_scatter | solution.py:567
  534.4 20.2 %collective-permute-start.78 = (bf16[320,640]{1,0:T(8,128)(2,1)S(1)}, bf16[320,640]{1,0:T(8,128)(2,1)S(1)}, u32[]{:S(2)}, u32[]{:S(2)}) collective-permute-start(bf16[320,640]{1,0:T(8,128)(2,1)S(1)} %fusion.42.refs_10_), channel_id=1, source_target_pairs={{0,24},{8,0},{16,8},{24,16},{1,25},{9,1},{17,9},{25,17},{2,26},{10... | collective-permute-start | bytes 1228808 | tf_op jit(solution)/shard_map/ppermute | solution.py:441
  548.9 65.9 %reduce-scatter.17.cloned.1.call-start = ((), (), s32[]{:S(2)}) async-start(), calls=%async_computation.14 | async-start | bytes 1310720 | tf_op jit(solution)/shard_map/reduce_scatter | solution.py:567
  569.8 24.1 %collective-permute-start.81 = (bf16[128,2048]{1,0:T(8,128)(2,1)}, bf16[128,2048]{1,0:T(8,128)(2,1)}, u32[]{:S(2)}, u32[]{:S(2)}) collective-permute-start(bf16[128,2048]{1,0:T(8,128)(2,1)} %get-tuple-element.223), channel_id=1, source_target_pairs={{0,1},{1,0},{2,3},{3,2},{4,5},{5,4},{6,7},{7,6},{8,9},{9,8},{10,11... | collective-permute-start | bytes 1572872 | tf_op jit(solution)/shard_map/ppermute | solution.py:445
  587.1 16.8 %collective-permute-start.85 = (bf16[128,2048]{1,0:T(8,128)(2,1)S(1)}, bf16[128,2048]{1,0:T(8,128)(2,1)S(1)}, u32[]{:S(2)}, u32[]{:S(2)}) collective-permute-start(bf16[128,2048]{1,0:T(8,128)(2,1)S(1)} %pad_maximum_fusion.22), channel_id=1, source_target_pairs={{0,8},{8,16},{16,24},{24,0},{1,9},{9,17},{17,25},{25,1},{2,10},{10... | collective-permute-start | bytes 1572872 | tf_op jit(solution)/shard_map/ppermute | solution.py:441
  591.4 21.8 %collective-permute-start.88 = (bf16[128,2048]{1,0:T(8,128)(2,1)S(1)}, bf16[128,2048]{1,0:T(8,128)(2,1)S(1)}, u32[]{:S(2)}, u32[]{:S(2)}) collective-permute-start(bf16[128,2048]{1,0:T(8,128)(2,1)S(1)} %pad_maximum_fusion.23), channel_id=1, source_target_pairs={{0,24},{8,0},{16,8},{24,16},{1,25},{9,1},{17,9},{25,17},{2,26},{10... | collective-permute-start | bytes 1572872 | tf_op jit(solution)/shard_map/ppermute | solution.py:441
  616.2 37.4 %collective-permute-start.105 = (bf16[256,1024]{1,0:T(8,128)(2,1)S(1)}, bf16[256,1024]{1,0:T(8,128)(2,1)S(1)}, u32[]{:S(2)}, u32[]{:S(2)}) collective-permute-start(bf16[256,1024]{1,0:T(8,128)(2,1)S(1)} %broadcast_select_fusion.8), channel_id=1, source_target_pairs={{0,1},{1,0},{2,3},{3,2},{4,5},{5,4},{6,7},{7,6},{8,9},{9,8},{10,11... | collective-permute-start | bytes 1572872 | tf_op jit(solution)/shard_map/ppermute | solution.py:445
  618.5 55.5 %collective-permute-start.104 = (bf16[256,2048]{1,0:T(8,128)(2,1)S(1)}, bf16[256,2048]{1,0:T(8,128)(2,1)S(1)}, u32[]{:S(2)}, u32[]{:S(2)}) collective-permute-start(bf16[256,2048]{1,0:T(8,128)(2,1)S(1)} %broadcast_select_fusion.4), channel_id=1, source_target_pairs={{0,1},{1,0},{2,3},{3,2},{4,5},{5,4},{6,7},{7,6},{8,9},{9,8},{10,11... | collective-permute-start | bytes 3145736 | tf_op jit(solution)/shard_map/ppermute | solution.py:445
  647.2 30.4 %collective-permute-start.101 = (bf16[128,512]{1,0:T(8,128)(2,1)S(1)}, bf16[128,512]{1,0:T(8,128)(2,1)S(1)}, u32[]{:S(2)}, u32[]{:S(2)}) collective-permute-start(bf16[128,512]{1,0:T(8,128)(2,1)S(1)} %slice.584), channel_id=1, source_target_pairs={{0,8},{8,16},{16,24},{24,0},{1,9},{9,17},{17,25},{25,1},{2,10},{10... | collective-permute-start | bytes 393224 | tf_op jit(solution)/shard_map/ppermute | solution.py:441
  651.1 26.5 %collective-permute-start.103 = (bf16[128,512]{1,0:T(8,128)(2,1)S(1)}, bf16[128,512]{1,0:T(8,128)(2,1)S(1)}, u32[]{:S(2)}, u32[]{:S(2)}) collective-permute-start(bf16[128,512]{1,0:T(8,128)(2,1)S(1)} %slice.585), channel_id=1, source_target_pairs={{0,24},{8,0},{16,8},{24,16},{1,25},{9,1},{17,9},{25,17},{2,26},{10... | collective-permute-start | bytes 393224 | tf_op jit(solution)/shard_map/ppermute | solution.py:441
  653.5 24.0 %collective-permute-start.97 = (bf16[128,512]{1,0:T(8,128)(2,1)S(1)}, bf16[128,512]{1,0:T(8,128)(2,1)S(1)}, u32[]{:S(2)}, u32[]{:S(2)}) collective-permute-start(bf16[128,512]{1,0:T(8,128)(2,1)S(1)} %slice.485), channel_id=1, source_target_pairs={{0,8},{8,16},{16,24},{24,0},{1,9},{9,17},{17,25},{25,1},{2,10},{10... | collective-permute-start | bytes 393224 | tf_op jit(solution)/shard_map/ppermute | solution.py:441
  (156 other events, 2390.1 us)
Sparse Core Ops, SparseCore 0:
  12.8 46.6 all-gather.3
  61.9 31.1 all-gather.5
  95.0 125.3 all-gather.7
  300.0 40.0 reduce-scatter.6
  352.2 52.0 reduce-scatter.8
  407.2 86.3 reduce-scatter.10
  497.5 30.9 reduce-scatter.12
  549.0 27.7 reduce-scatter.14
  580.2 27.7 reduce-scatter.16
